TPU v7x, 256 devices: a whole 4x4x8 slice. The times are simulated.
256 devices in a mesh: ctx: 32 (over x, z_hi, core), chan: 8 (over y, z_lo).
Axes of the slice: x: 4, y: 4, z: 8 (z_hi: 4, z_lo: 2; z = z_hi * 2 + z_lo), core: 2. Of those that a mesh axis runs over, the one named last changes fastest.
Arguments:
- query_proj: bfloat16 [16384, 4096], P('ctx', 'chan'), may hold values from -6 to 6
- key_proj: bfloat16 [16384, 4096], P('ctx', 'chan'), may hold values from -6 to 6
- value_proj: bfloat16 [16384, 4096], P('ctx', 'chan'), may hold values from -6 to 6
- long_filter: float32 [16384, 4096], P('ctx', 'chan'), may hold values from 0 to 1
- skip_gain: float32 [4096], P('chan'), may hold values from 0.5 to 1.5
- out_weight: bfloat16 [4096, 4096], P('ctx', 'chan'), may hold values from -0.09375 to 0.09375
Outputs:
- mixed: bfloat16 [16384, 4096], P('ctx', 'chan')
All inputs are finite; a program needn't handle non-finite values.
Results may differ from a plain program's by a relative error of at most 0.0049.
Values may be sent and summed in bfloat16 or wider, within the bound.
No kernel may reach another device: no remote copies, remote signals or barrier semaphores. Data moves between devices by JAX's collectives and lax.ppermute only.
A program may use at most 128 MiB of HBM per device.

v0:
```python
import math

import jax
import jax.numpy as jnp
from jax import lax
from jax.sharding import PartitionSpec as P


def phases(first, second, period):
    product_index = first[:, None] * second[None, :] % period
    angles = product_index.astype(jnp.float32) * (2.0 * math.pi / period)
    return (jnp.cos(angles), jnp.sin(angles))


def contract(matrix, operand, pattern):
    return jnp.einsum(pattern, matrix, operand, precision=lax.Precision.HIGHEST)


def forward(field, groups, within, period):
    mine = lax.axis_index("ctx")
    blocks = field.reshape(groups, within, field.shape[1])
    regrouped = lax.all_to_all(blocks, "ctx", split_axis=0, concat_axis=0, tiled=True)
    freq_low = jnp.arange(2 * groups, dtype=jnp.int32)
    cos_one, sin_one = phases(freq_low, jnp.arange(groups, dtype=jnp.int32), 2 * groups)
    first_real = contract(cos_one, regrouped, "gj,jrc->grc")
    first_imag = -contract(sin_one, regrouped, "gj,jrc->grc")
    positions = mine * within + jnp.arange(within, dtype=jnp.int32)
    cos_two, sin_two = phases(freq_low, positions, period)
    cos_two = cos_two[:, :, None]
    sin_two = sin_two[:, :, None]
    turned_real = first_real * cos_two + first_imag * sin_two
    turned_imag = first_imag * cos_two - first_real * sin_two
    moved_real, moved_imag = (
        lax.all_to_all(turned_real, "ctx", split_axis=0, concat_axis=1, tiled=True),
        lax.all_to_all(turned_imag, "ctx", split_axis=0, concat_axis=1, tiled=True),
    )
    length = moved_real.shape[1]
    steps_index = jnp.arange(length, dtype=jnp.int32)
    cos_three, sin_three = phases(steps_index, steps_index, length)
    spec_real = contract(cos_three, moved_real, "hs,gsc->ghc") + contract(
        sin_three, moved_imag, "hs,gsc->ghc"
    )
    spec_imag = contract(cos_three, moved_imag, "hs,gsc->ghc") - contract(
        sin_three, moved_real, "hs,gsc->ghc"
    )
    return (spec_real, spec_imag)


def inverse(spec_real, spec_imag, groups, within, period):
    mine = lax.axis_index("ctx")
    owned_rows, length = (spec_real.shape[0], spec_real.shape[1])
    steps_index = jnp.arange(length, dtype=jnp.int32)
    cos_three, sin_three = phases(steps_index, steps_index, length)
    back_real = contract(cos_three, spec_real, "sh,ghc->gsc") - contract(
        sin_three, spec_imag, "sh,ghc->gsc"
    )
    back_imag = contract(cos_three, spec_imag, "sh,ghc->gsc") + contract(
        sin_three, spec_real, "sh,ghc->gsc"
    )
    owned = owned_rows * mine + jnp.arange(owned_rows, dtype=jnp.int32)
    cos_two, sin_two = phases(owned, steps_index, period)
    cos_two = cos_two[:, :, None]
    sin_two = sin_two[:, :, None]
    turned_real = back_real * cos_two - back_imag * sin_two
    turned_imag = back_real * sin_two + back_imag * cos_two
    got_real, got_imag = (
        lax.all_to_all(turned_real, "ctx", split_axis=1, concat_axis=0, tiled=True),
        lax.all_to_all(turned_imag, "ctx", split_axis=1, concat_axis=0, tiled=True),
    )
    cos_four, sin_four = phases(
        jnp.arange(groups, dtype=jnp.int32), jnp.arange(2 * groups, dtype=jnp.int32), 2 * groups
    )
    spread = (
        contract(cos_four, got_real, "jg,grc->jrc") - contract(sin_four, got_imag, "jg,grc->jrc")
    ) / period
    returned = lax.all_to_all(spread, "ctx", split_axis=0, concat_axis=0, tiled=True)
    return returned.reshape(groups * within, returned.shape[2])


def on_device(query_proj, key_proj, value_proj, long_filter, skip_gain, out_weight):
    groups = lax.axis_size("ctx")
    tokens_here, width = key_proj.shape
    within = tokens_here // groups
    period = 2 * groups * tokens_here
    source = key_proj.astype(jnp.float32) * value_proj.astype(jnp.float32)
    src_real, src_imag = forward(source, groups, within, period)
    fil_real, fil_imag = forward(long_filter, groups, within, period)
    prod_real = src_real * fil_real - src_imag * fil_imag
    prod_imag = src_real * fil_imag + src_imag * fil_real
    conv = inverse(prod_real, prod_imag, groups, within, period)
    gated = (query_proj.astype(jnp.float32) * (conv + skip_gain[None, :] * source)).astype(
        jnp.bfloat16
    )
    features = lax.all_gather(gated, "chan", axis=1, tiled=True)
    return jnp.dot(
        features,
        lax.all_gather(out_weight, "ctx", axis=0, tiled=True),
        preferred_element_type=jnp.float32,
    ).astype(jnp.bfloat16)


def solution(mesh):
    return jax.shard_map(
        on_device,
        mesh=mesh,
        in_specs=(
            P("ctx", "chan"),
            P("ctx", "chan"),
            P("ctx", "chan"),
            P("ctx", "chan"),
            P("chan"),
            P("ctx", "chan"),
        ),
        out_specs=P("ctx", "chan"),
        check_vma=False,
    )
```

profile of v0, /device:TPU:1, one launch (start us, length us, event | category | flops | bytes accessed | tf_op | source)
XLA Modules:
  0.0 697.2 jit_solution(4307186029403769502)
XLA Ops:
  7.9 41.3 %all_to_all.123 = f32[32,16,512]{2,1,0:T(8,128)S(1)} all-to-all(f32[32,16,512]{2,1,0:T(8,128)S(1)} %bitcast.124), channel_id=1, replica_groups=mesh['ctx'=32,'chan'=8] {'ctx'}, dimensions={0} | all-to-all | bytes 2097152 | tf_op jit(solution)/shard_map/all_to_all | solution.py:22
  49.2 5.3 all-to-all-start.3
  54.6 3.8 fusion.43
  58.4 3.8 fusion.45
  62.2 20.8 %all-to-all-done.3 = f32[32,16,512]{2,1,0:T(8,128)S(1)} async-done(((f32[32,16,512]{2,1,0:T(8,128)}), f32[32,16,512]{2,1,0:T(8,128)S(1)}, u32[]{:S(2)}, u32[]{:S(2)}) %all-to-all-start.3) | async-done | bytes 1048608 | tf_op jit(solution)/shard_map/all_to_all | solution.py:22
  82.9 2.4 fusion.39
  85.4 6.0 multiply_subtract_fusion.1
  91.3 2.5 copy.65
  93.8 6.8 all-to-all-start.4
  100.6 4.2 copy.68
  104.8 47.4 %all-to-all-done.4 = f32[64,16,512]{2,1,0:T(8,128)} async-done(((f32[64,16,512]{2,1,0:T(8,128)}), f32[64,16,512]{2,1,0:T(8,128)}, u32[]{:S(2)}, u32[]{:S(2)}) %all-to-all-start.4) | async-done | bytes 2097184 | tf_op jit(solution)/shard_map/all_to_all | solution.py:34
  152.2 4.7 all-to-all-start.5
  157.0 4.2 copy.57
  161.2 47.8 %all-to-all-done.5 = f32[64,16,512]{2,1,0:T(8,128)} async-done(((f32[64,16,512]{2,1,0:T(8,128)}), f32[64,16,512]{2,1,0:T(8,128)}, u32[]{:S(2)}, u32[]{:S(2)}) %all-to-all-start.5) | async-done | bytes 2097184 | tf_op jit(solution)/shard_map/all_to_all | solution.py:35
  209.0 5.2 all-to-all-start.1
  214.2 2.6 copy.60
  216.8 49.1 %all-to-all-done.1 = f32[64,16,512]{2,1,0:T(8,128)} async-done(((f32[64,16,512]{2,1,0:T(8,128)}), f32[64,16,512]{2,1,0:T(8,128)}, u32[]{:S(2)}, u32[]{:S(2)}) %all-to-all-start.1) | async-done | bytes 2097184 | tf_op jit(solution)/shard_map/all_to_all | solution.py:34
  266.0 4.8 all-to-all-start.2
  270.9 1.8 copy.66
  272.8 2.6 copy.69
  275.4 1.8 copy.58
  277.3 10.9 %fusion.32 = f32[2,512,512]{2,1,0:T(8,128)S(1)} fusion(f32[2,512,512]{2,1,0:T(8,128)S(1)} %bitcast.116), kind=kOutput, calls=%fused_computation.46 | convolution fusion | flops 3224895488 | bytes 4194304 | tf_op jit(solution)/shard_map/hs,gsc->ghc/dot_general | solution.py:16
  288.2 11.5 %fusion.34 = f32[2,512,512]{2,1,0:T(8,128)} fusion(f32[2,512,512]{2,1,0:T(8,128)S(1)} %bitcast.114), kind=kOutput, calls=%fused_computation.48 | convolution fusion | flops 3224895488 | bytes 4194304 | tf_op jit(solution)/shard_map/hs,gsc->ghc/dot_general | solution.py:16
  299.7 11.7 %fusion.28 = f32[2,512,512]{2,1,0:T(8,128)} fusion(f32[2,512,512]{2,1,0:T(8,128)S(1)} %bitcast.118), kind=kOutput, calls=%fused_computation.42 | convolution fusion | flops 3224895488 | bytes 4194304 | tf_op jit(solution)/shard_map/hs,gsc->ghc/dot_general | solution.py:16
  311.4 11.2 %convolution_add_fusion = f32[2,512,512]{2,1,0:T(8,128)S(1)} fusion(f32[2,512,512]{2,1,0:T(8,128)S(1)} %fusion.32, f32[2,512,512]{2,1,0:T(8,128)S(1)} %bitcast.119), kind=kOutput, calls=%fused_computation.20 | convolution fusion | flops 3225419776 | bytes 6291456 | tf_op jit(solution)/shard_map/hs,gsc->ghc/dot_general | solution.py:16
  322.9 1.8 copy.61
  324.7 11.1 %fusion.30 = f32[2,512,512]{2,1,0:T(8,128)S(1)} fusion(f32[2,512,512]{2,1,0:T(8,128)S(1)} %bitcast.120), kind=kOutput, calls=%fused_computation.44 | convolution fusion | flops 3224895488 | bytes 4194304 | tf_op jit(solution)/shard_map/hs,gsc->ghc/dot_general | solution.py:16
  335.9 11.2 %convolution_add_fusion.1 = f32[2,512,512]{2,1,0:T(8,128)S(1)} fusion(f32[2,512,512]{2,1,0:T(8,128)S(1)} %copy-done.7, f32[2,512,512]{2,1,0:T(8,128)S(1)} %bitcast.121), kind=kOutput, calls=%fused_computation.21 | convolution fusion | flops 3225419776 | bytes 6291456 | tf_op jit(solution)/shard_map/hs,gsc->ghc/dot_general | solution.py:16
  347.2 11.6 %convolution_subtract_fusion = f32[2,512,512]{2,1,0:T(8,128)S(1)} fusion(f32[2,512,512]{2,1,0:T(8,128)S(1)} %copy-done.6, f32[2,512,512]{2,1,0:T(8,128)S(1)} %bitcast.117), kind=kOutput, calls=%fused_computation.18 | convolution fusion | flops 3225419776 | bytes 6291456 | tf_op jit(solution)/shard_map/hs,gsc->ghc/dot_general | solution.py:16
  358.8 11.6 %multiply_subtract_fusion = (f32[2,512,512]{2,1,0:T(8,128)S(1)}, f32[2,512,512]{2,1,0:T(8,128)S(1)}) fusion(f32[2,512,512]{2,1,0:T(8,128)S(1)} %convolution_subtract_fusion, f32[2,512,512]{2,1,0:T(8,128)S(1)} %convolution_add_fusion.1, f32[2,512,512]{2,1,0:T(8,128)S(1)} %convolution_add_fusion, f32[2,512,512]{2,1,0:T(8,128)S(1)} %fusion.30, ...), kind=kOutput, calls=%fused_computation.11 | convolution fusion | flops 3228565504 | bytes 14680064 | tf_op jit(solution)/shard_map/hs,gsc->ghc/dot_general | solution.py:16
  370.5 8.6 %fusion.2 = f32[2,512,512]{2,1,0:T(8,128)S(1)} fusion(f32[2,512,512]{2,1,0:T(8,128)S(1)} %get-tuple-element.6), kind=kOutput, calls=%fused_computation.2 | convolution fusion | flops 3224895488 | bytes 4194304 | tf_op jit(solution)/shard_map/sh,ghc->gsc/dot_general | solution.py:16
  379.1 8.4 %fusion = f32[2,512,512]{2,1,0:T(8,128)S(1)} fusion(f32[2,512,512]{2,1,0:T(8,128)S(1)} %get-tuple-element.6), kind=kOutput, calls=%fused_computation | convolution fusion | flops 3224895488 | bytes 4194304 | tf_op jit(solution)/shard_map/sh,ghc->gsc/dot_general | solution.py:16
  387.5 8.7 %fusion.8 = f32[2,512,512]{2,1,0:T(8,128)S(1)} fusion(f32[2,512,512]{2,1,0:T(8,128)S(1)} %fusion.2, f32[2,512,512]{2,1,0:T(8,128)S(1)} %get-tuple-element.5), kind=kOutput, calls=%fused_computation.16 | convolution fusion | flops 3225419776 | bytes 6291456 | tf_op jit(solution)/shard_map/sh,ghc->gsc/dot_general | solution.py:16
  396.1 8.9 %add_bitcast_fusion = (f32[2,512,512]{1,2,0:T(8,128)}, f32[2,512,512]{1,2,0:T(8,128)S(1)}) fusion(f32[2,512,512]{2,1,0:T(8,128)S(1)} %fusion.8, f32[2,512]{1,0:T(2,128)S(1)} %get-tuple-element.16, f32[2,512]{1,0:T(2,128)S(1)} %get-tuple-element.15, f32[2,512,512]{2,1,0:T(8,128)S(1)} %fusion, f32[2,512,512]{2,1,0:T(8,128)S(1)} %get-tuple-element.5), kind=kOutput, calls=%fused_computation.8 | convolution fusion | flops 3228565504 | bytes 10493952 | tf_op jit(solution)/shard_map/sh,ghc->gsc/dot_general | solution.py:16
  405.0 2.5 copy.75
  407.5 9.6 %all-to-all-start.6 = ((f32[2,512,512]{2,0,1:T(2,128)}), f32[2,512,512]{2,0,1:T(2,128)S(1)}, u32[]{:S(2)}, u32[]{:S(2)}) async-start(f32[2,512,512]{2,0,1:T(2,128)} %copy.75), calls=%async_computation.6 | async-start | bytes 4194304 | tf_op jit(solution)/shard_map/all_to_all | solution.py:67
  417.9 4.2 copy.78
  422.0 51.2 %all-to-all-done.6 = f32[2,512,512]{2,0,1:T(2,128)S(1)} async-done(((f32[2,512,512]{2,0,1:T(2,128)}), f32[2,512,512]{2,0,1:T(2,128)S(1)}, u32[]{:S(2)}, u32[]{:S(2)}) %all-to-all-start.6) | async-done | bytes 2097184 | tf_op jit(solution)/shard_map/all_to_all | solution.py:67
  473.2 5.0 all-to-all-start.7
  478.7 3.0 copy.77
  481.7 2.9 all_to_all.108
  484.6 62.4 %all-to-all-done.7 = f32[2,512,512]{2,0,1:T(2,128)} async-done(((f32[2,512,512]{2,0,1:T(2,128)}), f32[2,512,512]{2,0,1:T(2,128)}, u32[]{:S(2)}, u32[]{:S(2)}) %all-to-all-start.7) | async-done | bytes 2097184 | tf_op jit(solution)/shard_map/all_to_all | solution.py:68
  547.0 2.0 copy.79
  549.0 3.0 copy.80
  552.0 3.8 all_to_all.112
  559.2 33.8 %all_to_all.124 = f32[32,16,512]{2,1,0:T(8,128)S(1)} all-to-all(f32[32,16,512]{2,1,0:T(8,128)S(1)} %copy.81), channel_id=1, replica_groups=mesh['ctx'=32,'chan'=8] {'ctx'}, dimensions={0} | all-to-all | bytes 2097152 | tf_op jit(solution)/shard_map/all_to_all | solution.py:76
  594.3 89.1 %all-gather.3.cloned.1.call-done = bf16[512,4096]{1,0:T(8,128)(2,1)} async-done(((bf16[512,512]{1,0:T(8,128)(2,1)}), bf16[512,4096]{1,0:T(8,128)(2,1)}) %all-gather.3.cloned.1.call-update) | async-done | bytes 4194320 | tf_op jit(solution)/shard_map/all_gather | solution.py:94
  683.4 6.6 convolution_convert_fusion
  (40 shorter events, 7.7 us)
Async XLA Ops:
  49.2 33.7 %all-to-all-start.3 = ((f32[32,16,512]{2,1,0:T(8,128)}), f32[32,16,512]{2,1,0:T(8,128)S(1)}, u32[]{:S(2)}, u32[]{:S(2)}) async-start(f32[32,16,512]{2,1,0:T(8,128)} %bitcast.12), calls=%async_computation.3 | async-start | bytes 2097152 | tf_op jit(solution)/shard_map/all_to_all | solution.py:22
  82.9 2.4 copy-start.4
  93.8 58.4 %all-to-all-start.4 = ((f32[64,16,512]{2,1,0:T(8,128)}), f32[64,16,512]{2,1,0:T(8,128)}, u32[]{:S(2)}, u32[]{:S(2)}) async-start(f32[64,16,512]{2,1,0:T(8,128)} %copy.65), calls=%async_computation.4 | async-start | bytes 4194304 | tf_op jit(solution)/shard_map/all_to_all | solution.py:34
  152.2 56.8 %all-to-all-start.5 = ((f32[64,16,512]{2,1,0:T(8,128)}), f32[64,16,512]{2,1,0:T(8,128)}, u32[]{:S(2)}, u32[]{:S(2)}) async-start(f32[64,16,512]{2,1,0:T(8,128)} %copy.68), calls=%async_computation.5 | async-start | bytes 4194304 | tf_op jit(solution)/shard_map/all_to_all | solution.py:35
  209.0 57.0 %all-to-all-start.1 = ((f32[64,16,512]{2,1,0:T(8,128)}), f32[64,16,512]{2,1,0:T(8,128)}, u32[]{:S(2)}, u32[]{:S(2)}) async-start(f32[64,16,512]{2,1,0:T(8,128)} %copy.57), calls=%async_computation.1 | async-start | bytes 4194304 | tf_op jit(solution)/shard_map/all_to_all | solution.py:34
  266.0 56.9 %all-to-all-start.2 = ((f32[64,16,512]{2,1,0:T(8,128)}), f32[64,16,512]{2,1,0:T(8,128)}, u32[]{:S(2)}, u32[]{:S(2)}) async-start(f32[64,16,512]{2,1,0:T(8,128)} %copy.60), calls=%async_computation.2 | async-start | bytes 4194304 | tf_op jit(solution)/shard_map/all_to_all | solution.py:35
  272.8 4.5 copy-start.2
  277.3 10.9 %copy-start = (f32[2,32,16,512]{3,2,1,0:T(8,128)}, f32[2,32,16,512]{3,2,1,0:T(8,128)S(1)}, u32[]{:S(2)}) copy-start(f32[2,32,16,512]{3,2,1,0:T(8,128)S(1)} %copy.58) | copy-start | bytes 6291460
  324.7 11.1 %copy-start.7 = (f32[2,512,512]{2,1,0:T(8,128)S(1)}, f32[2,512,512]{2,1,0:T(8,128)}, u32[]{:S(2)}) copy-start(f32[2,512,512]{2,1,0:T(8,128)} %fusion.34) | copy-start | bytes 6291460
  335.9 11.3 %copy-start.3 = (f32[2,32,16,512]{3,2,1,0:T(8,128)S(1)}, f32[2,32,16,512]{3,2,1,0:T(8,128)}, u32[]{:S(2)}) copy-start(f32[2,32,16,512]{3,2,1,0:T(8,128)} %copy-done.2) | copy-start | bytes 6291460
  335.9 11.3 %copy-start.6 = (f32[2,512,512]{2,1,0:T(8,128)S(1)}, f32[2,512,512]{2,1,0:T(8,128)}, u32[]{:S(2)}) copy-start(f32[2,512,512]{2,1,0:T(8,128)} %fusion.28) | copy-start | bytes 6291460
  347.2 11.7 %copy-start.1 = (f32[2,32,16,512]{3,2,1,0:T(8,128)S(1)}, f32[2,32,16,512]{3,2,1,0:T(8,128)}, u32[]{:S(2)}) copy-start(f32[2,32,16,512]{3,2,1,0:T(8,128)} %copy-done) | copy-start | bytes 6291460
  407.5 65.7 %all-to-all-start.6 = ((f32[2,512,512]{2,0,1:T(2,128)}), f32[2,512,512]{2,0,1:T(2,128)S(1)}, u32[]{:S(2)}, u32[]{:S(2)}) async-start(f32[2,512,512]{2,0,1:T(2,128)} %copy.75), calls=%async_computation.6 | async-start | bytes 4194304 | tf_op jit(solution)/shard_map/all_to_all | solution.py:67
  417.1 177.1 %all-gather.5.cloned.1.call-start = ((), (), s32[]{:S(2)}) async-start(), calls=%async_computation.10 | async-start | bytes 4325376 | tf_op jit(solution)/shard_map/all_gather | solution.py:97
  473.2 73.8 %all-to-all-start.7 = ((f32[2,512,512]{2,0,1:T(2,128)}), f32[2,512,512]{2,0,1:T(2,128)}, u32[]{:S(2)}, u32[]{:S(2)}) async-start(f32[2,512,512]{2,0,1:T(2,128)} %copy.78), calls=%async_computation.7 | async-start | bytes 4194304 | tf_op jit(solution)/shard_map/all_to_all | solution.py:68
  478.2 205.1 %all-gather.3.cloned.1.call-start = ((), (), s32[]{:S(2)}) async-start(), calls=%async_computation.9 | async-start | bytes 4718592 | tf_op jit(solution)/shard_map/all_gather | solution.py:94
  555.8 1.6 copy-start.5
  558.6 34.5 %copy-start.8 = (bf16[512,512]{1,0:T(8,128)(2,1)S(1)}, bf16[512,512]{1,0:T(8,128)(2,1)}, u32[]{:S(2)}) copy-start(bf16[512,512]{1,0:T(8,128)(2,1)} %param.8) | copy-start | bytes 1572868
  558.6 34.5 %copy-start.9 = (bf16[512,512]{1,0:T(8,128)(2,1)S(1)}, bf16[512,512]{1,0:T(8,128)(2,1)}, u32[]{:S(2)}) copy-start(bf16[512,512]{1,0:T(8,128)(2,1)} %param.7) | copy-start | bytes 1572868
  558.6 34.5 %copy-start.10 = (bf16[512,512]{1,0:T(8,128)(2,1)S(1)}, bf16[512,512]{1,0:T(8,128)(2,1)}, u32[]{:S(2)}) copy-start(bf16[512,512]{1,0:T(8,128)(2,1)} %param.6) | copy-start | bytes 1572868
  558.6 34.5 %copy-start.11 = (f32[512]{0:T(512)S(1)}, f32[512]{0:T(512)}, u32[]{:S(2)}) copy-start(f32[512]{0:T(512)} %param.10) | copy-start | bytes 6148
Sparse Core Ops, SparseCore 0:
  420.5 124.1 all-gather.4
  594.4 88.9 all-gather.2
where the time goes:
time: 707 us; the launch traced here: 697 us
  waiting for transfers between devices  369 us (52%)
  matrix products  150 us (21%)
  blocking collectives  75.1 us (11%)
  local copies, waits for them, and re-layouts  44.4 us (6%)
  starting transfers between devices  41.6 us (6%)
  between operations  14.3 us (2%)
    dot_general x18, matrix products, contract(): return jnp.einsum(pattern, matrix, operand, precision=lax.Precision.HIGHEST)  144 us
    all_to_all x2, waiting for transfers between devices, forward(): lax.all_to_all(turned_real, 'ctx', split_axis=0, concat_axis=1, tiled=True)  96.6 us
    all_gather x1, waiting for transfers between devices, on_device(): features = lax.all_gather(gated, 'chan', axis=1, tiled=True)  89.1 us
    all_to_all x1, waiting for transfers between devices, inverse(): lax.all_to_all(turned_imag, 'ctx', split_axis=1, concat_axis=0, tiled=True)  62.4 us
    all_to_all x1, waiting for transfers between devices, inverse(): lax.all_to_all(turned_real, 'ctx', split_axis=1, concat_axis=0, tiled=True)  51.2 us
    all_to_all x2, waiting for transfers between devices, forward(): lax.all_to_all(turned_imag, 'ctx', split_axis=0, concat_axis=1, tiled=True)  48.1 us
    all_to_all x1, blocking collectives, forward(): lax.all_to_all(blocks, 'ctx', split_axis=0, concat_axis=0, tiled=True)  41.3 us
    all_to_all x1, blocking collectives, inverse(): lax.all_to_all(spread, 'ctx', split_axis=0, concat_axis=0, tiled=True)  33.8 us
  transfers between devices with their start and end apart: 9, of which 8 were waited for; matrix products, arithmetic and copies ran while one was open for 12% of the time, Pallas kernels for 0%

commit v1 on v0

v1 whole, which is shorter than its diff:
```python
import functools
import math

import jax
import jax.numpy as jnp
import numpy as np
from jax import lax
from jax.experimental import pallas as pl
from jax.experimental.pallas import tpu as pltpu
from jax.sharding import Mesh
from jax.sharding import PartitionSpec as P

AXES = ("x", "zh", "core", "y", "zl")
LINE = ("x", "zh", "zl")
BLOCKS = 32
BLOCK = 512
SLICE = 8
HALF = 256
STEPS = 64
INNER = 256
PERIOD = 32768
VMEM = 56 * 1024 * 1024
SWAP = [(0, 0), (1, 2), (2, 1), (3, 3)]
PAIR = [(0, 1), (1, 0)]


def halves(table):
    high = table.astype(np.float32).astype(jnp.bfloat16)
    low = (table - high.astype(np.float64)).astype(np.float32).astype(jnp.bfloat16)
    return high, low


def tables():
    odd = np.arange(STEPS) + 0.5
    steps = np.arange(STEPS)
    inner = np.arange(INNER)
    outer = 2 * math.pi * np.outer(odd, steps) / (2 * STEPS)
    same = np.eye(SLICE)
    order = steps.reshape(BLOCKS, 2).T.reshape(-1)
    cos_o, sin_o = np.cos(outer)[:, order], np.sin(outer)[:, order]
    first = np.concatenate([np.kron(cos_o, same), np.kron(-sin_o, same)], 0)
    last = np.concatenate([np.kron(cos_o.T, same), np.kron(-sin_o.T, same)], 1) / (PERIOD // 2)
    turn = 2 * math.pi * np.outer(odd, inner) / PERIOD
    turn = np.stack([np.cos(turn), np.sin(turn)]).astype(np.float32)
    angle = 2 * math.pi * (np.outer(inner, inner) % INNER) / INNER
    cos_i, sin_i = np.cos(angle), np.sin(angle)
    ahead = np.block([[cos_i, -sin_i], [sin_i, cos_i]])
    back = np.block([[cos_i, sin_i], [-sin_i, cos_i]])
    first_high, first_low = halves(first)
    last_high, last_low = halves(last)
    ahead_high, ahead_low = halves(ahead)
    back_high, back_low = halves(back)
    return (
        np.concatenate([first_high, first_low], 1),
        turn,
        np.concatenate([ahead_high, ahead_high, ahead_low], 0),
        np.concatenate([back_high, back_high, back_low], 0),
        np.concatenate([last_high, last_high, last_low], 1),
    )


def dot(left, right):
    return jnp.dot(left, right, preferred_element_type=jnp.float32)


def split(value):
    high = value.astype(jnp.bfloat16)
    return high, (value - high.astype(jnp.float32)).astype(jnp.bfloat16)


def params():
    return pltpu.CompilerParams(vmem_limit_bytes=VMEM)


def whole():
    return pl.BlockSpec(memory_space=pltpu.VMEM)


def prepare_kernel(far, key_ref, value_ref, filter_ref, out_ref):
    core = lax.axis_index("core")
    half = 1 - core if far else core
    columns = pl.ds(pl.multiple_of(half * HALF, HALF), HALF)
    source = key_ref[:, columns].astype(jnp.float32) * value_ref[:, columns].astype(jnp.float32)
    source = source.T.reshape(BLOCKS, SLICE, BLOCK)
    taps = filter_ref[:, columns].T.reshape(BLOCKS, SLICE, BLOCK)
    out_ref[...] = jnp.concatenate([source, taps], 1).astype(jnp.bfloat16)


def prepare(far, key, value, taps):
    return pl.pallas_call(
        functools.partial(prepare_kernel, far),
        out_shape=jax.ShapeDtypeStruct((BLOCKS, 2 * SLICE, BLOCK), jnp.bfloat16),
        in_specs=[whole()] * 3,
        out_specs=whole(),
        compiler_params=params(),
        name="prepare_far" if far else "prepare_near",
    )(key, value, taps)


def turn_kernel(query_ref, near_ref, far_ref):
    core = lax.axis_index("core")
    for half, ref in ((core, near_ref), (1 - core, far_ref)):
        columns = pl.ds(pl.multiple_of(half * HALF, HALF), HALF)
        ref[...] = query_ref[:, columns].astype(jnp.float32).T.astype(jnp.bfloat16)


def turn_query(query):
    return pl.pallas_call(
        turn_kernel,
        out_shape=[jax.ShapeDtypeStruct((HALF, BLOCK), jnp.bfloat16)] * 2,
        in_specs=[whole()],
        out_specs=[whole()] * 2,
        compiler_params=params(),
        name="turn_query",
    )(query)


def convolve_kernel(got_ref, own_ref, other_ref, first_ref, turn_ref, ahead_ref, back_ref, last_ref, out_ref):
    core, near = lax.axis_index("core"), lax.axis_index("zl")
    place = lax.axis_index("x") * 8 + lax.axis_index("zh") * 2 + near
    cos_t = turn_ref[0][:, None, :]
    sin_t = turn_ref[1][:, None, :]
    rows = STEPS * SLICE

    def turned(real, imag, sign):
        real = real.reshape(STEPS, SLICE, INNER)
        imag = imag.reshape(STEPS, SLICE, INNER)
        one = real * cos_t - (sign * imag) * sin_t
        two = imag * cos_t + (sign * real) * sin_t
        return one.reshape(rows, INNER), two.reshape(rows, INNER)

    outs = []
    for s in range(2):
        got = got_ref[:, s].astype(jnp.float32).reshape(16, 2, 2, SLICE, BLOCK)
        source = got[:, :, 0].reshape(BLOCKS * SLICE, BLOCK)
        taps = got[:, :, 1].reshape(BLOCKS * SLICE, BLOCK)
        both = jnp.concatenate(
            [
                jnp.concatenate([source[:, :INNER], taps[:, :INNER]], 1),
                jnp.concatenate([source[:, INNER:], taps[:, INNER:]], 1),
            ],
            0,
        ).astype(jnp.bfloat16)
        first = dot(first_ref[...], jnp.concatenate([both, both], 0))
        spectra = []
        for part in range(2):
            columns = slice(part * INNER, (part + 1) * INNER)
            real, imag = turned(first[:rows, columns], first[rows:, columns], -1.0)
            high, low = split(jnp.concatenate([real, imag], 1))
            spectra.append(dot(jnp.concatenate([high, low, high], 1), ahead_ref[...]))
        (ar, ai), (br, bi) = [(z[:, :INNER], z[:, INNER:]) for z in spectra]
        product = jnp.concatenate([ar * br - ai * bi, ar * bi + ai * br], 1)
        high, low = split(product)
        inner = dot(jnp.concatenate([high, low, high], 1), back_ref[...])
        real, imag = turned(inner[:, :INNER], inner[:, INNER:], 1.0)
        high, low = split(jnp.concatenate([real, imag], 0))
        conv = dot(last_ref[...], jnp.concatenate([high, low, high], 0))
        conv = jnp.concatenate([conv[: BLOCKS * SLICE], conv[BLOCKS * SLICE :]], 1)
        channel = core * HALF + place * SLICE + lax.broadcasted_iota(jnp.int32, (SLICE, BLOCK), 0)
        picked = channel == lax.broadcasted_iota(jnp.int32, (SLICE, BLOCK), 1)
        gains = jnp.where(near == s, own_ref[...], other_ref[...])
        gain = jnp.sum(jnp.where(picked, gains, 0.0), 1, keepdims=True)
        total = conv.reshape(BLOCKS, SLICE, BLOCK) + gain[None] * source.reshape(BLOCKS, SLICE, BLOCK)
        outs.append(total)
    out_ref[...] = jnp.concatenate(outs, 1).astype(jnp.bfloat16)


def convolve(got, own_gain, other_gain):
    return pl.pallas_call(
        convolve_kernel,
        out_shape=jax.ShapeDtypeStruct((BLOCKS, 2 * SLICE, BLOCK), jnp.bfloat16),
        in_specs=[whole()] * 8,
        out_specs=whole(),
        compiler_params=params(),
        name="convolve",
    )(got, own_gain, other_gain, *tables())


def gate_kernel(conv_ref, near_ref, sibling_ref, crossed_ref, out_ref):
    core, line = lax.axis_index("core"), lax.axis_index("zl")
    kept = jnp.where(core == line, near_ref[...].astype(jnp.float32), sibling_ref[...].astype(jnp.float32))
    crossed = crossed_ref[...].astype(jnp.float32)
    conv = conv_ref[...].astype(jnp.float32).reshape(BLOCKS, 2, SLICE, BLOCK)
    for s in range(2):
        query = jnp.where(line == s, kept, crossed)
        gated = query * conv[:, s].reshape(HALF, BLOCK)
        out_ref[:, s * HALF : (s + 1) * HALF] = gated.T.astype(jnp.bfloat16)


def gate(conv, near, sibling, crossed):
    return pl.pallas_call(
        gate_kernel,
        out_shape=jax.ShapeDtypeStruct((BLOCK, BLOCK), jnp.bfloat16),
        in_specs=[whole()] * 4,
        out_specs=whole(),
        compiler_params=params(),
        name="gate",
    )(conv, near, sibling, crossed)


def project_kernel(*refs):
    pieces, weight_ref, out_ref = refs[:8], refs[8], refs[9]
    core, y = lax.axis_index("core"), lax.axis_index("y")
    total = None
    for index, piece in enumerate(pieces):
        back, sibling = index // 2, index % 2
        owner = lax.rem(y + 4 - back, 4)
        side = 1 - core if sibling else core
        for s in range(2):
            start = pl.multiple_of(owner * 1024 + s * 512 + side * HALF, HALF)
            term = dot(piece[:, s * HALF : (s + 1) * HALF], weight_ref[pl.ds(start, HALF), :])
            total = term if total is None else total + term
    out_ref[...] = total.astype(jnp.bfloat16)


def project(pieces, weight):
    return pl.pallas_call(
        project_kernel,
        out_shape=jax.ShapeDtypeStruct((BLOCK, BLOCK), jnp.bfloat16),
        in_specs=[whole()] * 9,
        out_specs=whole(),
        compiler_params=params(),
        name="project",
    )(*pieces, weight)


def on_device(query, key, value, taps, gain, weight):
    core, line = lax.axis_index("core"), lax.axis_index("zl")
    weight = lax.ppermute(weight, ("core", "zl"), SWAP)
    weight = lax.all_gather(weight, LINE, axis=0, tiled=True)
    far = prepare(True, key, value, taps)
    arrived = lax.ppermute(far, "core", PAIR)
    near = prepare(False, key, value, taps)
    blocks = jnp.where(core == 0, jnp.stack([near, arrived], 1), jnp.stack([arrived, near], 1))
    got = lax.all_to_all(blocks, LINE, 0, 0, tiled=True)
    got = got.reshape(16, 2, 2, 2 * SLICE, BLOCK)
    gain = gain.reshape(1, BLOCK)
    other_gain = lax.ppermute(gain, "zl", PAIR)
    query_near, query_far = turn_query(query)
    sibling = lax.ppermute(query_far, "core", PAIR)
    crossing = jnp.where(core == line, sibling, query_near)
    crossed = lax.ppermute(crossing, "zl", PAIR)
    conv = convolve(got, gain, other_gain)
    conv = lax.all_to_all(conv, LINE, 0, 0, tiled=True)
    gated = gate(conv, query_near, sibling, crossed)
    pieces = [gated] + [lax.ppermute(gated, "y", [(i, (i + k) % 4) for i in range(4)]) for k in (1, 2, 3)]
    both = []
    for piece in pieces:
        both += [piece, lax.ppermute(piece, "core", PAIR)]
    mixed = project(both, weight)
    return lax.ppermute(mixed, ("core", "zl"), SWAP)


def solution(mesh):
    fine = Mesh(mesh.devices.reshape(4, 4, 2, 4, 2), AXES)
    rows, columns = ("x", "zh", "core"), ("y", "zl")
    placed = P(rows, columns)
    return jax.shard_map(
        on_device,
        mesh=fine,
        in_specs=(placed, placed, placed, placed, P(columns), placed),
        out_specs=placed,
        check_vma=False,
    )
```

time: 707 us -> 177 us (0.25); the launches traced: 697 us -> 176 us
  waiting for transfers between devices: 369 us -> 76.5 us
  matrix products: 150 us -> 0 us
  blocking collectives: 75.1 us -> 0 us
  local copies, waits for them, and re-layouts: 44.4 us -> 5.1 us
  Pallas kernels: 0 us -> 31.6 us
    all_to_all x7 -> x2, waiting for transfers between devices: 279 us -> 3.95 us  [the longest x1 3.95 us: on_device(): got = lax.all_to_all(blocks, LINE, 0, 0, tiled=True)]
    dot_general x19 -> x0, matrix products: 150 us -> none  [the longest x18 144 us: contract(): return jnp.einsum(pattern, matrix, operand, precision=lax.Precision.HIGHEST)]
    all_gather x2 -> x1, waiting for transfers between devices: 89.1 us -> 0.01 us  [on_device(): weight = lax.all_gather(weight, LINE, axis=0, tiled=True)]
    all_to_all x2 -> x0, blocking collectives: 75.1 us -> none  [the longest x1 41.3 us: forward(): lax.all_to_all(blocks, 'ctx', split_axis=0, concat_axis=0, tiled=True)]
    ppermute x0 -> x13, waiting for transfers between devices: none -> 72.5 us  [the longest x1 25.9 us: on_device(): other_gain = lax.ppermute(gain, 'zl', PAIR)]
    pallas_call x0 -> x6, Pallas kernels: none -> 31.6 us  [the longest x1 15.4 us: convolve(): pl.pallas_call(convolve_kernel, out_shape=jax.ShapeDtypeStruct((BLOCKS, 2...]
    ppermute x0 -> x13, starting transfers between devices: none -> 29.5 us  [the longest x4 14.3 us: on_device(): both += [piece, lax.ppermute(piece, 'core', PAIR)]]
    all_to_all x7 -> x2, starting transfers between devices: 41.5 us -> 17.6 us  [the longest x1 10.8 us: on_device(): got = lax.all_to_all(blocks, LINE, 0, 0, tiled=True)]
  transfers between devices with their start and end apart: 9 -> 16, of which waited for: 8 -> 9; matrix products, arithmetic and copies ran while one was open for 12% -> 2% of each run, Pallas kernels for 0% -> 14%
where the time goes in v1:
time: 177 us; the launch traced here: 176 us
  waiting for transfers between devices  76.5 us (43%)
  starting transfers between devices  47.1 us (27%)
  Pallas kernels  31.6 us (18%)
  between operations  13.5 us (8%)
  local copies, waits for them, and re-layouts  5.1 us (3%)
  other arithmetic  2.43 us (1%)
    ppermute x1, waiting for transfers between devices, on_device(): other_gain = lax.ppermute(gain, 'zl', PAIR)  25.9 us
    ppermute x1, waiting for transfers between devices, on_device(): crossed = lax.ppermute(crossing, 'zl', PAIR)  21.7 us
    pallas_call x1, Pallas kernels, convolve(): pl.pallas_call(convolve_kernel, out_shape=jax.ShapeDtypeStruct((BLOCKS, 2...  15.4 us
    ppermute x4, starting transfers between devices, on_device(): both += [piece, lax.ppermute(piece, 'core', PAIR)]  14.3 us
    ppermute x3, waiting for transfers between devices, on_device(): lax.ppermute(gated, 'y', [(i, (i + k) % 4) for i in range(4)])  12 us
    all_to_all x1, starting transfers between devices, on_device(): got = lax.all_to_all(blocks, LINE, 0, 0, tiled=True)  10.8 us
    ppermute x1, waiting for transfers between devices, on_device(): return lax.ppermute(mixed, ('core', 'zl'), SWAP)  7.06 us
    all_to_all x1, starting transfers between devices, on_device(): conv = lax.all_to_all(conv, LINE, 0, 0, tiled=True)  6.78 us
  transfers between devices with their start and end apart: 16, of which 9 were waited for; matrix products, arithmetic and copies ran while one was open for 2% of the time, Pallas kernels for 14%

profile of v1, /device:TPU:1, one launch (start us, length us, event | category | flops | bytes accessed | tf_op | source)
XLA Modules:
  0.0 176.3 jit_solution(7057830192942824655)
XLA Ops:
  6.5 4.9 %collective-permute-start.11 = (bf16[128,512]{1,0:T(8,128)(2,1)}, bf16[128,512]{1,0:T(8,128)(2,1)S(1)}, u32[]{:S(2)}, u32[]{:S(2)}) collective-permute-start(bf16[128,512]{1,0:T(8,128)(2,1)} %param.16), channel_id=1, source_target_pairs={{0,0},{1,8},{8,1},{9,9},{2,2},{3,10},{10,3},{11,11},{4,4},{5,12},{... | collective-permute-start | bytes 393224 | tf_op jit(solution)/shard_map/ppermute | solution.py:229
  11.5 2.8 %collective-permute-done.11 = bf16[128,512]{1,0:T(8,128)(2,1)S(1)} collective-permute-done((bf16[128,512]{1,0:T(8,128)(2,1)}, bf16[128,512]{1,0:T(8,128)(2,1)S(1)}, u32[]{:S(2)}, u32[]{:S(2)}) %collective-permute-start.11) | collective-permute-done | bytes 131104 | tf_op jit(solution)/shard_map/ppermute | solution.py:229
  14.3 0.6 copy-done.10
  15.0 0.0 all-gather.2.cloned.1.call-update
  15.0 2.6 %prepare_far.1 = bf16[32,16,512]{2,1,0:T(8,128)(2,1)} custom-call(bf16[512,512]{1,0:T(8,128)(2,1)} %key_ref.3, bf16[512,512]{1,0:T(8,128)(2,1)} %value_ref.3, f32[512,512]{1,0:T(8,128)} %filter_ref.3), custom_call_target="tpu_custom_call" | custom-call | tf_op jit(solution)/shard_map/prepare_far/pallas_call | solution.py:90
  17.5 0.0 collective-permute-start
  17.5 2.6 %prepare_near.1 = bf16[32,16,512]{2,1,0:T(8,128)(2,1)} custom-call(bf16[512,512]{1,0:T(8,128)(2,1)} %key_ref.3, bf16[512,512]{1,0:T(8,128)(2,1)} %value_ref.3, f32[512,512]{1,0:T(8,128)} %filter_ref.3), custom_call_target="tpu_custom_call" | custom-call | tf_op jit(solution)/shard_map/prepare_near/pallas_call | solution.py:90
  20.1 0.0 collective-permute-done
  20.1 1.4 maximum_select_fusion
  21.5 0.0 copy-start.11
  21.5 1.1 copy.13
  22.6 10.8 %all-to-all-start = ((bf16[32,2,16,512]{3,2,1,0:T(8,128)(2,1)}), bf16[32,2,16,512]{3,2,1,0:T(8,128)(2,1)S(1)}, u32[]{:S(2)}, u32[]{:S(2)}) async-start(bf16[32,2,16,512]{3,2,1,0:T(8,128)(2,1)} %copy.13), calls=%async_computation | async-start | bytes 2097152 | tf_op jit(solution)/shard_map/all_to_all | solution.py:235
  33.4 1.3 collective-permute-start.1
  34.7 25.9 %collective-permute-done.1.other_ref = f32[1,512]{1,0:T(1,128)S(1)} collective-permute-done((f32[1,512]{1,0:T(1,128)S(1)}, f32[1,512]{1,0:T(1,128)S(1)}, u32[]{:S(2)}, u32[]{:S(2)}) %collective-permute-start.1) | collective-permute-done | bytes 2080 | tf_op jit(solution)/shard_map/ppermute | solution.py:238
  60.6 3.9 %all-to-all-done = bf16[32,2,16,512]{3,2,1,0:T(8,128)(2,1)S(1)} async-done(((bf16[32,2,16,512]{3,2,1,0:T(8,128)(2,1)}), bf16[32,2,16,512]{3,2,1,0:T(8,128)(2,1)S(1)}, u32[]{:S(2)}, u32[]{:S(2)}) %all-to-all-start) | async-done | bytes 1048608 | tf_op jit(solution)/shard_map/all_to_all | solution.py:235
  64.5 1.0 copy-done
  65.6 15.4 %convolve.1 = bf16[32,16,512]{2,1,0:T(8,128)(2,1)} custom-call(bf16[16,2,2,16,512]{4,3,2,1,0:T(8,128)(2,1)} %bitcast.4, f32[1,512]{1,0:T(1,128)} %bitcast.7, f32[1,512]{1,0:T(1,128)} %copy-done.12, bf16[1024,1024]{1,0:T(8,128)(2,1)} %constant.20.clone.first_ref, f32[2,64,256]{2,1,0:T(8,128)} %constant.21.clone.turn_ref, ...), custom_call_target="tpu_custom_call" | custom-call | tf_op jit(solution)/shard_map/convolve/pallas_call | solution.py:169
  81.0 6.8 %all-to-all-start.1 = ((bf16[32,16,512]{2,1,0:T(8,128)(2,1)}), bf16[32,16,512]{2,1,0:T(8,128)(2,1)S(1)}, u32[]{:S(2)}, u32[]{:S(2)}) async-start(bf16[32,16,512]{2,1,0:T(8,128)(2,1)} %convolve.1), calls=%async_computation.1 | async-start | bytes 1048576 | tf_op jit(solution)/shard_map/all_to_all | solution.py:244
  87.8 2.0 %turn_query.1 = (bf16[256,512]{1,0:T(8,128)(2,1)}, bf16[256,512]{1,0:T(8,128)(2,1)}) custom-call(bf16[512,512]{1,0:T(8,128)(2,1)} %query_ref.1), custom_call_target="tpu_custom_call" | custom-call | tf_op jit(solution)/shard_map/turn_query/pallas_call | solution.py:108
  89.8 0.9 collective-permute-start.2
  90.7 1.4 collective-permute-done.2.sibling_ref
  92.0 1.1 broadcast_select_fusion
  93.1 0.7 collective-permute-start.3
  93.8 21.7 %collective-permute-done.3.crossed_ref = bf16[256,512]{1,0:T(8,128)(2,1)S(1)} collective-permute-done((bf16[256,512]{1,0:T(8,128)(2,1)S(1)}, bf16[256,512]{1,0:T(8,128)(2,1)S(1)}, u32[]{:S(2)}, u32[]{:S(2)}) %collective-permute-start.3) | collective-permute-done | bytes 262176 | tf_op jit(solution)/shard_map/ppermute | solution.py:242
  115.5 0.0 all-to-all-done.1.conv_ref
  115.6 0.7 copy-done.9
  116.3 0.8 copy-done.1
  117.1 2.4 %gate.1.refs_0_ = bf16[512,512]{1,0:T(8,128)(2,1)} custom-call(bf16[32,16,512]{2,1,0:T(8,128)(2,1)} %copy-done.1, bf16[256,512]{1,0:T(8,128)(2,1)} %get-tuple-element.7.near_ref, bf16[256,512]{1,0:T(8,128)(2,1)} %copy-done.2, bf16[256,512]{1,0:T(8,128)(2,1)} %copy-done.9), custom_call_target="tpu_custom_call" | custom-call | tf_op jit(solution)/shard_map/gate/pallas_call | solution.py:191
  119.4 2.8 %collective-permute-start.9 = (bf16[512,512]{1,0:T(8,128)(2,1)}, bf16[512,512]{1,0:T(8,128)(2,1)S(1)}, u32[]{:S(2)}, u32[]{:S(2)}) collective-permute-start(bf16[512,512]{1,0:T(8,128)(2,1)} %gate.1.refs_0_), channel_id=1, source_target_pairs={{0,6},{2,0},{4,2},{6,4},{1,7},{3,1},{5,3},{7,5},{8,14},{10,8},{12,... | collective-permute-start | bytes 1572872 | tf_op jit(solution)/shard_map/ppermute | solution.py:246
  122.2 0.5 collective-permute-start.7
  122.7 0.5 collective-permute-start.5
  123.2 1.9 %collective-permute-start.4 = (bf16[512,512]{1,0:T(8,128)(2,1)}, bf16[512,512]{1,0:T(8,128)(2,1)S(1)}, u32[]{:S(2)}, u32[]{:S(2)}) collective-permute-start(bf16[512,512]{1,0:T(8,128)(2,1)} %gate.1.refs_0_), channel_id=1, source_target_pairs={{0,8},{8,0},{1,9},{9,1},{2,10},{10,2},{3,11},{11,3},{4,12},{12,4},... | collective-permute-start | bytes 1572872 | tf_op jit(solution)/shard_map/ppermute | solution.py:249
  125.1 9.0 %collective-permute-done.9.refs_6_ = bf16[512,512]{1,0:T(8,128)(2,1)S(1)} collective-permute-done((bf16[512,512]{1,0:T(8,128)(2,1)}, bf16[512,512]{1,0:T(8,128)(2,1)S(1)}, u32[]{:S(2)}, u32[]{:S(2)}) %collective-permute-start.9) | collective-permute-done | bytes 524320 | tf_op jit(solution)/shard_map/ppermute | solution.py:246
  134.1 11.8 %collective-permute-start.10 = (bf16[512,512]{1,0:T(8,128)(2,1)S(1)}, bf16[512,512]{1,0:T(8,128)(2,1)S(1)}, u32[]{:S(2)}, u32[]{:S(2)}) collective-permute-start(bf16[512,512]{1,0:T(8,128)(2,1)S(1)} %collective-permute-done.9.refs_6_), channel_id=1, source_target_pairs={{0,8},{8,0},{1,9},{9,1},{2,10},{10,2},{3,11},{11,3},{4,12},{12,4},... | collective-permute-start | bytes 1572872 | tf_op jit(solution)/shard_map/ppermute | solution.py:249
  145.9 0.0 collective-permute-done.7.refs_4_
  145.9 0.1 collective-permute-start.8
  146.0 3.0 %collective-permute-done.5.refs_2_ = bf16[512,512]{1,0:T(8,128)(2,1)S(1)} collective-permute-done((bf16[512,512]{1,0:T(8,128)(2,1)}, bf16[512,512]{1,0:T(8,128)(2,1)S(1)}, u32[]{:S(2)}, u32[]{:S(2)}) %collective-permute-start.5) | collective-permute-done | bytes 524320 | tf_op jit(solution)/shard_map/ppermute | solution.py:246
  149.0 0.5 collective-permute-start.6
  149.5 0.0 collective-permute-done.4.refs_1_
  149.5 0.0 collective-permute-done.10.refs_7_
  149.5 0.0 collective-permute-done.8.refs_5_
  149.5 0.0 copy-start.8
  149.6 1.6 collective-permute-done.6.refs_3_
  151.2 0.0 copy-done.5
  151.2 6.7 %project.1 = bf16[512,512]{1,0:T(8,128)(2,1)} custom-call(bf16[512,512]{1,0:T(8,128)(2,1)} %gate.1.refs_0_, bf16[512,512]{1,0:T(8,128)(2,1)} %copy-done.6, bf16[512,512]{1,0:T(8,128)(2,1)} %copy-done.5, bf16[512,512]{1,0:T(8,128)(2,1)} %collective-permute-done.6.refs_3_, bf16[512,512]{1,0:T(8,128)(2,1)} %copy-done.4, bf16[512,512]{1,0:T(8,128)(2,1)} %copy-done.8, ...), custom_call_target="tpu_custom_call" | custom-call | tf_op jit(solution)/shard_map/project/pallas_call | solution.py:217
  157.9 3.7 %collective-permute-start.12 = (bf16[512,512]{1,0:T(8,128)(2,1)}, bf16[512,512]{1,0:T(8,128)(2,1)S(1)}, u32[]{:S(2)}, u32[]{:S(2)}) collective-permute-start(bf16[512,512]{1,0:T(8,128)(2,1)} %project.1), channel_id=1, source_target_pairs={{0,0},{1,8},{8,1},{9,9},{2,2},{3,10},{10,3},{11,11},{4,4},{5,12},{... | collective-permute-start | bytes 1572872 | tf_op jit(solution)/shard_map/ppermute | solution.py:251
  161.6 7.1 %collective-permute-done.12 = bf16[512,512]{1,0:T(8,128)(2,1)S(1)} collective-permute-done((bf16[512,512]{1,0:T(8,128)(2,1)}, bf16[512,512]{1,0:T(8,128)(2,1)S(1)}, u32[]{:S(2)}, u32[]{:S(2)}) %collective-permute-start.12) | collective-permute-done | bytes 524320 | tf_op jit(solution)/shard_map/ppermute | solution.py:251
  168.6 0.8 copy.15
  (21 shorter events, 0.0 us)
Async XLA Ops:
  6.5 144.7 %all-gather.2.cloned.1.call-start = ((), (), s32[]{:S(2)}) async-start(), calls=%async_computation.2 | async-start | bytes 4325376 | tf_op jit(solution)/shard_map/all_gather | solution.py:230
  6.5 7.8 %collective-permute-start.11 = (bf16[128,512]{1,0:T(8,128)(2,1)}, bf16[128,512]{1,0:T(8,128)(2,1)S(1)}, u32[]{:S(2)}, u32[]{:S(2)}) collective-permute-start(bf16[128,512]{1,0:T(8,128)(2,1)} %param.16), channel_id=1, source_target_pairs={{0,0},{1,8},{8,1},{9,9},{2,2},{3,10},{10,3},{11,11},{4,4},{5,12},{... | collective-permute-start | bytes 393224 | tf_op jit(solution)/shard_map/ppermute | solution.py:229
  14.3 0.7 copy-start.10
  17.5 2.6 %collective-permute-start = (bf16[32,16,512]{2,1,0:T(8,128)(2,1)}, bf16[32,16,512]{2,1,0:T(8,128)(2,1)S(1)}, u32[]{:S(2)}, u32[]{:S(2)}) collective-permute-start(bf16[32,16,512]{2,1,0:T(8,128)(2,1)} %prepare_far.1), channel_id=1, source_target_pairs={{0,8},{8,0},{1,9},{9,1},{2,10},{10,2},{3,11},{11,3},{4,12},{12,4},... | collective-permute-start | bytes 1572872 | tf_op jit(solution)/shard_map/ppermute | solution.py:232
  21.5 11.9 %copy-start.11 = (f32[512]{0:T(512)S(1)}, f32[512]{0:T(512)}, u32[]{:S(2)}) copy-start(f32[512]{0:T(512)} %param.15) | copy-start | bytes 6148
  22.6 42.0 %all-to-all-start = ((bf16[32,2,16,512]{3,2,1,0:T(8,128)(2,1)}), bf16[32,2,16,512]{3,2,1,0:T(8,128)(2,1)S(1)}, u32[]{:S(2)}, u32[]{:S(2)}) async-start(bf16[32,2,16,512]{3,2,1,0:T(8,128)(2,1)} %copy.13), calls=%async_computation | async-start | bytes 2097152 | tf_op jit(solution)/shard_map/all_to_all | solution.py:235
  33.4 27.2 %collective-permute-start.1 = (f32[1,512]{1,0:T(1,128)S(1)}, f32[1,512]{1,0:T(1,128)S(1)}, u32[]{:S(2)}, u32[]{:S(2)}) collective-permute-start(f32[1,512]{1,0:T(1,128)S(1)} %bitcast.8), channel_id=1, source_target_pairs={{0,1},{1,0},{2,3},{3,2},{4,5},{5,4},{6,7},{7,6},{8,9},{9,8},{10,11... | collective-permute-start | bytes 6152 | tf_op jit(solution)/shard_map/ppermute | solution.py:238
  60.6 4.0 %copy-start.12 = (f32[1,512]{1,0:T(1,128)}, f32[1,512]{1,0:T(1,128)S(1)}, u32[]{:S(2)}) copy-start(f32[1,512]{1,0:T(1,128)S(1)} %collective-permute-done.1.other_ref) | copy-start | bytes 6148
  64.5 1.0 copy-start
  81.0 34.6 %all-to-all-start.1 = ((bf16[32,16,512]{2,1,0:T(8,128)(2,1)}), bf16[32,16,512]{2,1,0:T(8,128)(2,1)S(1)}, u32[]{:S(2)}, u32[]{:S(2)}) async-start(bf16[32,16,512]{2,1,0:T(8,128)(2,1)} %convolve.1), calls=%async_computation.1 | async-start | bytes 1048576 | tf_op jit(solution)/shard_map/all_to_all | solution.py:244
  89.8 2.3 %collective-permute-start.2 = (bf16[256,512]{1,0:T(8,128)(2,1)}, bf16[256,512]{1,0:T(8,128)(2,1)S(1)}, u32[]{:S(2)}, u32[]{:S(2)}) collective-permute-start(bf16[256,512]{1,0:T(8,128)(2,1)} %get-tuple-element.8), channel_id=1, source_target_pairs={{0,8},{8,0},{1,9},{9,1},{2,10},{10,2},{3,11},{11,3},{4,12},{12,4},... | collective-permute-start | bytes 786440 | tf_op jit(solution)/shard_map/ppermute | solution.py:240
  92.0 23.5 %copy-start.2 = (bf16[256,512]{1,0:T(8,128)(2,1)}, bf16[256,512]{1,0:T(8,128)(2,1)S(1)}, u32[]{:S(2)}) copy-start(bf16[256,512]{1,0:T(8,128)(2,1)S(1)} %collective-permute-done.2.sibling_ref) | copy-start | bytes 786436
  93.1 22.4 %collective-permute-start.3 = (bf16[256,512]{1,0:T(8,128)(2,1)S(1)}, bf16[256,512]{1,0:T(8,128)(2,1)S(1)}, u32[]{:S(2)}, u32[]{:S(2)}) collective-permute-start(bf16[256,512]{1,0:T(8,128)(2,1)S(1)} %broadcast_select_fusion), channel_id=1, source_target_pairs={{0,1},{1,0},{2,3},{3,2},{4,5},{5,4},{6,7},{7,6},{8,9},{9,8},{10,11... | collective-permute-start | bytes 786440 | tf_op jit(solution)/shard_map/ppermute | solution.py:242
  115.5 0.7 copy-start.9
  116.3 0.8 copy-start.1
  119.4 14.7 %collective-permute-start.9 = (bf16[512,512]{1,0:T(8,128)(2,1)}, bf16[512,512]{1,0:T(8,128)(2,1)S(1)}, u32[]{:S(2)}, u32[]{:S(2)}) collective-permute-start(bf16[512,512]{1,0:T(8,128)(2,1)} %gate.1.refs_0_), channel_id=1, source_target_pairs={{0,6},{2,0},{4,2},{6,4},{1,7},{3,1},{5,3},{7,5},{8,14},{10,8},{12,... | collective-permute-start | bytes 1572872 | tf_op jit(solution)/shard_map/ppermute | solution.py:246
  122.2 23.7 %collective-permute-start.7 = (bf16[512,512]{1,0:T(8,128)(2,1)}, bf16[512,512]{1,0:T(8,128)(2,1)S(1)}, u32[]{:S(2)}, u32[]{:S(2)}) collective-permute-start(bf16[512,512]{1,0:T(8,128)(2,1)} %gate.1.refs_0_), channel_id=1, source_target_pairs={{0,4},{2,6},{4,0},{6,2},{1,5},{3,7},{5,1},{7,3},{8,12},{10,14},{12... | collective-permute-start | bytes 1572872 | tf_op jit(solution)/shard_map/ppermute | solution.py:246
  122.7 26.3 %collective-permute-start.5 = (bf16[512,512]{1,0:T(8,128)(2,1)}, bf16[512,512]{1,0:T(8,128)(2,1)S(1)}, u32[]{:S(2)}, u32[]{:S(2)}) collective-permute-start(bf16[512,512]{1,0:T(8,128)(2,1)} %gate.1.refs_0_), channel_id=1, source_target_pairs={{0,2},{2,4},{4,6},{6,0},{1,3},{3,5},{5,7},{7,1},{8,10},{10,12},{12... | collective-permute-start | bytes 1572872 | tf_op jit(solution)/shard_map/ppermute | solution.py:246
  123.2 26.3 %collective-permute-start.4 = (bf16[512,512]{1,0:T(8,128)(2,1)}, bf16[512,512]{1,0:T(8,128)(2,1)S(1)}, u32[]{:S(2)}, u32[]{:S(2)}) collective-permute-start(bf16[512,512]{1,0:T(8,128)(2,1)} %gate.1.refs_0_), channel_id=1, source_target_pairs={{0,8},{8,0},{1,9},{9,1},{2,10},{10,2},{3,11},{11,3},{4,12},{12,4},... | collective-permute-start | bytes 1572872 | tf_op jit(solution)/shard_map/ppermute | solution.py:249
  134.1 17.1 %copy-start.3 = (bf16[512,512]{1,0:T(8,128)(2,1)}, bf16[512,512]{1,0:T(8,128)(2,1)S(1)}, u32[]{:S(2)}) copy-start(bf16[512,512]{1,0:T(8,128)(2,1)S(1)} %collective-permute-done.9.refs_6_) | copy-start | bytes 1572868
  134.1 15.4 %collective-permute-start.10 = (bf16[512,512]{1,0:T(8,128)(2,1)S(1)}, bf16[512,512]{1,0:T(8,128)(2,1)S(1)}, u32[]{:S(2)}, u32[]{:S(2)}) collective-permute-start(bf16[512,512]{1,0:T(8,128)(2,1)S(1)} %collective-permute-done.9.refs_6_), channel_id=1, source_target_pairs={{0,8},{8,0},{1,9},{9,1},{2,10},{10,2},{3,11},{11,3},{4,12},{12,4},... | collective-permute-start | bytes 1572872 | tf_op jit(solution)/shard_map/ppermute | solution.py:249
  145.9 5.3 %copy-start.4 = (bf16[512,512]{1,0:T(8,128)(2,1)}, bf16[512,512]{1,0:T(8,128)(2,1)S(1)}, u32[]{:S(2)}) copy-start(bf16[512,512]{1,0:T(8,128)(2,1)S(1)} %collective-permute-done.7.refs_4_) | copy-start | bytes 1572868
  145.9 3.6 %collective-permute-start.8 = (bf16[512,512]{1,0:T(8,128)(2,1)S(1)}, bf16[512,512]{1,0:T(8,128)(2,1)S(1)}, u32[]{:S(2)}, u32[]{:S(2)}) collective-permute-start(bf16[512,512]{1,0:T(8,128)(2,1)S(1)} %collective-permute-done.7.refs_4_), channel_id=1, source_target_pairs={{0,8},{8,0},{1,9},{9,1},{2,10},{10,2},{3,11},{11,3},{4,12},{12,4},... | collective-permute-start | bytes 1572872 | tf_op jit(solution)/shard_map/ppermute | solution.py:249
  149.0 2.2 %copy-start.5 = (bf16[512,512]{1,0:T(8,128)(2,1)}, bf16[512,512]{1,0:T(8,128)(2,1)S(1)}, u32[]{:S(2)}) copy-start(bf16[512,512]{1,0:T(8,128)(2,1)S(1)} %collective-permute-done.5.refs_2_) | copy-start | bytes 1572868
  149.0 2.2 %collective-permute-start.6 = (bf16[512,512]{1,0:T(8,128)(2,1)S(1)}, bf16[512,512]{1,0:T(8,128)(2,1)}, u32[]{:S(2)}, u32[]{:S(2)}) collective-permute-start(bf16[512,512]{1,0:T(8,128)(2,1)S(1)} %collective-permute-done.5.refs_2_), channel_id=1, source_target_pairs={{0,8},{8,0},{1,9},{9,1},{2,10},{10,2},{3,11},{11,3},{4,12},{12,4},... | collective-permute-start | bytes 1572872 | tf_op jit(solution)/shard_map/ppermute | solution.py:249
  149.5 1.7 copy-start.6
  149.5 1.7 copy-start.7
  149.5 1.7 copy-start.8
  157.9 10.7 %collective-permute-start.12 = (bf16[512,512]{1,0:T(8,128)(2,1)}, bf16[512,512]{1,0:T(8,128)(2,1)S(1)}, u32[]{:S(2)}, u32[]{:S(2)}) collective-permute-start(bf16[512,512]{1,0:T(8,128)(2,1)} %project.1), channel_id=1, source_target_pairs={{0,0},{1,8},{8,1},{9,9},{2,2},{3,10},{10,3},{11,11},{4,4},{5,12},{... | collective-permute-start | bytes 1572872 | tf_op jit(solution)/shard_map/ppermute | solution.py:251
Sparse Core Ops, SparseCore 0:
  15.1 98.9 all-gather.1

commit v2 on v1

--- a/solution.py
+++ b/solution.py
@@ -19,9 +19,9 @@
 STEPS = 64
 INNER = 256
 PERIOD = 32768
-VMEM = 56 * 1024 * 1024
 SWAP = [(0, 0), (1, 2), (2, 1), (3, 3)]
 PAIR = [(0, 1), (1, 0)]
+ROWS = [(4 * h + 2 * a + b, 4 * h + 2 * b + a) for h in range(2) for a in range(2) for b in range(2)]
 
 
 def halves(table):
@@ -68,32 +68,56 @@
     return high, (value - high.astype(jnp.float32)).astype(jnp.bfloat16)
 
 
-def params():
-    return pltpu.CompilerParams(vmem_limit_bytes=VMEM)
+def params(mebibytes):
+    return pltpu.CompilerParams(vmem_limit_bytes=mebibytes * 1024 * 1024)
 
 
 def whole():
     return pl.BlockSpec(memory_space=pltpu.VMEM)
 
 
-def prepare_kernel(far, key_ref, value_ref, filter_ref, out_ref):
-    core = lax.axis_index("core")
-    half = 1 - core if far else core
-    columns = pl.ds(pl.multiple_of(half * HALF, HALF), HALF)
-    source = key_ref[:, columns].astype(jnp.float32) * value_ref[:, columns].astype(jnp.float32)
-    source = source.T.reshape(BLOCKS, SLICE, BLOCK)
-    taps = filter_ref[:, columns].T.reshape(BLOCKS, SLICE, BLOCK)
-    out_ref[...] = jnp.concatenate([source, taps], 1).astype(jnp.bfloat16)
-
-
-def prepare(far, key, value, taps):
-    return pl.pallas_call(
-        functools.partial(prepare_kernel, far),
-        out_shape=jax.ShapeDtypeStruct((BLOCKS, 2 * SLICE, BLOCK), jnp.bfloat16),
-        in_specs=[whole()] * 3,
-        out_specs=whole(),
-        compiler_params=params(),
-        name="prepare_far" if far else "prepare_near",
+def anywhere():
+    return pl.BlockSpec(memory_space=pl.ANY)
+
+
+def prepare_kernel(key_hbm, value_hbm, filter_hbm, out_hbm, key_ref, value_ref, filter_ref, out_ref, sems, out_sems):
+    moves = []
+    for i in range(4):
+        columns = pl.ds(i * 128, 128)
+        for j, (far, near) in enumerate(((key_hbm, key_ref), (value_hbm, value_ref), (filter_hbm, filter_ref))):
+            moves.append(pltpu.make_async_copy(far.at[:, columns], near.at[i], sems.at[i, j]))
+            moves[-1].start()
+    outs = []
+    for i in range(4):
+        for move in moves[3 * i : 3 * i + 3]:
+            move.wait()
+        source = key_ref[i].astype(jnp.float32) * value_ref[i].astype(jnp.float32)
+        source = source.T.reshape(8, 2, SLICE, BLOCK)
+        taps = filter_ref[i].T.reshape(8, 2, SLICE, BLOCK)
+        out_ref[i] = jnp.concatenate([source, taps], 2).astype(jnp.bfloat16)
+        place = out_hbm.at[pl.ds((i % 2) * 8, 8), i // 2]
+        outs.append(pltpu.make_async_copy(out_ref.at[i], place, out_sems.at[i]))
+        outs[-1].start()
+    for out in outs:
+        out.wait()
+
+
+def prepare(key, value, taps):
+    return pl.pallas_call(
+        prepare_kernel,
+        out_shape=jax.ShapeDtypeStruct((16, 2, 2, 2 * SLICE, BLOCK), jnp.bfloat16),
+        in_specs=[anywhere()] * 3,
+        out_specs=anywhere(),
+        scratch_shapes=[
+            pltpu.VMEM((4, BLOCK, 128), jnp.bfloat16),
+            pltpu.VMEM((4, BLOCK, 128), jnp.bfloat16),
+            pltpu.VMEM((4, BLOCK, 128), jnp.float32),
+            pltpu.VMEM((4, 8, 2, 2 * SLICE, BLOCK), jnp.bfloat16),
+            pltpu.SemaphoreType.DMA((4, 3)),
+            pltpu.SemaphoreType.DMA((4,)),
+        ],
+        compiler_params=params(56),
+        name="prepare",
     )(key, value, taps)
 
 
@@ -110,12 +134,17 @@
         out_shape=[jax.ShapeDtypeStruct((HALF, BLOCK), jnp.bfloat16)] * 2,
         in_specs=[whole()],
         out_specs=[whole()] * 2,
-        compiler_params=params(),
+        compiler_params=params(16),
         name="turn_query",
     )(query)
 
 
-def convolve_kernel(got_ref, own_ref, other_ref, first_ref, turn_ref, ahead_ref, back_ref, last_ref, out_ref):
+def convolve_kernel(got_ref, own_ref, other_ref, turn_ref, *refs):
+    out_ref, tables_here, sems = refs[4], refs[5:9], refs[9]
+    copies = [pltpu.make_async_copy(refs[i], tables_here[i], sems.at[i]) for i in range(4)]
+    for copy in copies:
+        copy.start()
+    first_ref, ahead_ref, back_ref, last_ref = tables_here
     core, near = lax.axis_index("core"), lax.axis_index("zl")
     place = lax.axis_index("x") * 8 + lax.axis_index("zh") * 2 + near
     cos_t = turn_ref[0][:, None, :]
@@ -131,7 +160,7 @@
 
     outs = []
     for s in range(2):
-        got = got_ref[:, s].astype(jnp.float32).reshape(16, 2, 2, SLICE, BLOCK)
+        got = got_ref[:, :, s].astype(jnp.float32).reshape(16, 2, 2, SLICE, BLOCK)
         source = got[:, :, 0].reshape(BLOCKS * SLICE, BLOCK)
         taps = got[:, :, 1].reshape(BLOCKS * SLICE, BLOCK)
         both = jnp.concatenate(
@@ -141,7 +170,11 @@
             ],
             0,
         ).astype(jnp.bfloat16)
+        if s == 0:
+            copies[0].wait()
         first = dot(first_ref[...], jnp.concatenate([both, both], 0))
+        if s == 0:
+            copies[1].wait()
         spectra = []
         for part in range(2):
             columns = slice(part * INNER, (part + 1) * INNER)
@@ -151,9 +184,13 @@
         (ar, ai), (br, bi) = [(z[:, :INNER], z[:, INNER:]) for z in spectra]
         product = jnp.concatenate([ar * br - ai * bi, ar * bi + ai * br], 1)
         high, low = split(product)
+        if s == 0:
+            copies[2].wait()
         inner = dot(jnp.concatenate([high, low, high], 1), back_ref[...])
         real, imag = turned(inner[:, :INNER], inner[:, INNER:], 1.0)
         high, low = split(jnp.concatenate([real, imag], 0))
+        if s == 0:
+            copies[3].wait()
         conv = dot(last_ref[...], jnp.concatenate([high, low, high], 0))
         conv = jnp.concatenate([conv[: BLOCKS * SLICE], conv[BLOCKS * SLICE :]], 1)
         channel = core * HALF + place * SLICE + lax.broadcasted_iota(jnp.int32, (SLICE, BLOCK), 0)
@@ -166,14 +203,17 @@
 
 
 def convolve(got, own_gain, other_gain):
+    first, turn, ahead, back, last = tables()
     return pl.pallas_call(
         convolve_kernel,
         out_shape=jax.ShapeDtypeStruct((BLOCKS, 2 * SLICE, BLOCK), jnp.bfloat16),
-        in_specs=[whole()] * 8,
+        in_specs=[whole()] * 4 + [pl.BlockSpec(memory_space=pl.ANY)] * 4,
         out_specs=whole(),
-        compiler_params=params(),
+        scratch_shapes=[pltpu.VMEM(table.shape, jnp.bfloat16) for table in (first, ahead, back, last)]
+        + [pltpu.SemaphoreType.DMA((4,))],
+        compiler_params=params(56),
         name="convolve",
-    )(got, own_gain, other_gain, *tables())
+    )(got, own_gain, other_gain, turn, first, ahead, back, last)
 
 
 def gate_kernel(conv_ref, near_ref, sibling_ref, crossed_ref, out_ref):
@@ -193,62 +233,122 @@
         out_shape=jax.ShapeDtypeStruct((BLOCK, BLOCK), jnp.bfloat16),
         in_specs=[whole()] * 4,
         out_specs=whole(),
-        compiler_params=params(),
+        compiler_params=params(16),
         name="gate",
     )(conv, near, sibling, crossed)
 
 
-def project_kernel(*refs):
-    pieces, weight_ref, out_ref = refs[:8], refs[8], refs[9]
-    core, y = lax.axis_index("core"), lax.axis_index("y")
-    total = None
-    for index, piece in enumerate(pieces):
-        back, sibling = index // 2, index % 2
-        owner = lax.rem(y + 4 - back, 4)
-        side = 1 - core if sibling else core
-        for s in range(2):
-            start = pl.multiple_of(owner * 1024 + s * 512 + side * HALF, HALF)
-            term = dot(piece[:, s * HALF : (s + 1) * HALF], weight_ref[pl.ds(start, HALF), :])
-            total = term if total is None else total + term
-    out_ref[...] = total.astype(jnp.bfloat16)
-
-
-def project(pieces, weight):
+def project_kernel(own_ref, after_ref, ahead_ref, *refs):
+    weights, (top_ref, low_ref, last_ref, held, sems) = refs[:5], refs[5:]
+    x, y = lax.axis_index("x"), lax.axis_index("y")
+    first, second = pl.ds(0, 2), pl.ds(2, 2)
+    parts = [(weights[0].at[first], weights[0].at[second]), (weights[1].at[first], weights[1].at[second])]
+    parts += [(weights[2], weights[3]), (weights[4].at[first], weights[4].at[second])]
+    steps = (0, 1, 3, 2)
+    for index, back in enumerate(steps):
+        away = lax.rem(x - y + back + 4, 4)
+        for number, pair in enumerate(parts):
+
+            @pl.when(away == number)
+            def _():
+                for half in range(2):
+                    pltpu.make_async_copy(pair[half], held.at[index, half], sems.at[index, half]).start()
+
+    pieces = (own_ref, after_ref, ahead_ref)
+    totals = [None, None]
+    for index in range(4):
+        for half in range(2):
+            pltpu.make_async_copy(weights[2], held.at[index, half], sems.at[index, half]).wait()
+        for side in range(2):
+            block = held[index, :, :, side].reshape(BLOCK, BLOCK)
+            if index < 3:
+                term = dot(pieces[index][...], block)
+                totals[side] = term if totals[side] is None else totals[side] + term
+            else:
+                last_ref[side] = block
+    for side in range(2):
+        top_ref[side] = totals[side][:HALF]
+        low_ref[side] = totals[side][HALF:]
+
+
+def project(pieces, weights):
+    part = jax.ShapeDtypeStruct((2, HALF, BLOCK), jnp.float32)
     return pl.pallas_call(
         project_kernel,
-        out_shape=jax.ShapeDtypeStruct((BLOCK, BLOCK), jnp.bfloat16),
-        in_specs=[whole()] * 9,
-        out_specs=whole(),
-        compiler_params=params(),
+        out_shape=[part, part, jax.ShapeDtypeStruct((2, BLOCK, BLOCK), jnp.bfloat16)],
+        in_specs=[whole()] * 3 + [anywhere()] * 5,
+        out_specs=[whole()] * 3,
+        scratch_shapes=[
+            pltpu.VMEM((4, 2, 2, 2, 128, BLOCK), jnp.bfloat16),
+            pltpu.SemaphoreType.DMA((4, 2)),
+        ],
+        compiler_params=params(24),
+        cost_estimate=pl.CostEstimate(flops=6 * BLOCK * BLOCK * 1024, bytes_accessed=8 * 2**20, transcendentals=0),
         name="project",
-    )(*pieces, weight)
+    )(*pieces, *weights)
+
+
+def finish_kernel(piece_ref, before_ref, weight_ref, keep_ref, send_ref):
+    core = lax.axis_index("core")
+    for side, ref in ((core, keep_ref), (1 - core, send_ref)):
+        ref[...] = before_ref[side] + dot(piece_ref[...], weight_ref[side])
+
+
+def finish(piece, before, weight):
+    return pl.pallas_call(
+        finish_kernel,
+        out_shape=[jax.ShapeDtypeStruct((HALF, BLOCK), jnp.float32)] * 2,
+        in_specs=[whole()] * 3,
+        out_specs=[whole()] * 2,
+        compiler_params=params(16),
+        name="finish",
+    )(piece, before, weight)
+
+
+def along(steps):
+    return [(i, (i + steps) % 4) for i in range(4)]
+
+
+def cross(value):
+    return lax.ppermute(value, "core", PAIR)
 
 
 def on_device(query, key, value, taps, gain, weight):
     core, line = lax.axis_index("core"), lax.axis_index("zl")
-    weight = lax.ppermute(weight, ("core", "zl"), SWAP)
-    weight = lax.all_gather(weight, LINE, axis=0, tiled=True)
-    far = prepare(True, key, value, taps)
-    arrived = lax.ppermute(far, "core", PAIR)
-    near = prepare(False, key, value, taps)
-    blocks = jnp.where(core == 0, jnp.stack([near, arrived], 1), jnp.stack([arrived, near], 1))
-    got = lax.all_to_all(blocks, LINE, 0, 0, tiled=True)
+    weight = lax.ppermute(weight, ("zh", "core"), ROWS)
+    blocks = prepare(key, value, taps)
+    blocks, weight = lax.optimization_barrier((blocks, weight))
+    weight = lax.all_gather(weight, ("zh", "zl"), axis=0, tiled=True)
+    got = lax.all_to_all(blocks.reshape(64, 2 * SLICE, BLOCK), ("x", "zh", "core", "zl"), 0, 0, tiled=True)
     got = got.reshape(16, 2, 2, 2 * SLICE, BLOCK)
+    gain, query, _ = lax.optimization_barrier((gain, query, blocks))
     gain = gain.reshape(1, BLOCK)
     other_gain = lax.ppermute(gain, "zl", PAIR)
     query_near, query_far = turn_query(query)
-    sibling = lax.ppermute(query_far, "core", PAIR)
+    sibling = cross(query_far)
     crossing = jnp.where(core == line, sibling, query_near)
     crossed = lax.ppermute(crossing, "zl", PAIR)
     conv = convolve(got, gain, other_gain)
+    weight, _ = lax.optimization_barrier((weight, conv))
+    weight = weight.reshape(4, 2, 128, BLOCK)
+    weight_1 = lax.ppermute(weight, "x", along(1))
+    weight_3 = lax.ppermute(weight, "x", along(3))
+    weight_top = lax.ppermute(weight_1[:2], "x", along(1))
+    weight_low = lax.ppermute(weight_3[2:], "x", along(3))
+    weights = (weight, weight_1, weight_top, weight_low, weight_3)
     conv = lax.all_to_all(conv, LINE, 0, 0, tiled=True)
     gated = gate(conv, query_near, sibling, crossed)
-    pieces = [gated] + [lax.ppermute(gated, "y", [(i, (i + k) % 4) for i in range(4)]) for k in (1, 2, 3)]
-    both = []
-    for piece in pieces:
-        both += [piece, lax.ppermute(piece, "core", PAIR)]
-    mixed = project(both, weight)
-    return lax.ppermute(mixed, ("core", "zl"), SWAP)
+    after = lax.ppermute(gated, "y", along(1))
+    ahead = lax.ppermute(gated, "y", along(3))
+    upper = lax.ppermute(after[:HALF], "y", along(1))
+    lower = lax.ppermute(ahead[HALF:], "y", along(3))
+    top, low, last = project([gated, after, ahead], weights)
+    mixed = []
+    for part, piece in ((top, upper), (low, lower)):
+        keep, send = finish(piece, part, last)
+        done = (keep + cross(send)).astype(jnp.bfloat16)
+        mixed.append(lax.ppermute(done, ("core", "zl"), SWAP))
+    return jnp.concatenate(mixed, 0)
 
 
 def solution(mesh):

time: 177 us -> 153 us (0.86)
  waiting for transfers between devices: 76.5 us -> 64.3 us
  Pallas kernels: 31.6 us -> 22.4 us
  local copies, waits for them, and re-layouts: 5.1 us -> 1.1 us
  starting transfers between devices: 47.1 us -> 50.3 us
    ppermute x1, waiting for transfers between devices: 21.7 us -> 10.1 us  [on_device(): crossed = lax.ppermute(crossing, 'zl', PAIR)]
    pallas_call x3 -> x4, Pallas kernels: 11.8 us -> 6.07 us  [the longest x1 2.61 us: prepare(): pl.pallas_call(prepare_kernel, out_shape=jax.ShapeDtypeStruct((16, 2, 2,...]
    unnamed x27 -> x12, local copies, waits for them, and re-layouts: 4 us -> 0.99 us
    pallas_call x1, Pallas kernels: 2.38 us -> 0.31 us  [gate(): pl.pallas_call(gate_kernel, out_shape=jax.ShapeDtypeStruct((BLOCK, BLOCK)...]
    ppermute x11 -> x14, starting transfers between devices: 27.5 us -> 29.5 us  [the longest x1 6.41 us: on_device(): weight = lax.ppermute(weight, ('zh', 'core'), ROWS)]
    ppermute x11 -> x14, waiting for transfers between devices: 25 us -> 24.7 us  [the longest x1 7.55 us: on_device(): weight_3 = lax.ppermute(weight, 'x', along(3))]
  transfers between devices with their start and end apart: 16 -> 19, of which waited for: 9 -> 11; matrix products, arithmetic and copies ran while one was open for 2% -> 0% of each run, Pallas kernels for 14% -> 15%
where the time goes in v2:
time: 153 us
  waiting for transfers between devices  64.3 us (42%)
  starting transfers between devices  50.3 us (33%)
  Pallas kernels  22.4 us (15%)
  between operations  13.6 us (9%)
    ppermute x1, waiting for transfers between devices, on_device(): other_gain = lax.ppermute(gain, 'zl', PAIR)  25.1 us
    pallas_call x1, Pallas kernels, convolve(): pl.pallas_call(convolve_kernel, out_shape=jax.ShapeDtypeStruct((BLOCKS, 2...  15.1 us
    all_to_all x1, starting transfers between devices, on_device(): lax.all_to_all(blocks.reshape(64, 2 * SLICE, BLOCK), ('x', 'zh', 'core',...  12.1 us
    ppermute x1, waiting for transfers between devices, on_device(): crossed = lax.ppermute(crossing, 'zl', PAIR)  10.1 us
    ppermute x1, waiting for transfers between devices, on_device(): weight_3 = lax.ppermute(weight, 'x', along(3))  7.55 us
    ppermute x1, starting transfers between devices, on_device(): weight = lax.ppermute(weight, ('zh', 'core'), ROWS)  6.41 us
    ppermute x1, waiting for transfers between devices, on_device(): weight_low = lax.ppermute(weight_3[2:], 'x', along(3))  6.1 us
    all_to_all x1, starting transfers between devices, on_device(): conv = lax.all_to_all(conv, LINE, 0, 0, tiled=True)  5.86 us
  transfers between devices with their start and end apart: 19, of which 11 were waited for; matrix products, arithmetic and copies ran while one was open for 0% of the time, Pallas kernels for 15%

profile of v2, /device:TPU:1, one launch (start us, length us, event | category | flops | bytes accessed | tf_op | source)
XLA Modules:
  0.0 152.7 jit_solution(3771542083507865176)
XLA Ops:
  6.5 6.4 %collective-permute-start = (bf16[128,512]{1,0:T(8,128)(2,1)}, bf16[128,512]{1,0:T(8,128)(2,1)S(1)}, u32[]{:S(2)}, u32[]{:S(2)}) collective-permute-start(bf16[128,512]{1,0:T(8,128)(2,1)} %param.16), channel_id=1, source_target_pairs={{0,0},{8,16},{16,8},{24,24},{32,32},{40,48},{48,40},{56,56},{1,1},... | collective-permute-start | bytes 393224 | tf_op jit(solution)/shard_map/ppermute | solution.py:318
  13.0 2.6 %prepare.1 = bf16[16,2,2,16,512]{4,3,2,1,0:T(8,128)(2,1)} custom-call(bf16[512,512]{1,0:T(8,128)(2,1)} %key_hbm.1, bf16[512,512]{1,0:T(8,128)(2,1)} %value_hbm.1, f32[512,512]{1,0:T(8,128)} %filter_hbm.1), custom_call_target="tpu_custom_call" | custom-call | tf_op jit(solution)/shard_map/prepare/pallas_call | solution.py:106
  15.6 0.2 collective-permute-done
  15.8 12.1 %all-to-all-start = ((bf16[64,16,512]{2,1,0:T(8,128)(2,1)}), bf16[64,16,512]{2,1,0:T(8,128)(2,1)S(1)}, u32[]{:S(2)}, u32[]{:S(2)}) async-start(bf16[64,16,512]{2,1,0:T(8,128)(2,1)} %bitcast.8), calls=%async_computation | async-start | bytes 2097152 | tf_op jit(solution)/shard_map/all_to_all | solution.py:322
  27.9 0.0 all-gather.2.cloned.1.call-start
  28.0 0.7 all-gather.2.cloned.1.call-update
  28.6 1.5 collective-permute-start.1
  30.1 25.1 %collective-permute-done.1.other_ref = f32[1,512]{1,0:T(1,128)S(1)} collective-permute-done((f32[1,512]{1,0:T(1,128)S(1)}, f32[1,512]{1,0:T(1,128)S(1)}, u32[]{:S(2)}, u32[]{:S(2)}) %collective-permute-start.1) | collective-permute-done | bytes 2080 | tf_op jit(solution)/shard_map/ppermute | solution.py:326
  55.2 3.7 %all-to-all-done = bf16[64,16,512]{2,1,0:T(8,128)(2,1)S(1)} async-done(((bf16[64,16,512]{2,1,0:T(8,128)(2,1)}), bf16[64,16,512]{2,1,0:T(8,128)(2,1)S(1)}, u32[]{:S(2)}, u32[]{:S(2)}) %all-to-all-start) | async-done | bytes 1048608 | tf_op jit(solution)/shard_map/all_to_all | solution.py:322
  58.9 1.0 copy-done.2
  59.9 15.1 %convolve.1 = bf16[32,16,512]{2,1,0:T(8,128)(2,1)} custom-call(bf16[16,2,2,16,512]{4,3,2,1,0:T(8,128)(2,1)} %bitcast.7, f32[1,512]{1,0:T(1,128)} %bitcast.9, f32[1,512]{1,0:T(1,128)} %copy-done.5, f32[2,64,256]{2,1,0:T(8,128)} %constant.18.clone.turn_ref, bf16[1024,1024]{1,0:T(8,128)(2,1)} %constant.19.clone.refs_0_, ...), custom_call_target="tpu_custom_call" | custom-call | tf_op jit(solution)/shard_map/convolve/pallas_call | solution.py:207
  75.0 5.9 %all-to-all-start.1 = ((bf16[32,16,512]{2,1,0:T(8,128)(2,1)}), bf16[32,16,512]{2,1,0:T(8,128)(2,1)S(1)}, u32[]{:S(2)}, u32[]{:S(2)}) async-start(bf16[32,16,512]{2,1,0:T(8,128)(2,1)} %convolve.1), calls=%async_computation.1 | async-start | bytes 1048576 | tf_op jit(solution)/shard_map/all_to_all | solution.py:339
  80.8 0.0 all-gather.2.cloned.1.call-done
  80.9 2.6 %collective-permute-start.9 = (bf16[4,2,128,512]{3,2,1,0:T(8,128)(2,1)}, bf16[4,2,128,512]{3,2,1,0:T(8,128)(2,1)S(1)}, u32[]{:S(2)}, u32[]{:S(2)}) collective-permute-start(bf16[4,2,128,512]{3,2,1,0:T(8,128)(2,1)} %bitcast.4), channel_id=1, source_target_pairs={{0,192},{64,0},{128,64},{192,128},{1,193},{65,1},{129,65},{193,129... | collective-permute-start | bytes 3145736 | tf_op jit(solution)/shard_map/ppermute | solution.py:335
  83.4 0.0 collective-permute-start.7
  83.4 0.9 turn_query.1
  84.3 2.1 %collective-permute-start.2 = (bf16[256,512]{1,0:T(8,128)(2,1)}, bf16[256,512]{1,0:T(8,128)(2,1)S(1)}, u32[]{:S(2)}, u32[]{:S(2)}) collective-permute-start(bf16[256,512]{1,0:T(8,128)(2,1)} %get-tuple-element.23), channel_id=1, source_target_pairs={{0,8},{8,0},{1,9},{9,1},{2,10},{10,2},{3,11},{11,3},{4,12},{12,4},... | collective-permute-start | bytes 786440 | tf_op jit(solution)/shard_map/ppermute | solution.py:313
  86.5 1.4 collective-permute-done.2.sibling_ref
  87.9 1.3 collective-permute-start.3
  89.2 10.1 %collective-permute-done.3.crossed_ref = bf16[256,512]{1,0:T(8,128)(2,1)S(1)} collective-permute-done((bf16[256,512]{1,0:T(8,128)(2,1)S(1)}, bf16[256,512]{1,0:T(8,128)(2,1)S(1)}, u32[]{:S(2)}, u32[]{:S(2)}) %collective-permute-start.3) | collective-permute-done | bytes 262176 | tf_op jit(solution)/shard_map/ppermute | solution.py:330
  99.2 0.0 all-to-all-done.1.conv_ref
  99.2 0.3 gate.1.own_ref
  99.6 1.5 collective-permute-start.4
  101.0 1.6 %collective-permute-start.6 = (bf16[512,512]{1,0:T(8,128)(2,1)S(1)}, bf16[512,512]{1,0:T(8,128)(2,1)S(1)}, u32[]{:S(2)}, u32[]{:S(2)}) collective-permute-start(bf16[512,512]{1,0:T(8,128)(2,1)S(1)} %gate.1.own_ref), channel_id=1, source_target_pairs={{0,6},{2,0},{4,2},{6,4},{1,7},{3,1},{5,3},{7,5},{8,14},{10,8},{12,... | collective-permute-start | bytes 1572872 | tf_op jit(solution)/shard_map/ppermute | solution.py:342
  102.6 7.5 %collective-permute-done.9.refs_4_ = bf16[4,2,128,512]{3,2,1,0:T(8,128)(2,1)S(1)} collective-permute-done((bf16[4,2,128,512]{3,2,1,0:T(8,128)(2,1)}, bf16[4,2,128,512]{3,2,1,0:T(8,128)(2,1)S(1)}, u32[]{:S(2)}, u32[]{:S(2)}) %collective-permute-start.9) | collective-permute-done | bytes 1048608 | tf_op jit(solution)/shard_map/ppermute | solution.py:335
  110.2 3.4 %collective-permute-start.10 = (bf16[2,2,128,512]{3,2,1,0:T(8,128)(2,1)S(1)}, bf16[2,2,128,512]{3,2,1,0:T(8,128)(2,1)S(1)}, u32[]{:S(2)}, u32[]{:S(2)}) collective-permute-start(bf16[2,2,128,512]{3,2,1,0:T(8,128)(2,1)S(1)} %slice.18), channel_id=1, source_target_pairs={{0,192},{64,0},{128,64},{192,128},{1,193},{65,1},{129,65},{193,129... | collective-permute-start | bytes 1572872 | tf_op jit(solution)/shard_map/ppermute | solution.py:337
  113.6 0.0 collective-permute-done.7.refs_1_
  113.6 0.1 collective-permute-start.8
  113.7 0.0 collective-permute-done.4.after_ref
  113.8 1.5 collective-permute-start.5
  115.3 1.6 %collective-permute-start.13 = (bf16[256,512]{1,0:T(8,128)(2,1)S(1)}, bf16[256,512]{1,0:T(8,128)(2,1)S(1)}, u32[]{:S(2)}, u32[]{:S(2)}) collective-permute-start(bf16[256,512]{1,0:T(8,128)(2,1)S(1)} %slice.19), channel_id=1, source_target_pairs={{0,6},{2,0},{4,2},{6,4},{1,7},{3,1},{5,3},{7,5},{8,14},{10,8},{12,... | collective-permute-start | bytes 786440 | tf_op jit(solution)/shard_map/ppermute | solution.py:344
  116.9 6.1 %collective-permute-done.10.refs_3_ = bf16[2,2,128,512]{3,2,1,0:T(8,128)(2,1)S(1)} collective-permute-done((bf16[2,2,128,512]{3,2,1,0:T(8,128)(2,1)S(1)}, bf16[2,2,128,512]{3,2,1,0:T(8,128)(2,1)S(1)}, u32[]{:S(2)}, u32[]{:S(2)}) %collective-permute-start.10) | collective-permute-done | bytes 524320 | tf_op jit(solution)/shard_map/ppermute | solution.py:337
  123.0 3.2 %collective-permute-done.8.refs_2_ = bf16[2,2,128,512]{3,2,1,0:T(8,128)(2,1)S(1)} collective-permute-done((bf16[2,2,128,512]{3,2,1,0:T(8,128)(2,1)S(1)}, bf16[2,2,128,512]{3,2,1,0:T(8,128)(2,1)S(1)}, u32[]{:S(2)}, u32[]{:S(2)}) %collective-permute-start.8) | collective-permute-done | bytes 524320 | tf_op jit(solution)/shard_map/ppermute | solution.py:336
  126.2 2.6 %project.1 = (f32[2,256,512]{2,1,0:T(8,128)S(1)}, f32[2,256,512]{2,1,0:T(8,128)S(1)}, bf16[2,512,512]{2,1,0:T(8,128)(2,1)S(1)}) custom-call(bf16[512,512]{1,0:T(8,128)(2,1)S(1)} %gate.1.own_ref, bf16[512,512]{1,0:T(8,128)(2,1)S(1)} %collective-permute-done.4.after_ref, bf16[512,512]{1,0:T(8,128)(2,1)S(1)} %collective-permute-done.6.ahead_ref, ...), custom_call_target="tpu_custom_call" | custom-call | flops 1610612736 | bytes 8388608 | tf_op jit(solution)/shard_map/project/pallas_call | solution.py:276
  128.8 0.4 finish.2
  129.3 3.1 %collective-permute-start.11 = (f32[256,512]{1,0:T(8,128)S(1)}, f32[256,512]{1,0:T(8,128)S(1)}, u32[]{:S(2)}, u32[]{:S(2)}) collective-permute-start(f32[256,512]{1,0:T(8,128)S(1)} %get-tuple-element.29), channel_id=1, source_target_pairs={{0,8},{8,0},{1,9},{9,1},{2,10},{10,2},{3,11},{11,3},{4,12},{12,4},... | collective-permute-start | bytes 1572872 | tf_op jit(solution)/shard_map/ppermute | solution.py:313
  132.4 0.0 collective-permute-done.13.piece_ref
  132.4 0.4 finish.3
  132.9 0.1 collective-permute-start.14
  133.0 1.0 collective-permute-done.11
  134.0 0.1 add_convert_fusion.1
  134.0 3.1 %collective-permute-start.12 = (bf16[256,512]{1,0:T(8,128)(2,1)S(1)}, bf16[256,512]{1,0:T(8,128)(2,1)S(1)}, u32[]{:S(2)}, u32[]{:S(2)}) collective-permute-start(bf16[256,512]{1,0:T(8,128)(2,1)S(1)} %add_convert_fusion.1), channel_id=1, source_target_pairs={{0,0},{1,8},{8,1},{9,9},{2,2},{3,10},{10,3},{11,11},{4,4},{5,12},{... | collective-permute-start | bytes 786440 | tf_op jit(solution)/shard_map/ppermute | solution.py:350
  137.2 0.0 collective-permute-done.14
  137.2 0.1 add_convert_fusion
  137.3 2.4 %collective-permute-start.15 = (bf16[256,512]{1,0:T(8,128)(2,1)S(1)}, bf16[256,512]{1,0:T(8,128)(2,1)S(1)}, u32[]{:S(2)}, u32[]{:S(2)}) collective-permute-start(bf16[256,512]{1,0:T(8,128)(2,1)S(1)} %add_convert_fusion), channel_id=1, source_target_pairs={{0,0},{1,8},{8,1},{9,9},{2,2},{3,10},{10,3},{11,11},{4,4},{5,12},{... | collective-permute-start | bytes 786440 | tf_op jit(solution)/shard_map/ppermute | solution.py:350
  139.7 2.0 %collective-permute-done.12 = bf16[256,512]{1,0:T(8,128)(2,1)S(1)} collective-permute-done((bf16[256,512]{1,0:T(8,128)(2,1)S(1)}, bf16[256,512]{1,0:T(8,128)(2,1)S(1)}, u32[]{:S(2)}, u32[]{:S(2)}) %collective-permute-start.12) | collective-permute-done | bytes 262176 | tf_op jit(solution)/shard_map/ppermute | solution.py:350
  141.7 3.2 %collective-permute-done.15 = bf16[256,512]{1,0:T(8,128)(2,1)S(1)} collective-permute-done((bf16[256,512]{1,0:T(8,128)(2,1)S(1)}, bf16[256,512]{1,0:T(8,128)(2,1)S(1)}, u32[]{:S(2)}, u32[]{:S(2)}) %collective-permute-start.15) | collective-permute-done | bytes 262176 | tf_op jit(solution)/shard_map/ppermute | solution.py:350
  145.0 0.8 pad_maximum_fusion
  (18 shorter events, 0.2 us)
Async XLA Ops:
  6.5 22.1 %copy-start.4 = (f32[512]{0:T(512)S(1)}, f32[512]{0:T(512)}, u32[]{:S(2)}) copy-start(f32[512]{0:T(512)} %param.15) | copy-start | bytes 6148
  6.5 9.3 %collective-permute-start = (bf16[128,512]{1,0:T(8,128)(2,1)}, bf16[128,512]{1,0:T(8,128)(2,1)S(1)}, u32[]{:S(2)}, u32[]{:S(2)}) collective-permute-start(bf16[128,512]{1,0:T(8,128)(2,1)} %param.16), channel_id=1, source_target_pairs={{0,0},{8,16},{16,8},{24,24},{32,32},{40,48},{48,40},{56,56},{1,1},... | collective-permute-start | bytes 393224 | tf_op jit(solution)/shard_map/ppermute | solution.py:318
  15.8 12.1 %copy-start.3 = (bf16[128,512]{1,0:T(8,128)(2,1)}, bf16[128,512]{1,0:T(8,128)(2,1)S(1)}, u32[]{:S(2)}) copy-start(bf16[128,512]{1,0:T(8,128)(2,1)S(1)} %collective-permute-done) | copy-start | bytes 393220
  15.8 43.1 %all-to-all-start = ((bf16[64,16,512]{2,1,0:T(8,128)(2,1)}), bf16[64,16,512]{2,1,0:T(8,128)(2,1)S(1)}, u32[]{:S(2)}, u32[]{:S(2)}) async-start(bf16[64,16,512]{2,1,0:T(8,128)(2,1)} %bitcast.8), calls=%async_computation | async-start | bytes 2097152 | tf_op jit(solution)/shard_map/all_to_all | solution.py:322
  27.9 53.0 %all-gather.2.cloned.1.call-start = ((), (), s32[]{:S(2)}) async-start(), calls=%async_computation.2 | async-start | bytes 1179648 | tf_op jit(solution)/shard_map/all_gather | solution.py:321
  28.6 26.5 %collective-permute-start.1 = (f32[1,512]{1,0:T(1,128)S(1)}, f32[1,512]{1,0:T(1,128)S(1)}, u32[]{:S(2)}, u32[]{:S(2)}) collective-permute-start(f32[1,512]{1,0:T(1,128)S(1)} %bitcast.10), channel_id=1, source_target_pairs={{0,1},{1,0},{2,3},{3,2},{4,5},{5,4},{6,7},{7,6},{8,9},{9,8},{10,11... | collective-permute-start | bytes 6152 | tf_op jit(solution)/shard_map/ppermute | solution.py:326
  55.2 3.7 %copy-start.5 = (f32[1,512]{1,0:T(1,128)}, f32[1,512]{1,0:T(1,128)S(1)}, u32[]{:S(2)}) copy-start(f32[1,512]{1,0:T(1,128)S(1)} %collective-permute-done.1.other_ref) | copy-start | bytes 6148
  58.9 1.0 copy-start.2
  59.9 23.5 %copy-start = (bf16[512,512]{1,0:T(8,128)(2,1)S(1)}, bf16[512,512]{1,0:T(8,128)(2,1)}, u32[]{:S(2)}) copy-start(bf16[512,512]{1,0:T(8,128)(2,1)} %query_ref) | copy-start | bytes 1572868
  75.0 24.3 %all-to-all-start.1 = ((bf16[32,16,512]{2,1,0:T(8,128)(2,1)}), bf16[32,16,512]{2,1,0:T(8,128)(2,1)S(1)}, u32[]{:S(2)}, u32[]{:S(2)}) async-start(bf16[32,16,512]{2,1,0:T(8,128)(2,1)} %convolve.1), calls=%async_computation.1 | async-start | bytes 1048576 | tf_op jit(solution)/shard_map/all_to_all | solution.py:339
  80.9 29.3 %collective-permute-start.9 = (bf16[4,2,128,512]{3,2,1,0:T(8,128)(2,1)}, bf16[4,2,128,512]{3,2,1,0:T(8,128)(2,1)S(1)}, u32[]{:S(2)}, u32[]{:S(2)}) collective-permute-start(bf16[4,2,128,512]{3,2,1,0:T(8,128)(2,1)} %bitcast.4), channel_id=1, source_target_pairs={{0,192},{64,0},{128,64},{192,128},{1,193},{65,1},{129,65},{193,129... | collective-permute-start | bytes 3145736 | tf_op jit(solution)/shard_map/ppermute | solution.py:335
  83.4 30.2 %collective-permute-start.7 = (bf16[4,2,128,512]{3,2,1,0:T(8,128)(2,1)}, bf16[4,2,128,512]{3,2,1,0:T(8,128)(2,1)S(1)}, u32[]{:S(2)}, u32[]{:S(2)}) collective-permute-start(bf16[4,2,128,512]{3,2,1,0:T(8,128)(2,1)} %bitcast.5), channel_id=1, source_target_pairs={{0,64},{64,128},{128,192},{192,0},{1,65},{65,129},{129,193},{193,1... | collective-permute-start | bytes 3145736 | tf_op jit(solution)/shard_map/ppermute | solution.py:334
  84.3 3.5 %collective-permute-start.2 = (bf16[256,512]{1,0:T(8,128)(2,1)}, bf16[256,512]{1,0:T(8,128)(2,1)S(1)}, u32[]{:S(2)}, u32[]{:S(2)}) collective-permute-start(bf16[256,512]{1,0:T(8,128)(2,1)} %get-tuple-element.23), channel_id=1, source_target_pairs={{0,8},{8,0},{1,9},{9,1},{2,10},{10,2},{3,11},{11,3},{4,12},{12,4},... | collective-permute-start | bytes 786440 | tf_op jit(solution)/shard_map/ppermute | solution.py:313
  87.9 11.4 %collective-permute-start.3 = (bf16[256,512]{1,0:T(8,128)(2,1)S(1)}, bf16[256,512]{1,0:T(8,128)(2,1)S(1)}, u32[]{:S(2)}, u32[]{:S(2)}) collective-permute-start(bf16[256,512]{1,0:T(8,128)(2,1)S(1)} %broadcast_select_fusion), channel_id=1, source_target_pairs={{0,1},{1,0},{2,3},{3,2},{4,5},{5,4},{6,7},{7,6},{8,9},{9,8},{10,11... | collective-permute-start | bytes 786440 | tf_op jit(solution)/shard_map/ppermute | solution.py:330
  99.2 27.0 %copy-start.1 = (bf16[1024,512]{1,0:T(8,128)(2,1)S(1)}, bf16[1024,512]{1,0:T(8,128)(2,1)}, u32[]{:S(2)}) copy-start(bf16[1024,512]{1,0:T(8,128)(2,1)} %all-gather.2.cloned.1.call-done) | copy-start | bytes 3145732
  99.6 14.2 %collective-permute-start.4 = (bf16[512,512]{1,0:T(8,128)(2,1)S(1)}, bf16[512,512]{1,0:T(8,128)(2,1)S(1)}, u32[]{:S(2)}, u32[]{:S(2)}) collective-permute-start(bf16[512,512]{1,0:T(8,128)(2,1)S(1)} %gate.1.own_ref), channel_id=1, source_target_pairs={{0,2},{2,4},{4,6},{6,0},{1,3},{3,5},{5,7},{7,1},{8,10},{10,12},{12... | collective-permute-start | bytes 1572872 | tf_op jit(solution)/shard_map/ppermute | solution.py:341
  101.0 14.2 %collective-permute-start.6 = (bf16[512,512]{1,0:T(8,128)(2,1)S(1)}, bf16[512,512]{1,0:T(8,128)(2,1)S(1)}, u32[]{:S(2)}, u32[]{:S(2)}) collective-permute-start(bf16[512,512]{1,0:T(8,128)(2,1)S(1)} %gate.1.own_ref), channel_id=1, source_target_pairs={{0,6},{2,0},{4,2},{6,4},{1,7},{3,1},{5,3},{7,5},{8,14},{10,8},{12,... | collective-permute-start | bytes 1572872 | tf_op jit(solution)/shard_map/ppermute | solution.py:342
  110.2 12.8 %collective-permute-start.10 = (bf16[2,2,128,512]{3,2,1,0:T(8,128)(2,1)S(1)}, bf16[2,2,128,512]{3,2,1,0:T(8,128)(2,1)S(1)}, u32[]{:S(2)}, u32[]{:S(2)}) collective-permute-start(bf16[2,2,128,512]{3,2,1,0:T(8,128)(2,1)S(1)} %slice.18), channel_id=1, source_target_pairs={{0,192},{64,0},{128,64},{192,128},{1,193},{65,1},{129,65},{193,129... | collective-permute-start | bytes 1572872 | tf_op jit(solution)/shard_map/ppermute | solution.py:337
  113.6 12.6 %collective-permute-start.8 = (bf16[2,2,128,512]{3,2,1,0:T(8,128)(2,1)S(1)}, bf16[2,2,128,512]{3,2,1,0:T(8,128)(2,1)S(1)}, u32[]{:S(2)}, u32[]{:S(2)}) collective-permute-start(bf16[2,2,128,512]{3,2,1,0:T(8,128)(2,1)S(1)} %slice.17), channel_id=1, source_target_pairs={{0,64},{64,128},{128,192},{192,0},{1,65},{65,129},{129,193},{193,1... | collective-permute-start | bytes 1572872 | tf_op jit(solution)/shard_map/ppermute | solution.py:336
  113.8 15.0 %collective-permute-start.5 = (bf16[256,512]{1,0:T(8,128)(2,1)S(1)}, bf16[256,512]{1,0:T(8,128)(2,1)S(1)}, u32[]{:S(2)}, u32[]{:S(2)}) collective-permute-start(bf16[256,512]{1,0:T(8,128)(2,1)S(1)} %slice.16), channel_id=1, source_target_pairs={{0,2},{2,4},{4,6},{6,0},{1,3},{3,5},{5,7},{7,1},{8,10},{10,12},{12... | collective-permute-start | bytes 786440 | tf_op jit(solution)/shard_map/ppermute | solution.py:343
  115.3 17.1 %collective-permute-start.13 = (bf16[256,512]{1,0:T(8,128)(2,1)S(1)}, bf16[256,512]{1,0:T(8,128)(2,1)S(1)}, u32[]{:S(2)}, u32[]{:S(2)}) collective-permute-start(bf16[256,512]{1,0:T(8,128)(2,1)S(1)} %slice.19), channel_id=1, source_target_pairs={{0,6},{2,0},{4,2},{6,4},{1,7},{3,1},{5,3},{7,5},{8,14},{10,8},{12,... | collective-permute-start | bytes 786440 | tf_op jit(solution)/shard_map/ppermute | solution.py:344
  129.3 4.7 %collective-permute-start.11 = (f32[256,512]{1,0:T(8,128)S(1)}, f32[256,512]{1,0:T(8,128)S(1)}, u32[]{:S(2)}, u32[]{:S(2)}) collective-permute-start(f32[256,512]{1,0:T(8,128)S(1)} %get-tuple-element.29), channel_id=1, source_target_pairs={{0,8},{8,0},{1,9},{9,1},{2,10},{10,2},{3,11},{11,3},{4,12},{12,4},... | collective-permute-start | bytes 1572872 | tf_op jit(solution)/shard_map/ppermute | solution.py:313
  132.9 4.3 %collective-permute-start.14 = (f32[256,512]{1,0:T(8,128)S(1)}, f32[256,512]{1,0:T(8,128)S(1)}, u32[]{:S(2)}, u32[]{:S(2)}) collective-permute-start(f32[256,512]{1,0:T(8,128)S(1)} %get-tuple-element.32), channel_id=1, source_target_pairs={{0,8},{8,0},{1,9},{9,1},{2,10},{10,2},{3,11},{11,3},{4,12},{12,4},... | collective-permute-start | bytes 1572872 | tf_op jit(solution)/shard_map/ppermute | solution.py:313
  134.0 7.7 %collective-permute-start.12 = (bf16[256,512]{1,0:T(8,128)(2,1)S(1)}, bf16[256,512]{1,0:T(8,128)(2,1)S(1)}, u32[]{:S(2)}, u32[]{:S(2)}) collective-permute-start(bf16[256,512]{1,0:T(8,128)(2,1)S(1)} %add_convert_fusion.1), channel_id=1, source_target_pairs={{0,0},{1,8},{8,1},{9,9},{2,2},{3,10},{10,3},{11,11},{4,4},{5,12},{... | collective-permute-start | bytes 786440 | tf_op jit(solution)/shard_map/ppermute | solution.py:350
  137.3 7.7 %collective-permute-start.15 = (bf16[256,512]{1,0:T(8,128)(2,1)S(1)}, bf16[256,512]{1,0:T(8,128)(2,1)S(1)}, u32[]{:S(2)}, u32[]{:S(2)}) collective-permute-start(bf16[256,512]{1,0:T(8,128)(2,1)S(1)} %add_convert_fusion), channel_id=1, source_target_pairs={{0,0},{1,8},{8,1},{9,9},{2,2},{3,10},{10,3},{11,11},{4,4},{5,12},{... | collective-permute-start | bytes 786440 | tf_op jit(solution)/shard_map/ppermute | solution.py:350
Sparse Core Ops, SparseCore 0:
  30.5 40.5 all-gather.1

commit v3 on v2

v3 whole, which is shorter than its diff:
```python
import functools
import math

import jax
import jax.numpy as jnp
import numpy as np
from jax import lax
from jax.experimental import pallas as pl
from jax.experimental.pallas import tpu as pltpu
from jax.sharding import Mesh
from jax.sharding import PartitionSpec as P

AXES = ("x", "zh", "core", "y", "zl")
TOKENS = ("x", "zh", "core")
BLOCKS = 32
BLOCK = 512
CHANNELS = 16
SLICE = 8
HALF = 256
STEPS = 64
INNER = 256
PERIOD = 32768
PAIR = [(0, 1), (1, 0)]


def halves(table):
    high = table.astype(np.float32).astype(jnp.bfloat16)
    low = (table - high.astype(np.float64)).astype(np.float32).astype(jnp.bfloat16)
    return high, low


def tables():
    odd = np.arange(STEPS) + 0.5
    steps = np.arange(STEPS)
    inner = np.arange(INNER)
    outer = 2 * math.pi * np.outer(odd, steps) / (2 * STEPS)
    same = np.eye(SLICE)
    order = steps.reshape(BLOCKS, 2).T.reshape(-1)
    cos_o, sin_o = np.cos(outer)[:, order], np.sin(outer)[:, order]
    first = np.concatenate([np.kron(cos_o, same), np.kron(-sin_o, same)], 0)
    last = np.concatenate([np.kron(cos_o.T, same), np.kron(-sin_o.T, same)], 1) / (PERIOD // 2)
    turn = 2 * math.pi * np.outer(odd, inner) / PERIOD
    turn = np.stack([np.cos(turn), np.sin(turn)]).astype(np.float32)
    angle = 2 * math.pi * (np.outer(inner, inner) % INNER) / INNER
    cos_i, sin_i = np.cos(angle), np.sin(angle)
    ahead = np.block([[cos_i, -sin_i], [sin_i, cos_i]])
    back = np.block([[cos_i, sin_i], [-sin_i, cos_i]])
    first_high, first_low = halves(first)
    last_high, last_low = halves(last)
    ahead_high, ahead_low = halves(ahead)
    back_high, back_low = halves(back)
    return (
        np.concatenate([first_high, first_low], 1),
        turn,
        np.concatenate([ahead_high, ahead_low], 0),
        np.concatenate([back_high, back_low], 0),
        np.concatenate([last_high, last_low], 1),
    )


def dot(left, right):
    return jnp.dot(left, right, preferred_element_type=jnp.float32)


def split(value):
    high = value.astype(jnp.bfloat16)
    return high, (value - high.astype(jnp.float32)).astype(jnp.bfloat16)


def params(mebibytes):
    return pltpu.CompilerParams(vmem_limit_bytes=mebibytes * 1024 * 1024)


def whole():
    return pl.BlockSpec(memory_space=pltpu.VMEM)


def anywhere():
    return pl.BlockSpec(memory_space=pl.ANY)


def prepare_kernel(key_hbm, value_hbm, filter_hbm, out_hbm, key_ref, value_ref, filter_ref, out_ref, sems, out_sems):
    moves = []
    for i in range(4):
        columns = pl.ds(i * 128, 128)
        for j, (far, near) in enumerate(((key_hbm, key_ref), (value_hbm, value_ref), (filter_hbm, filter_ref))):
            moves.append(pltpu.make_async_copy(far.at[:, columns], near.at[i], sems.at[i, j]))
            moves[-1].start()
    outs = []
    for i in range(4):
        for move in moves[3 * i : 3 * i + 3]:
            move.wait()
        source = key_ref[i].astype(jnp.float32) * value_ref[i].astype(jnp.float32)
        source = source.T.reshape(8, CHANNELS, BLOCK)
        taps = filter_ref[i].T.reshape(8, CHANNELS, BLOCK)
        out_ref[i] = jnp.concatenate([source, taps], 1).astype(jnp.bfloat16)
        outs.append(pltpu.make_async_copy(out_ref.at[i], out_hbm.at[pl.ds(i * 8, 8)], out_sems.at[i]))
        outs[-1].start()
    for out in outs:
        out.wait()


def prepare(key, value, taps):
    return pl.pallas_call(
        prepare_kernel,
        out_shape=jax.ShapeDtypeStruct((BLOCKS, 2 * CHANNELS, BLOCK), jnp.bfloat16),
        in_specs=[anywhere()] * 3,
        out_specs=anywhere(),
        scratch_shapes=[
            pltpu.VMEM((4, BLOCK, 128), jnp.bfloat16),
            pltpu.VMEM((4, BLOCK, 128), jnp.bfloat16),
            pltpu.VMEM((4, BLOCK, 128), jnp.float32),
            pltpu.VMEM((4, 8, 2 * CHANNELS, BLOCK), jnp.bfloat16),
            pltpu.SemaphoreType.DMA((4, 3)),
            pltpu.SemaphoreType.DMA((4,)),
        ],
        compiler_params=params(56),
        name="prepare",
    )(key, value, taps)


def thrice(table_ref):
    return jnp.concatenate([table_ref[:BLOCK], table_ref[...]], 0)


def convolve_kernel(got_ref, gain_ref, turn_ref, *refs):
    out_ref, tables_here, sems = refs[4], refs[5:9], refs[9]
    copies = []
    for i in range(4):
        part = refs[i].shape[0] // 4
        for j in range(4):
            rows = pl.ds(j * part, part)
            copies.append(pltpu.make_async_copy(refs[i].at[rows], tables_here[i].at[rows], sems.at[i, j]))
            copies[-1].start()

    def arrived(i):
        for copy in copies[4 * i : 4 * i + 4]:
            copy.wait()

    first_ref, ahead_ref, back_ref, last_ref = tables_here
    place = lax.axis_index("x") * 8 + lax.axis_index("zh") * 2 + lax.axis_index("core")
    cos_t = turn_ref[0][:, None, :]
    sin_t = turn_ref[1][:, None, :]
    rows = STEPS * SLICE

    def turned(real, imag, sign):
        real = real.reshape(STEPS, SLICE, INNER)
        imag = imag.reshape(STEPS, SLICE, INNER)
        one = real * cos_t - (sign * imag) * sin_t
        two = imag * cos_t + (sign * real) * sin_t
        return one.reshape(rows, INNER), two.reshape(rows, INNER)

    outs = []
    for s in range(2):
        got = got_ref[...].astype(jnp.float32).reshape(BLOCKS, 2, 2, SLICE, BLOCK)
        source = got[:, 0, s].reshape(BLOCKS * SLICE, BLOCK)
        taps = got[:, 1, s].reshape(BLOCKS * SLICE, BLOCK)
        both = jnp.concatenate(
            [
                jnp.concatenate([source[:, :INNER], taps[:, :INNER]], 1),
                jnp.concatenate([source[:, INNER:], taps[:, INNER:]], 1),
            ],
            0,
        ).astype(jnp.bfloat16)
        if s == 0:
            arrived(0)
        first = dot(first_ref[...], jnp.concatenate([both, both], 0))
        if s == 0:
            arrived(1)
        spectra = []
        for part in range(2):
            columns = slice(part * INNER, (part + 1) * INNER)
            real, imag = turned(first[:rows, columns], first[rows:, columns], -1.0)
            high, low = split(jnp.concatenate([real, imag], 1))
            spectra.append(dot(jnp.concatenate([high, low, high], 1), thrice(ahead_ref)))
        (ar, ai), (br, bi) = [(z[:, :INNER], z[:, INNER:]) for z in spectra]
        product = jnp.concatenate([ar * br - ai * bi, ar * bi + ai * br], 1)
        high, low = split(product)
        if s == 0:
            arrived(2)
        inner = dot(jnp.concatenate([high, low, high], 1), thrice(back_ref))
        real, imag = turned(inner[:, :INNER], inner[:, INNER:], 1.0)
        high, low = split(jnp.concatenate([real, imag], 0))
        if s == 0:
            arrived(3)
        conv = dot(jnp.concatenate([last_ref[:, :1024], last_ref[...]], 1), jnp.concatenate([high, low, high], 0))
        conv = jnp.concatenate([conv[: BLOCKS * SLICE], conv[BLOCKS * SLICE :]], 1)
        channel = place * CHANNELS + s * SLICE + lax.broadcasted_iota(jnp.int32, (SLICE, BLOCK), 0)
        picked = channel == lax.broadcasted_iota(jnp.int32, (SLICE, BLOCK), 1)
        gain = jnp.sum(jnp.where(picked, gain_ref[...], 0.0), 1, keepdims=True)
        total = conv.reshape(BLOCKS, SLICE, BLOCK) + gain[None] * source.reshape(BLOCKS, SLICE, BLOCK)
        outs.append(total)
    out_ref[...] = jnp.concatenate(outs, 1).astype(jnp.bfloat16)


def convolve(got, gain):
    first, turn, ahead, back, last = tables()
    return pl.pallas_call(
        convolve_kernel,
        out_shape=jax.ShapeDtypeStruct((BLOCKS, CHANNELS, BLOCK), jnp.bfloat16),
        in_specs=[whole()] * 3 + [anywhere()] * 4,
        out_specs=whole(),
        scratch_shapes=[pltpu.VMEM(table.shape, jnp.bfloat16) for table in (first, ahead, back, last)]
        + [pltpu.SemaphoreType.DMA((4, 4))],
        compiler_params=params(56),
        name="convolve",
    )(got, gain, turn, first, ahead, back, last)


def gate_kernel(conv_ref, query_ref, out_ref, top_ref, low_ref):
    conv = conv_ref[...].astype(jnp.float32).reshape(BLOCK, BLOCK).T
    gated = (query_ref[...].astype(jnp.float32) * conv).astype(jnp.bfloat16)
    out_ref[...] = gated
    top_ref[...] = gated[:HALF]
    low_ref[...] = gated[HALF:]


def gate(conv, query):
    half = jax.ShapeDtypeStruct((HALF, BLOCK), jnp.bfloat16)
    return pl.pallas_call(
        gate_kernel,
        out_shape=[jax.ShapeDtypeStruct((BLOCK, BLOCK), jnp.bfloat16), half, half],
        in_specs=[whole()] * 2,
        out_specs=[whole()] * 3,
        compiler_params=params(16),
        name="gate",
    )(conv, query)


def order_kernel(own_ref, sibling_ref, *refs):
    outs, sems = refs[:4], refs[4]
    core, x, y, zh = (lax.axis_index(axis) for axis in ("core", "x", "y", "zh"))
    moves = []
    for back, out in enumerate(outs):
        away = lax.rem(x - y + back + 4, 4)
        for k in range(4):
            place = 2 * lax.rem(zh + 4 - k, 4)
            moves.append(pltpu.make_async_copy(own_ref.at[away, k], out.at[place + core], sems.at[back, k, 0]))
            moves.append(pltpu.make_async_copy(sibling_ref.at[away, k], out.at[place + 1 - core], sems.at[back, k, 1]))
    for move in moves:
        move.start()
    for move in moves:
        move.wait()


def order(own, sibling):
    return pl.pallas_call(
        order_kernel,
        out_shape=[jax.ShapeDtypeStruct((8, 128, BLOCK), jnp.bfloat16)] * 4,
        in_specs=[anywhere()] * 2,
        out_specs=[anywhere()] * 4,
        scratch_shapes=[pltpu.SemaphoreType.DMA((4, 4, 2))],
        compiler_params=params(16),
        name="order",
    )(own, sibling)


def rows_of(weight_ref, column):
    start = pl.multiple_of(column * 4, 4)
    return weight_ref[pl.ds(start, 4)].reshape(BLOCK, BLOCK)


def project_kernel(sides, begins, *refs):
    count = len(sides)
    weights, pieces = refs[:count], refs[count:-1]
    line = lax.axis_index("zl")
    totals = [None, None] if begins else [refs[-2][:HALF], refs[-2][HALF:]]
    for side, weight in zip(sides, weights):
        if pieces[0].shape[0] == BLOCK:
            parts, pieces = [pieces[0][:HALF], pieces[0][HALF:]], pieces[1:]
        else:
            parts, pieces = [pieces[0][...], pieces[1][...]], pieces[2:]
        rows = rows_of(weight, 1 - line if side else line)
        for half in range(2):
            term = dot(parts[half], rows)
            totals[half] = term if totals[half] is None else totals[half] + term
    refs[-1][:HALF] = totals[0]
    refs[-1][HALF:] = totals[1]


def project(sides, pieces, weights, before=None):
    count = len(weights)
    operands = list(weights) + list(pieces) + ([] if before is None else [before])
    return pl.pallas_call(
        functools.partial(project_kernel, sides, before is None),
        out_shape=jax.ShapeDtypeStruct((BLOCK, BLOCK), jnp.float32),
        in_specs=[whole()] * len(operands),
        out_specs=whole(),
        compiler_params=params(16),
        cost_estimate=pl.CostEstimate(
            flops=2 * count * BLOCK**3, bytes_accessed=(count + 2) * 2**20, transcendentals=0
        ),
        name="project",
    )(*operands)


def finish_kernel(upper_ref, lower_ref, upper_far_ref, lower_far_ref, weight_ref, before_ref, out_ref):
    line = lax.axis_index("zl")
    near, far = rows_of(weight_ref, line), rows_of(weight_ref, 1 - line)
    for start, piece, piece_far in ((0, upper_ref, upper_far_ref), (HALF, lower_ref, lower_far_ref)):
        rows = slice(start, start + HALF)
        total = before_ref[rows] + dot(piece[...], near) + dot(piece_far[...], far)
        out_ref[rows] = total.astype(jnp.bfloat16)


def finish(upper, lower, upper_far, lower_far, weight, before):
    return pl.pallas_call(
        finish_kernel,
        out_shape=jax.ShapeDtypeStruct((BLOCK, BLOCK), jnp.bfloat16),
        in_specs=[whole()] * 6,
        out_specs=whole(),
        compiler_params=params(16),
        name="finish",
    )(upper, lower, upper_far, lower_far, weight, before)


def along(steps):
    return [(i, (i + steps) % 4) for i in range(4)]


def on_device(query, key, value, taps, gain, weight):
    blocks = prepare(key, value, taps)
    got = lax.all_to_all(blocks, TOKENS, 0, 0, tiled=True)
    weight, _ = lax.optimization_barrier((weight, blocks))
    weight = [weight] + [lax.ppermute(weight, "zh", along(k)) for k in (1, 2, 3)]
    conv = convolve(got, gain.reshape(1, BLOCK))
    conv, *weight = lax.optimization_barrier((conv, *weight))
    weight = jnp.stack(weight)
    weight = [weight] + [lax.ppermute(weight, "x", along(k)) for k in (1, 2, 3)]
    conv = lax.all_to_all(conv, TOKENS, 0, 0, tiled=True)
    gated, top, low = gate(conv, query)
    far_top = lax.ppermute(top, "zl", PAIR)
    after = lax.ppermute(gated, "y", along(1))
    ahead = lax.ppermute(gated, "y", along(3))
    far_low = lax.ppermute(low, "zl", PAIR)
    *weight, _, _, _ = lax.optimization_barrier((*weight, after, ahead, far_low))
    weight = jnp.stack(weight)
    weights = order(weight, lax.ppermute(weight, "core", PAIR))
    after_far = [lax.ppermute(part, "y", along(1)) for part in (far_top, far_low)]
    ahead_far = [lax.ppermute(part, "y", along(3)) for part in (far_top, far_low)]
    upper = lax.ppermute(after[:HALF], "y", along(1))
    lower = lax.ppermute(ahead[HALF:], "y", along(3))
    upper_far = lax.ppermute(after_far[0], "y", along(1))
    lower_far = lax.ppermute(ahead_far[1], "y", along(3))
    total = project(
        (0, 0, 0, 1), [gated, after, ahead, far_top, far_low], [weights[0], weights[1], weights[3], weights[0]]
    )
    total = project((1, 1), after_far + ahead_far, [weights[1], weights[3]], total)
    return finish(upper, lower, upper_far, lower_far, weights[2], total)


def solution(mesh):
    fine = Mesh(mesh.devices.reshape(4, 4, 2, 4, 2), AXES)
    columns = ("y", "zl")
    placed = P(TOKENS, columns)
    return jax.shard_map(
        on_device,
        mesh=fine,
        in_specs=(placed, placed, placed, placed, P(columns), placed),
        out_specs=placed,
        check_vma=False,
    )
```

time: 153 us -> 138 us (0.902); the launches traced: 153 us -> 136 us
  between operations: 13.6 us -> 0.2 us
  waiting for transfers between devices: 64.3 us -> 55.8 us
  Pallas kernels: 22.4 us -> 27.1 us
    ppermute x12 -> x15, waiting for transfers between devices: 59.9 us -> 21.4 us  [the longest x3 9.19 us: on_device(): weight = [weight] + [lax.ppermute(weight, 'x', along(k)) for k in (1, 2, 3)]]
    all_to_all x2, waiting for transfers between devices: 3.73 us -> 34.4 us  [the longest x1 23.1 us: on_device(): got = lax.all_to_all(blocks, TOKENS, 0, 0, tiled=True)]
    pallas_call x7, Pallas kernels: 22.4 us -> 27.1 us  [the longest x1 15 us: convolve(): pl.pallas_call(convolve_kernel, out_shape=jax.ShapeDtypeStruct((BLOCKS, C...]
    ppermute x12 -> x15, starting transfers between devices: 26.1 us -> 28.2 us  [the longest x3 8.95 us: on_device(): lax.ppermute(weight, 'zh', along(k))]
  transfers between devices with their start and end apart: 19 -> 21, of which waited for: 11 -> 8; matrix products, arithmetic and copies ran while one was open for 0% -> 0% of each run, Pallas kernels for 15% -> 17%
where the time goes in v3:
time: 138 us; the launch traced here: 136 us
  waiting for transfers between devices  55.8 us (40%)
  starting transfers between devices  51.4 us (37%)
  Pallas kernels  27.1 us (20%)
    all_to_all x1, waiting for transfers between devices, on_device(): got = lax.all_to_all(blocks, TOKENS, 0, 0, tiled=True)  23.1 us
    pallas_call x1, Pallas kernels, convolve(): pl.pallas_call(convolve_kernel, out_shape=jax.ShapeDtypeStruct((BLOCKS, C...  15 us
    all_to_all x1, starting transfers between devices, on_device(): got = lax.all_to_all(blocks, TOKENS, 0, 0, tiled=True)  12.6 us
    all_to_all x1, waiting for transfers between devices, on_device(): conv = lax.all_to_all(conv, TOKENS, 0, 0, tiled=True)  11.3 us
    ppermute x3, waiting for transfers between devices, on_device(): weight = [weight] + [lax.ppermute(weight, 'x', along(k)) for k in (1, 2, 3)]  9.19 us
    ppermute x3, starting transfers between devices, on_device(): lax.ppermute(weight, 'zh', along(k))  8.95 us
    all_to_all x1, starting transfers between devices, on_device(): conv = lax.all_to_all(conv, TOKENS, 0, 0, tiled=True)  6.63 us
    ppermute x2, waiting for transfers between devices, on_device(): lax.ppermute(part, 'y', along(1))  6.37 us
  transfers between devices with their start and end apart: 21, of which 8 were waited for; matrix products, arithmetic and copies ran while one was open for 0% of the time, Pallas kernels for 17%

profile of v3, /device:TPU:1, one launch (start us, length us, event | category | flops | bytes accessed | tf_op | source)
XLA Modules:
  0.0 135.9 jit_solution(2972712525119245985)
XLA Ops:
  0.0 2.6 %prepare.1 = bf16[32,32,512]{2,1,0:T(8,128)(2,1)} custom-call(bf16[512,512]{1,0:T(8,128)(2,1)} %key_hbm.1, bf16[512,512]{1,0:T(8,128)(2,1)} %value_hbm.1, f32[512,512]{1,0:T(8,128)} %filter_hbm.1), custom_call_target="tpu_custom_call" | custom-call | tf_op jit(solution)/shard_map/prepare/pallas_call | solution.py:104
  2.6 12.6 %all-to-all-start = ((bf16[32,32,512]{2,1,0:T(8,128)(2,1)}), bf16[32,32,512]{2,1,0:T(8,128)(2,1)S(1)}, u32[]{:S(2)}, u32[]{:S(2)}) async-start(bf16[32,32,512]{2,1,0:T(8,128)(2,1)} %prepare.1), calls=%async_computation | async-start | bytes 2097152 | tf_op jit(solution)/shard_map/all_to_all | solution.py:323
  15.2 2.4 %collective-permute-start = (bf16[128,512]{1,0:T(8,128)(2,1)S(1)}, bf16[128,512]{1,0:T(8,128)(2,1)S(1)}, u32[]{:S(2)}, u32[]{:S(2)}) collective-permute-start(bf16[128,512]{1,0:T(8,128)(2,1)S(1)} %copy-done.2), channel_id=1, source_target_pairs={{0,16},{16,32},{32,48},{48,0},{1,17},{17,33},{33,49},{49,1},{2,18}... | collective-permute-start | bytes 393224 | tf_op jit(solution)/shard_map/ppermute | solution.py:325
  17.6 3.3 %collective-permute-start.1 = (bf16[128,512]{1,0:T(8,128)(2,1)S(1)}, bf16[128,512]{1,0:T(8,128)(2,1)S(1)}, u32[]{:S(2)}, u32[]{:S(2)}) collective-permute-start(bf16[128,512]{1,0:T(8,128)(2,1)S(1)} %copy-done.2), channel_id=1, source_target_pairs={{0,32},{16,48},{32,0},{48,16},{1,33},{17,49},{33,1},{49,17},{2,34}... | collective-permute-start | bytes 393224 | tf_op jit(solution)/shard_map/ppermute | solution.py:325
  20.9 3.3 %collective-permute-start.2 = (bf16[128,512]{1,0:T(8,128)(2,1)S(1)}, bf16[128,512]{1,0:T(8,128)(2,1)S(1)}, u32[]{:S(2)}, u32[]{:S(2)}) collective-permute-start(bf16[128,512]{1,0:T(8,128)(2,1)S(1)} %copy-done.2), channel_id=1, source_target_pairs={{0,48},{16,0},{32,16},{48,32},{1,49},{17,1},{33,17},{49,33},{2,50}... | collective-permute-start | bytes 393224 | tf_op jit(solution)/shard_map/ppermute | solution.py:325
  24.2 23.1 %all-to-all-done.got_ref = bf16[32,32,512]{2,1,0:T(8,128)(2,1)S(1)} async-done(((bf16[32,32,512]{2,1,0:T(8,128)(2,1)}), bf16[32,32,512]{2,1,0:T(8,128)(2,1)S(1)}, u32[]{:S(2)}, u32[]{:S(2)}) %all-to-all-start) | async-done | bytes 1048608 | tf_op jit(solution)/shard_map/all_to_all | solution.py:323
  47.3 1.0 copy-done.1
  48.3 15.0 %convolve.1 = bf16[32,16,512]{2,1,0:T(8,128)(2,1)} custom-call(bf16[32,32,512]{2,1,0:T(8,128)(2,1)} %copy-done.1, f32[1,512]{1,0:T(1,128)} %bitcast.17, f32[2,64,256]{2,1,0:T(8,128)} %constant.10.clone.turn_ref, bf16[1024,1024]{1,0:T(8,128)(2,1)} %constant.11.clone.refs_0_, bf16[1024,512]{1,0:T(8,128)(2,1)} %constant.12.clone.refs_1_, ...), custom_call_target="tpu_custom_call" | custom-call | tf_op jit(solution)/shard_map/convolve/pallas_call | solution.py:198
  63.3 0.0 copy-start
  63.4 0.0 collective-permute-done.2
  63.4 6.6 %all-to-all-start.1 = ((bf16[32,16,512]{2,1,0:T(8,128)(2,1)}), bf16[32,16,512]{2,1,0:T(8,128)(2,1)S(1)}, u32[]{:S(2)}, u32[]{:S(2)}) async-start(bf16[32,16,512]{2,1,0:T(8,128)(2,1)} %convolve.1), calls=%async_computation.1 | async-start | bytes 1048576 | tf_op jit(solution)/shard_map/all_to_all | solution.py:330
  70.0 0.1 pad_maximum_fusion.1
  70.1 1.6 %collective-permute-start.13 = (bf16[4,128,512]{2,1,0:T(8,128)(2,1)S(1)}, bf16[4,128,512]{2,1,0:T(8,128)(2,1)S(1)}, u32[]{:S(2)}, u32[]{:S(2)}) collective-permute-start(bf16[4,128,512]{2,1,0:T(8,128)(2,1)S(1)} %pad_maximum_fusion.1), channel_id=1, source_target_pairs={{0,64},{64,128},{128,192},{192,0},{1,65},{65,129},{129,193},{193,1... | collective-permute-start | bytes 1572872 | tf_op jit(solution)/shard_map/ppermute | solution.py:329
  71.7 2.4 %collective-permute-start.14 = (bf16[4,128,512]{2,1,0:T(8,128)(2,1)S(1)}, bf16[4,128,512]{2,1,0:T(8,128)(2,1)S(1)}, u32[]{:S(2)}, u32[]{:S(2)}) collective-permute-start(bf16[4,128,512]{2,1,0:T(8,128)(2,1)S(1)} %pad_maximum_fusion.1), channel_id=1, source_target_pairs={{0,128},{64,192},{128,0},{192,64},{1,129},{65,193},{129,1},{193,65... | collective-permute-start | bytes 1572872 | tf_op jit(solution)/shard_map/ppermute | solution.py:329
  74.2 1.1 collective-permute-start.15
  75.3 11.3 %all-to-all-done.1.conv_ref = bf16[32,16,512]{2,1,0:T(8,128)(2,1)S(1)} async-done(((bf16[32,16,512]{2,1,0:T(8,128)(2,1)}), bf16[32,16,512]{2,1,0:T(8,128)(2,1)S(1)}, u32[]{:S(2)}, u32[]{:S(2)}) %all-to-all-start.1) | async-done | bytes 524320 | tf_op jit(solution)/shard_map/all_to_all | solution.py:330
  86.7 0.2 gate.1
  86.9 1.4 %collective-permute-start.3 = (bf16[512,512]{1,0:T(8,128)(2,1)S(1)}, bf16[512,512]{1,0:T(8,128)(2,1)S(1)}, u32[]{:S(2)}, u32[]{:S(2)}) collective-permute-start(bf16[512,512]{1,0:T(8,128)(2,1)S(1)} %get-tuple-element.24.refs_4_), channel_id=1, source_target_pairs={{0,2},{2,4},{4,6},{6,0},{1,3},{3,5},{5,7},{7,1},{8,10},{10,12},{12... | collective-permute-start | bytes 1572872 | tf_op jit(solution)/shard_map/ppermute | solution.py:333
  88.3 1.5 %collective-permute-start.5 = (bf16[512,512]{1,0:T(8,128)(2,1)S(1)}, bf16[512,512]{1,0:T(8,128)(2,1)S(1)}, u32[]{:S(2)}, u32[]{:S(2)}) collective-permute-start(bf16[512,512]{1,0:T(8,128)(2,1)S(1)} %get-tuple-element.24.refs_4_), channel_id=1, source_target_pairs={{0,6},{2,0},{4,2},{6,4},{1,7},{3,1},{5,3},{7,5},{8,14},{10,8},{12,... | collective-permute-start | bytes 1572872 | tf_op jit(solution)/shard_map/ppermute | solution.py:334
  89.8 0.6 collective-permute-done.13
  90.4 2.8 %collective-permute-start.10 = (bf16[256,512]{1,0:T(8,128)(2,1)S(1)}, bf16[256,512]{1,0:T(8,128)(2,1)S(1)}, u32[]{:S(2)}, u32[]{:S(2)}) collective-permute-start(bf16[256,512]{1,0:T(8,128)(2,1)S(1)} %get-tuple-element.26), channel_id=1, source_target_pairs={{0,1},{1,0},{2,3},{3,2},{4,5},{5,4},{6,7},{7,6},{8,9},{9,8},{10,11... | collective-permute-start | bytes 786440 | tf_op jit(solution)/shard_map/ppermute | solution.py:335
  93.2 8.6 %collective-permute-done.14 = bf16[4,128,512]{2,1,0:T(8,128)(2,1)S(1)} collective-permute-done((bf16[4,128,512]{2,1,0:T(8,128)(2,1)S(1)}, bf16[4,128,512]{2,1,0:T(8,128)(2,1)S(1)}, u32[]{:S(2)}, u32[]{:S(2)}) %collective-permute-start.14) | collective-permute-done | bytes 524320 | tf_op jit(solution)/shard_map/ppermute | solution.py:329
  101.8 0.0 collective-permute-done.15
  101.8 0.0 collective-permute-done.10.refs_8_
  101.8 0.0 collective-permute-done.3.refs_5_
  101.8 0.0 collective-permute-done.5.refs_6_
  101.8 0.3 pad_maximum_fusion.own_ref
  102.1 1.0 collective-permute-start.16
  103.1 3.2 %collective-permute-start.7 = (bf16[256,512]{1,0:T(8,128)(2,1)S(1)}, bf16[256,512]{1,0:T(8,128)(2,1)S(1)}, u32[]{:S(2)}, u32[]{:S(2)}) collective-permute-start(bf16[256,512]{1,0:T(8,128)(2,1)S(1)} %get-tuple-element.25), channel_id=1, source_target_pairs={{0,1},{1,0},{2,3},{3,2},{4,5},{5,4},{6,7},{7,6},{8,9},{9,8},{10,11... | collective-permute-start | bytes 786440 | tf_op jit(solution)/shard_map/ppermute | solution.py:332
  106.4 2.7 %collective-permute-start.11 = (bf16[256,512]{1,0:T(8,128)(2,1)S(1)}, bf16[256,512]{1,0:T(8,128)(2,1)S(1)}, u32[]{:S(2)}, u32[]{:S(2)}) collective-permute-start(bf16[256,512]{1,0:T(8,128)(2,1)S(1)} %collective-permute-done.10.refs_8_), channel_id=1, source_target_pairs={{0,6},{2,0},{4,2},{6,4},{1,7},{3,1},{5,3},{7,5},{8,14},{10,8},{12,... | collective-permute-start | bytes 786440 | tf_op jit(solution)/shard_map/ppermute | solution.py:340
  109.1 0.0 collective-permute-start.17
  109.1 3.8 %collective-permute-done.7.refs_7_ = bf16[256,512]{1,0:T(8,128)(2,1)S(1)} collective-permute-done((bf16[256,512]{1,0:T(8,128)(2,1)S(1)}, bf16[256,512]{1,0:T(8,128)(2,1)S(1)}, u32[]{:S(2)}, u32[]{:S(2)}) %collective-permute-start.7) | collective-permute-done | bytes 262176 | tf_op jit(solution)/shard_map/ppermute | solution.py:332
  112.9 1.3 collective-permute-start.8
  114.2 1.4 %collective-permute-start.18 = (bf16[256,512]{1,0:T(8,128)(2,1)S(1)}, bf16[256,512]{1,0:T(8,128)(2,1)S(1)}, u32[]{:S(2)}, u32[]{:S(2)}) collective-permute-start(bf16[256,512]{1,0:T(8,128)(2,1)S(1)} %collective-permute-done.7.refs_7_), channel_id=1, source_target_pairs={{0,6},{2,0},{4,2},{6,4},{1,7},{3,1},{5,3},{7,5},{8,14},{10,8},{12,... | collective-permute-start | bytes 786440 | tf_op jit(solution)/shard_map/ppermute | solution.py:340
  115.7 0.0 collective-permute-done.11.refs_5_
  115.7 0.1 collective-permute-start.4
  115.8 1.7 %collective-permute-done.17.refs_3_ = bf16[256,512]{1,0:T(8,128)(2,1)S(1)} collective-permute-done((bf16[256,512]{1,0:T(8,128)(2,1)S(1)}, bf16[256,512]{1,0:T(8,128)(2,1)S(1)}, u32[]{:S(2)}, u32[]{:S(2)}) %collective-permute-start.17) | collective-permute-done | bytes 262176 | tf_op jit(solution)/shard_map/ppermute | solution.py:339
  117.5 1.0 collective-permute-start.6
  118.5 4.7 %collective-permute-done.8.refs_2_ = bf16[256,512]{1,0:T(8,128)(2,1)S(1)} collective-permute-done((bf16[256,512]{1,0:T(8,128)(2,1)S(1)}, bf16[256,512]{1,0:T(8,128)(2,1)S(1)}, u32[]{:S(2)}, u32[]{:S(2)}) %collective-permute-start.8) | collective-permute-done | bytes 262176 | tf_op jit(solution)/shard_map/ppermute | solution.py:339
  123.1 0.0 collective-permute-start.12
  123.2 1.5 %collective-permute-start.9 = (bf16[256,512]{1,0:T(8,128)(2,1)S(1)}, bf16[256,512]{1,0:T(8,128)(2,1)S(1)}, u32[]{:S(2)}, u32[]{:S(2)}) collective-permute-start(bf16[256,512]{1,0:T(8,128)(2,1)S(1)} %collective-permute-done.8.refs_2_), channel_id=1, source_target_pairs={{0,2},{2,4},{4,6},{6,0},{1,3},{3,5},{5,7},{7,1},{8,10},{10,12},{12... | collective-permute-start | bytes 786440 | tf_op jit(solution)/shard_map/ppermute | solution.py:343
  124.6 5.7 %order.1 = (bf16[8,128,512]{2,1,0:T(8,128)(2,1)S(1)}, bf16[8,128,512]{2,1,0:T(8,128)(2,1)S(1)}, bf16[8,128,512]{2,1,0:T(8,128)(2,1)S(1)}, bf16[8,128,512]{2,1,0:T(8,128)(2,1)S(1)}) custom-call(bf16[4,4,128,512]{3,2,1,0:T(8,128)(2,1)S(1)} %pad_maximum_fusion.own_ref, bf16[4,4,128,512]{3,2,1,0:T(8,128)(2,1)S(1)} %collective-permute-done.16.sibling_ref), custom_call_target="tpu_custom_call" | custom-call | tf_op jit(solution)/shard_map/order/pallas_call | solution.py:247
  130.4 1.2 project.2.refs_6_
  131.6 0.7 project.3.before_ref
  132.4 0.0 collective-permute-done.6.lower_ref
  132.4 0.0 collective-permute-done.12.lower_far_ref
  132.4 2.0 %collective-permute-done.9.upper_far_ref = bf16[256,512]{1,0:T(8,128)(2,1)S(1)} collective-permute-done((bf16[256,512]{1,0:T(8,128)(2,1)S(1)}, bf16[256,512]{1,0:T(8,128)(2,1)S(1)}, u32[]{:S(2)}, u32[]{:S(2)}) %collective-permute-start.9) | collective-permute-done | bytes 262176 | tf_op jit(solution)/shard_map/ppermute | solution.py:343
  134.4 1.5 %finish.1 = bf16[512,512]{1,0:T(8,128)(2,1)} custom-call(bf16[256,512]{1,0:T(8,128)(2,1)S(1)} %collective-permute-done.4.upper_ref, bf16[256,512]{1,0:T(8,128)(2,1)S(1)} %collective-permute-done.6.lower_ref, bf16[256,512]{1,0:T(8,128)(2,1)S(1)} %collective-permute-done.9.upper_far_ref, bf16[256,512]{1,0:T(8,128)(2,1)S(1)} %collective-permute-done.12.lower_far_ref, ...), custom_call_target="tpu_custom_call" | custom-call | tf_op jit(solution)/shard_map/finish/pallas_call | solution.py:307
  (11 shorter events, 0.1 us)
Async XLA Ops:
  0.0 15.2 %copy-start.2 = (bf16[128,512]{1,0:T(8,128)(2,1)S(1)}, bf16[128,512]{1,0:T(8,128)(2,1)}, u32[]{:S(2)}) copy-start(bf16[128,512]{1,0:T(8,128)(2,1)} %param.16) | copy-start | bytes 393220
  2.6 44.7 %all-to-all-start = ((bf16[32,32,512]{2,1,0:T(8,128)(2,1)}), bf16[32,32,512]{2,1,0:T(8,128)(2,1)S(1)}, u32[]{:S(2)}, u32[]{:S(2)}) async-start(bf16[32,32,512]{2,1,0:T(8,128)(2,1)} %prepare.1), calls=%async_computation | async-start | bytes 2097152 | tf_op jit(solution)/shard_map/all_to_all | solution.py:323
  15.2 48.1 %collective-permute-start = (bf16[128,512]{1,0:T(8,128)(2,1)S(1)}, bf16[128,512]{1,0:T(8,128)(2,1)S(1)}, u32[]{:S(2)}, u32[]{:S(2)}) collective-permute-start(bf16[128,512]{1,0:T(8,128)(2,1)S(1)} %copy-done.2), channel_id=1, source_target_pairs={{0,16},{16,32},{32,48},{48,0},{1,17},{17,33},{33,49},{49,1},{2,18}... | collective-permute-start | bytes 393224 | tf_op jit(solution)/shard_map/ppermute | solution.py:325
  17.6 45.8 %collective-permute-start.1 = (bf16[128,512]{1,0:T(8,128)(2,1)S(1)}, bf16[128,512]{1,0:T(8,128)(2,1)S(1)}, u32[]{:S(2)}, u32[]{:S(2)}) collective-permute-start(bf16[128,512]{1,0:T(8,128)(2,1)S(1)} %copy-done.2), channel_id=1, source_target_pairs={{0,32},{16,48},{32,0},{48,16},{1,33},{17,49},{33,1},{49,17},{2,34}... | collective-permute-start | bytes 393224 | tf_op jit(solution)/shard_map/ppermute | solution.py:325
  20.9 42.5 %collective-permute-start.2 = (bf16[128,512]{1,0:T(8,128)(2,1)S(1)}, bf16[128,512]{1,0:T(8,128)(2,1)S(1)}, u32[]{:S(2)}, u32[]{:S(2)}) collective-permute-start(bf16[128,512]{1,0:T(8,128)(2,1)S(1)} %copy-done.2), channel_id=1, source_target_pairs={{0,48},{16,0},{32,16},{48,32},{1,49},{17,1},{33,17},{49,33},{2,50}... | collective-permute-start | bytes 393224 | tf_op jit(solution)/shard_map/ppermute | solution.py:325
  47.3 1.0 copy-start.1
  63.3 23.3 %copy-start = (bf16[512,512]{1,0:T(8,128)(2,1)S(1)}, bf16[512,512]{1,0:T(8,128)(2,1)}, u32[]{:S(2)}) copy-start(bf16[512,512]{1,0:T(8,128)(2,1)} %query_ref.1) | copy-start | bytes 1572868
  63.4 23.3 %all-to-all-start.1 = ((bf16[32,16,512]{2,1,0:T(8,128)(2,1)}), bf16[32,16,512]{2,1,0:T(8,128)(2,1)S(1)}, u32[]{:S(2)}, u32[]{:S(2)}) async-start(bf16[32,16,512]{2,1,0:T(8,128)(2,1)} %convolve.1), calls=%async_computation.1 | async-start | bytes 1048576 | tf_op jit(solution)/shard_map/all_to_all | solution.py:330
  70.1 20.3 %collective-permute-start.13 = (bf16[4,128,512]{2,1,0:T(8,128)(2,1)S(1)}, bf16[4,128,512]{2,1,0:T(8,128)(2,1)S(1)}, u32[]{:S(2)}, u32[]{:S(2)}) collective-permute-start(bf16[4,128,512]{2,1,0:T(8,128)(2,1)S(1)} %pad_maximum_fusion.1), channel_id=1, source_target_pairs={{0,64},{64,128},{128,192},{192,0},{1,65},{65,129},{129,193},{193,1... | collective-permute-start | bytes 1572872 | tf_op jit(solution)/shard_map/ppermute | solution.py:329
  71.7 30.1 %collective-permute-start.14 = (bf16[4,128,512]{2,1,0:T(8,128)(2,1)S(1)}, bf16[4,128,512]{2,1,0:T(8,128)(2,1)S(1)}, u32[]{:S(2)}, u32[]{:S(2)}) collective-permute-start(bf16[4,128,512]{2,1,0:T(8,128)(2,1)S(1)} %pad_maximum_fusion.1), channel_id=1, source_target_pairs={{0,128},{64,192},{128,0},{192,64},{1,129},{65,193},{129,1},{193,65... | collective-permute-start | bytes 1572872 | tf_op jit(solution)/shard_map/ppermute | solution.py:329
  74.2 27.6 %collective-permute-start.15 = (bf16[4,128,512]{2,1,0:T(8,128)(2,1)S(1)}, bf16[4,128,512]{2,1,0:T(8,128)(2,1)S(1)}, u32[]{:S(2)}, u32[]{:S(2)}) collective-permute-start(bf16[4,128,512]{2,1,0:T(8,128)(2,1)S(1)} %pad_maximum_fusion.1), channel_id=1, source_target_pairs={{0,192},{64,0},{128,64},{192,128},{1,193},{65,1},{129,65},{193,129... | collective-permute-start | bytes 1572872 | tf_op jit(solution)/shard_map/ppermute | solution.py:329
  86.9 14.9 %collective-permute-start.3 = (bf16[512,512]{1,0:T(8,128)(2,1)S(1)}, bf16[512,512]{1,0:T(8,128)(2,1)S(1)}, u32[]{:S(2)}, u32[]{:S(2)}) collective-permute-start(bf16[512,512]{1,0:T(8,128)(2,1)S(1)} %get-tuple-element.24.refs_4_), channel_id=1, source_target_pairs={{0,2},{2,4},{4,6},{6,0},{1,3},{3,5},{5,7},{7,1},{8,10},{10,12},{12... | collective-permute-start | bytes 1572872 | tf_op jit(solution)/shard_map/ppermute | solution.py:333
  88.3 13.5 %collective-permute-start.5 = (bf16[512,512]{1,0:T(8,128)(2,1)S(1)}, bf16[512,512]{1,0:T(8,128)(2,1)S(1)}, u32[]{:S(2)}, u32[]{:S(2)}) collective-permute-start(bf16[512,512]{1,0:T(8,128)(2,1)S(1)} %get-tuple-element.24.refs_4_), channel_id=1, source_target_pairs={{0,6},{2,0},{4,2},{6,4},{1,7},{3,1},{5,3},{7,5},{8,14},{10,8},{12,... | collective-permute-start | bytes 1572872 | tf_op jit(solution)/shard_map/ppermute | solution.py:334
  90.4 11.4 %collective-permute-start.10 = (bf16[256,512]{1,0:T(8,128)(2,1)S(1)}, bf16[256,512]{1,0:T(8,128)(2,1)S(1)}, u32[]{:S(2)}, u32[]{:S(2)}) collective-permute-start(bf16[256,512]{1,0:T(8,128)(2,1)S(1)} %get-tuple-element.26), channel_id=1, source_target_pairs={{0,1},{1,0},{2,3},{3,2},{4,5},{5,4},{6,7},{7,6},{8,9},{9,8},{10,11... | collective-permute-start | bytes 786440 | tf_op jit(solution)/shard_map/ppermute | solution.py:335
  102.1 21.1 %collective-permute-start.16 = (bf16[4,4,128,512]{3,2,1,0:T(8,128)(2,1)S(1)}, bf16[4,4,128,512]{3,2,1,0:T(8,128)(2,1)S(1)}, u32[]{:S(2)}, u32[]{:S(2)}) collective-permute-start(bf16[4,4,128,512]{3,2,1,0:T(8,128)(2,1)S(1)} %pad_maximum_fusion.own_ref), channel_id=1, source_target_pairs={{0,8},{8,0},{1,9},{9,1},{2,10},{10,2},{3,11},{11,3},{4,12},{12,4},... | collective-permute-start | bytes 6291464 | tf_op jit(solution)/shard_map/ppermute | solution.py:338
  103.1 9.8 %collective-permute-start.7 = (bf16[256,512]{1,0:T(8,128)(2,1)S(1)}, bf16[256,512]{1,0:T(8,128)(2,1)S(1)}, u32[]{:S(2)}, u32[]{:S(2)}) collective-permute-start(bf16[256,512]{1,0:T(8,128)(2,1)S(1)} %get-tuple-element.25), channel_id=1, source_target_pairs={{0,1},{1,0},{2,3},{3,2},{4,5},{5,4},{6,7},{7,6},{8,9},{9,8},{10,11... | collective-permute-start | bytes 786440 | tf_op jit(solution)/shard_map/ppermute | solution.py:332
  106.4 9.4 %collective-permute-start.11 = (bf16[256,512]{1,0:T(8,128)(2,1)S(1)}, bf16[256,512]{1,0:T(8,128)(2,1)S(1)}, u32[]{:S(2)}, u32[]{:S(2)}) collective-permute-start(bf16[256,512]{1,0:T(8,128)(2,1)S(1)} %collective-permute-done.10.refs_8_), channel_id=1, source_target_pairs={{0,6},{2,0},{4,2},{6,4},{1,7},{3,1},{5,3},{7,5},{8,14},{10,8},{12,... | collective-permute-start | bytes 786440 | tf_op jit(solution)/shard_map/ppermute | solution.py:340
  109.1 8.4 %collective-permute-start.17 = (bf16[256,512]{1,0:T(8,128)(2,1)S(1)}, bf16[256,512]{1,0:T(8,128)(2,1)S(1)}, u32[]{:S(2)}, u32[]{:S(2)}) collective-permute-start(bf16[256,512]{1,0:T(8,128)(2,1)S(1)} %collective-permute-done.10.refs_8_), channel_id=1, source_target_pairs={{0,2},{2,4},{4,6},{6,0},{1,3},{3,5},{5,7},{7,1},{8,10},{10,12},{12... | collective-permute-start | bytes 786440 | tf_op jit(solution)/shard_map/ppermute | solution.py:339
  112.9 10.2 %collective-permute-start.8 = (bf16[256,512]{1,0:T(8,128)(2,1)S(1)}, bf16[256,512]{1,0:T(8,128)(2,1)S(1)}, u32[]{:S(2)}, u32[]{:S(2)}) collective-permute-start(bf16[256,512]{1,0:T(8,128)(2,1)S(1)} %collective-permute-done.7.refs_7_), channel_id=1, source_target_pairs={{0,2},{2,4},{4,6},{6,0},{1,3},{3,5},{5,7},{7,1},{8,10},{10,12},{12... | collective-permute-start | bytes 786440 | tf_op jit(solution)/shard_map/ppermute | solution.py:339
  114.2 17.4 %collective-permute-start.18 = (bf16[256,512]{1,0:T(8,128)(2,1)S(1)}, bf16[256,512]{1,0:T(8,128)(2,1)S(1)}, u32[]{:S(2)}, u32[]{:S(2)}) collective-permute-start(bf16[256,512]{1,0:T(8,128)(2,1)S(1)} %collective-permute-done.7.refs_7_), channel_id=1, source_target_pairs={{0,6},{2,0},{4,2},{6,4},{1,7},{3,1},{5,3},{7,5},{8,14},{10,8},{12,... | collective-permute-start | bytes 786440 | tf_op jit(solution)/shard_map/ppermute | solution.py:340
  115.7 16.6 %collective-permute-start.4 = (bf16[256,512]{1,0:T(8,128)(2,1)S(1)}, bf16[256,512]{1,0:T(8,128)(2,1)S(1)}, u32[]{:S(2)}, u32[]{:S(2)}) collective-permute-start(bf16[256,512]{1,0:T(8,128)(2,1)S(1)} %slice.8), channel_id=1, source_target_pairs={{0,2},{2,4},{4,6},{6,0},{1,3},{3,5},{5,7},{7,1},{8,10},{10,12},{12... | collective-permute-start | bytes 786440 | tf_op jit(solution)/shard_map/ppermute | solution.py:341
  117.5 14.8 %collective-permute-start.6 = (bf16[256,512]{1,0:T(8,128)(2,1)S(1)}, bf16[256,512]{1,0:T(8,128)(2,1)S(1)}, u32[]{:S(2)}, u32[]{:S(2)}) collective-permute-start(bf16[256,512]{1,0:T(8,128)(2,1)S(1)} %slice.9), channel_id=1, source_target_pairs={{0,6},{2,0},{4,2},{6,4},{1,7},{3,1},{5,3},{7,5},{8,14},{10,8},{12,... | collective-permute-start | bytes 786440 | tf_op jit(solution)/shard_map/ppermute | solution.py:342
  123.1 9.2 %collective-permute-start.12 = (bf16[256,512]{1,0:T(8,128)(2,1)S(1)}, bf16[256,512]{1,0:T(8,128)(2,1)S(1)}, u32[]{:S(2)}, u32[]{:S(2)}) collective-permute-start(bf16[256,512]{1,0:T(8,128)(2,1)S(1)} %collective-permute-done.11.refs_5_), channel_id=1, source_target_pairs={{0,6},{2,0},{4,2},{6,4},{1,7},{3,1},{5,3},{7,5},{8,14},{10,8},{12,... | collective-permute-start | bytes 786440 | tf_op jit(solution)/shard_map/ppermute | solution.py:344
  123.2 11.2 %collective-permute-start.9 = (bf16[256,512]{1,0:T(8,128)(2,1)S(1)}, bf16[256,512]{1,0:T(8,128)(2,1)S(1)}, u32[]{:S(2)}, u32[]{:S(2)}) collective-permute-start(bf16[256,512]{1,0:T(8,128)(2,1)S(1)} %collective-permute-done.8.refs_2_), channel_id=1, source_target_pairs={{0,2},{2,4},{4,6},{6,0},{1,3},{3,5},{5,7},{7,1},{8,10},{10,12},{12... | collective-permute-start | bytes 786440 | tf_op jit(solution)/shard_map/ppermute | solution.py:343

commit v4 on v3

v4 whole, which is shorter than its diff:
```python
import functools
import math

import jax
import jax.numpy as jnp
import numpy as np
from jax import lax
from jax.experimental import pallas as pl
from jax.experimental.pallas import tpu as pltpu
from jax.sharding import Mesh
from jax.sharding import PartitionSpec as P

AXES = ("x", "zh", "core", "y", "zl")
TOKENS = ("x", "zh", "core")
BLOCKS = 32
BLOCK = 512
CHANNELS = 16
SLICE = 8
HALF = 256
STEPS = 64
INNER = 256
PERIOD = 32768
PAIR = [(0, 1), (1, 0)]


def halves(table):
    high = table.astype(np.float32).astype(jnp.bfloat16)
    low = (table - high.astype(np.float64)).astype(np.float32).astype(jnp.bfloat16)
    return high, low


def tables():
    odd = np.arange(STEPS // 2) + 0.5
    same = np.eye(SLICE)
    first, last = [], []
    for parity in range(2):
        outer = 2 * math.pi * np.outer(odd, 2 * np.arange(BLOCKS) + parity) / (2 * STEPS)
        first.append(np.concatenate([np.kron(np.cos(outer), same), np.kron(-np.sin(outer), same)], 0))
        last.append(first[-1].T / (PERIOD // 2))
    inner = np.arange(INNER)
    turn = 2 * math.pi * np.outer(np.concatenate([odd, STEPS - odd]), inner) / PERIOD
    turn = np.stack([np.cos(turn), np.sin(turn)]).astype(np.float32)
    angle = 2 * math.pi * (np.outer(inner, inner) % INNER) / INNER
    cos_i, sin_i = np.cos(angle), np.sin(angle)
    ahead = np.block([[cos_i, -sin_i], [sin_i, cos_i]])
    back = np.block([[cos_i, sin_i], [-sin_i, cos_i]])
    return (
        np.stack([np.concatenate(halves(table), 1) for table in first]),
        turn,
        np.concatenate(halves(ahead), 0),
        np.concatenate(halves(back), 0),
        np.stack([np.concatenate(halves(table), 1) for table in last]),
    )


def dot(left, right):
    return jnp.dot(left, right, preferred_element_type=jnp.float32)


def split(value):
    high = value.astype(jnp.bfloat16)
    return high, (value - high.astype(jnp.float32)).astype(jnp.bfloat16)


def params(mebibytes):
    return pltpu.CompilerParams(vmem_limit_bytes=mebibytes * 1024 * 1024)


def whole():
    return pl.BlockSpec(memory_space=pltpu.VMEM)


def anywhere():
    return pl.BlockSpec(memory_space=pl.ANY)


def prepare_kernel(key_hbm, value_hbm, filter_hbm, out_hbm, key_ref, value_ref, filter_ref, out_ref, sems, out_sems):
    moves = []
    for i in range(4):
        columns = pl.ds(i * 128, 128)
        for j, (far, near) in enumerate(((key_hbm, key_ref), (value_hbm, value_ref), (filter_hbm, filter_ref))):
            moves.append(pltpu.make_async_copy(far.at[:, columns], near.at[i], sems.at[i, j]))
            moves[-1].start()
    outs = []
    for i in range(4):
        for move in moves[3 * i : 3 * i + 3]:
            move.wait()
        source = key_ref[i].astype(jnp.float32) * value_ref[i].astype(jnp.float32)
        source = source.T.reshape(8, CHANNELS, BLOCK)
        taps = filter_ref[i].T.reshape(8, CHANNELS, BLOCK)
        out_ref[i] = jnp.concatenate([source, taps], 1).astype(jnp.bfloat16)
        outs.append(pltpu.make_async_copy(out_ref.at[i], out_hbm.at[pl.ds(i * 8, 8)], out_sems.at[i]))
        outs[-1].start()
    for out in outs:
        out.wait()


def prepare(key, value, taps):
    return pl.pallas_call(
        prepare_kernel,
        out_shape=jax.ShapeDtypeStruct((BLOCKS, 2 * CHANNELS, BLOCK), jnp.bfloat16),
        in_specs=[anywhere()] * 3,
        out_specs=anywhere(),
        scratch_shapes=[
            pltpu.VMEM((4, BLOCK, 128), jnp.bfloat16),
            pltpu.VMEM((4, BLOCK, 128), jnp.bfloat16),
            pltpu.VMEM((4, BLOCK, 128), jnp.float32),
            pltpu.VMEM((4, 8, 2 * CHANNELS, BLOCK), jnp.bfloat16),
            pltpu.SemaphoreType.DMA((4, 3)),
            pltpu.SemaphoreType.DMA((4,)),
        ],
        compiler_params=params(56),
        name="prepare",
    )(key, value, taps)


def thrice(table_ref):
    return jnp.concatenate([table_ref[:BLOCK], table_ref[...]], 0)


def convolve_kernel(got_ref, gain_ref, turn_ref, *refs):
    out_ref, tables_here, sems = refs[4], refs[5:9], refs[9]
    moves = []
    for i in range(4):
        part = refs[i].shape[-2] // 2
        for j in range(4):
            rows = pl.ds(j % 2 * part, part)
            place = (j // 2, rows) if i in (0, 3) else pl.ds(j * (part // 2), part // 2)
            moves.append(pltpu.make_async_copy(refs[i].at[place], tables_here[i].at[place], sems.at[i, j]))

    def started(i):
        for move in moves[4 * i : 4 * i + 4]:
            move.start()

    def arrived(i):
        for move in moves[4 * i : 4 * i + 4]:
            move.wait()

    started(0)
    first_ref, ahead_ref, back_ref, last_ref = tables_here
    place = lax.axis_index("x") * 8 + lax.axis_index("zh") * 2 + lax.axis_index("core")
    cos_t = turn_ref[0][:, None, :]
    sin_t = turn_ref[1][:, None, :]
    rows = STEPS * SLICE
    half = rows // 2

    def turned(real, imag, sign):
        real = real.reshape(STEPS, SLICE, INNER)
        imag = imag.reshape(STEPS, SLICE, INNER)
        one = real * cos_t - (sign * imag) * sin_t
        two = imag * cos_t + (sign * real) * sin_t
        return one.reshape(rows, INNER), two.reshape(rows, INNER)

    got = got_ref[...].astype(jnp.float32).reshape(BLOCKS, 2, 2, SLICE, BLOCK)
    outs = []
    for s in range(2):
        source = got[:, 0, s].reshape(BLOCKS * SLICE, BLOCK)
        taps = got[:, 1, s].reshape(BLOCKS * SLICE, BLOCK)
        sums = []
        for parity in range(2):
            lanes = slice(parity * INNER, (parity + 1) * INNER)
            both = jnp.concatenate([source[:, lanes], taps[:, lanes]], 1).astype(jnp.bfloat16)
            if s == 0 and parity == 0:
                arrived(0)
                for i in (1, 2, 3):
                    started(i)
            sums.append(dot(first_ref[parity], jnp.concatenate([both, both], 0)))
        even, uneven = sums
        real = jnp.concatenate([even[:half] + uneven[:half], even[:half] - uneven[:half]], 0)
        imag = jnp.concatenate([even[half:] + uneven[half:], uneven[half:] - even[half:]], 0)
        if s == 0:
            arrived(1)
        spectra = []
        for part in range(2):
            columns = slice(part * INNER, (part + 1) * INNER)
            high, low = split(jnp.concatenate(turned(real[:, columns], imag[:, columns], -1.0), 1))
            spectra.append(dot(jnp.concatenate([high, low, high], 1), thrice(ahead_ref)))
        (ar, ai), (br, bi) = [(z[:, :INNER], z[:, INNER:]) for z in spectra]
        product = jnp.concatenate([ar * br - ai * bi, ar * bi + ai * br], 1)
        high, low = split(product)
        if s == 0:
            arrived(2)
        inner = dot(jnp.concatenate([high, low, high], 1), thrice(back_ref))
        real, imag = turned(inner[:, :INNER], inner[:, INNER:], 1.0)
        if s == 0:
            arrived(3)
        conv = []
        for parity, sign in ((0, 1.0), (1, -1.0)):
            real_p = real[:half] + sign * real[half:]
            imag_p = imag[:half] - sign * imag[half:]
            high, low = split(jnp.concatenate([real_p, imag_p], 0))
            table = jnp.concatenate([last_ref[parity, :, :BLOCK], last_ref[parity]], 1)
            conv.append(dot(table, jnp.concatenate([high, low, high], 0)))
        conv = jnp.concatenate(conv, 1)
        channel = place * CHANNELS + s * SLICE + lax.broadcasted_iota(jnp.int32, (SLICE, BLOCK), 0)
        picked = channel == lax.broadcasted_iota(jnp.int32, (SLICE, BLOCK), 1)
        gain = jnp.sum(jnp.where(picked, gain_ref[...], 0.0), 1, keepdims=True)
        outs.append(conv.reshape(BLOCKS, SLICE, BLOCK) + gain[None] * source.reshape(BLOCKS, SLICE, BLOCK))
    out_ref[...] = jnp.concatenate(outs, 1).astype(jnp.bfloat16)


def convolve(got, gain):
    first, turn, ahead, back, last = tables()
    return pl.pallas_call(
        convolve_kernel,
        out_shape=jax.ShapeDtypeStruct((BLOCKS, CHANNELS, BLOCK), jnp.bfloat16),
        in_specs=[whole()] * 3 + [anywhere()] * 4,
        out_specs=whole(),
        scratch_shapes=[pltpu.VMEM(table.shape, jnp.bfloat16) for table in (first, ahead, back, last)]
        + [pltpu.SemaphoreType.DMA((4, 4))],
        compiler_params=params(40),
        name="convolve",
    )(got, gain, turn, first, ahead, back, last)


def gate_kernel(conv_ref, query_ref, out_ref):
    conv = conv_ref[...].astype(jnp.float32).reshape(BLOCK, BLOCK).T
    out_ref[...] = (query_ref[...].astype(jnp.float32) * conv).astype(jnp.bfloat16)


def gate(conv, query):
    return pl.pallas_call(
        gate_kernel,
        out_shape=jax.ShapeDtypeStruct((BLOCK, BLOCK), jnp.bfloat16),
        in_specs=[whole()] * 2,
        out_specs=whole(),
        compiler_params=params(16),
        name="gate",
    )(conv, query)


def project_kernel(items, extras, begins, own_w, sibling_w, *refs):
    pieces, refs = refs[: len(items)], refs[len(items) :]
    before_ref, refs = (None, refs) if begins else (refs[0], refs[1:])
    total_ref, (held, sems) = refs[0], refs[-2:]
    core, x, y, zh, line = (lax.axis_index(axis) for axis in ("core", "x", "y", "zh", "zl"))
    moves = []
    for index, (back, far) in enumerate(items + extras):
        away = lax.rem(x - y + back + 4, 4)
        column = 1 - line if far else line
        out = refs[1].at[index - len(items)] if index >= len(items) else held.at[index]
        for j in range(2):
            k = lax.rem(zh + 4 - 2 * column - j, 4)
            mine, other = pl.ds((2 * j + core) * 128, 128), pl.ds((2 * j + 1 - core) * 128, 128)
            moves.append(pltpu.make_async_copy(own_w.at[away, k], out.at[mine], sems.at[index, j, 0]))
            moves.append(pltpu.make_async_copy(sibling_w.at[away, k], out.at[other], sems.at[index, j, 1]))
    for move in moves:
        move.start()
    total = None if begins else before_ref[...]
    for index, piece in enumerate(pieces):
        for move in moves[4 * index : 4 * index + 4]:
            move.wait()
        term = dot(piece[...], held[index])
        total = term if total is None else total + term
    total_ref[...] = total
    for move in moves[4 * len(items) :]:
        move.wait()


def project(weights, items, pieces, before=None, extras=()):
    count = len(items)
    outs = [jax.ShapeDtypeStruct((BLOCK, BLOCK), jnp.float32)]
    if extras:
        outs.append(jax.ShapeDtypeStruct((len(extras), BLOCK, BLOCK), jnp.bfloat16))
    operands = list(pieces) + ([] if before is None else [before])
    return pl.pallas_call(
        functools.partial(project_kernel, items, extras, before is None),
        out_shape=outs,
        in_specs=[anywhere()] * 2 + [whole()] * len(operands),
        out_specs=[whole()] * len(outs),
        scratch_shapes=[
            pltpu.VMEM((count, BLOCK, BLOCK), jnp.bfloat16),
            pltpu.SemaphoreType.DMA((count + len(extras), 2, 2)),
        ],
        compiler_params=params(16),
        cost_estimate=pl.CostEstimate(
            flops=2 * count * BLOCK**3, bytes_accessed=(count + 3) * 2**20, transcendentals=0
        ),
        name="project",
    )(*weights, *operands)


def finish_kernel(after_ref, ahead_ref, weight_ref, before_ref, out_ref):
    total = before_ref[...] + dot(after_ref[...], weight_ref[0]) + dot(ahead_ref[...], weight_ref[1])
    out_ref[...] = total.astype(jnp.bfloat16)


def finish(after, ahead, weight, before):
    return pl.pallas_call(
        finish_kernel,
        out_shape=jax.ShapeDtypeStruct((BLOCK, BLOCK), jnp.bfloat16),
        in_specs=[whole()] * 4,
        out_specs=whole(),
        compiler_params=params(16),
        name="finish",
    )(after, ahead, weight, before)


def along(steps):
    return [(i, (i + steps) % 4) for i in range(4)]


def on_device(query, key, value, taps, gain, weight):
    blocks = prepare(key, value, taps)
    got = lax.all_to_all(blocks, TOKENS, 0, 0, tiled=True)
    weight, _ = lax.optimization_barrier((weight, blocks))
    weight = [weight] + [lax.ppermute(weight, "zh", along(k)) for k in (1, 2, 3)]
    conv = convolve(got, gain.reshape(1, BLOCK))
    conv, *weight = lax.optimization_barrier((conv, *weight))
    weight = jnp.stack(weight)
    weight = [weight] + [lax.ppermute(weight, "x", along(k)) for k in (1, 2, 3)]
    conv = lax.all_to_all(conv, TOKENS, 0, 0, tiled=True)
    gated = gate(conv, query)
    across = lax.ppermute(gated, "y", along(2))
    far = lax.ppermute(gated, "zl", PAIR)
    after = lax.ppermute(gated, "y", along(1))
    ahead = lax.ppermute(gated, "y", along(3))
    across_far = lax.ppermute(across, "zl", PAIR)
    after_far = lax.ppermute(far, "y", along(1))
    ahead_far = lax.ppermute(far, "y", along(3))
    *weight, _, _ = lax.optimization_barrier((*weight, far, across))
    weight = jnp.stack(weight)
    weight = (weight, lax.ppermute(weight, "core", PAIR))
    (total,) = project(weight, ((0, 0), (0, 1), (2, 0)), [gated, far, across])
    total, last = project(
        weight, ((1, 0), (3, 0), (2, 1)), [after, ahead, across_far], total, ((1, 1), (3, 1))
    )
    return finish(after_far, ahead_far, last, total)


def solution(mesh):
    fine = Mesh(mesh.devices.reshape(4, 4, 2, 4, 2), AXES)
    columns = ("y", "zl")
    placed = P(TOKENS, columns)
    return jax.shard_map(
        on_device,
        mesh=fine,
        in_specs=(placed, placed, placed, placed, P(columns), placed),
        out_specs=placed,
        check_vma=False,
    )
```

time: 138 us -> 131 us (0.949); the launches traced: 136 us -> 130 us
  Pallas kernels: 27.1 us -> 21.8 us
  starting transfers between devices: 51.4 us -> 47.1 us
  waiting for transfers between devices: 55.8 us -> 57.5 us
  local copies, waits for them, and re-layouts: 1.06 us -> 2.47 us
    pallas_call x1, Pallas kernels: 15 us -> 9.37 us  [convolve(): pl.pallas_call(convolve_kernel, out_shape=jax.ShapeDtypeStruct((BLOCKS, C...]
    ppermute x1, waiting for transfers between devices: 0.01 us -> 5.07 us  [on_device(): after = lax.ppermute(gated, 'y', along(1))]
    ppermute x11 -> x6, starting transfers between devices: 15.1 us -> 11.1 us  [the longest x1 3.55 us: on_device(): far = lax.ppermute(gated, 'zl', PAIR)]
    ppermute x11 -> x6, waiting for transfers between devices: 12.2 us -> 9.44 us  [the longest x1 5.69 us: on_device(): after_far = lax.ppermute(far, 'y', along(1))]
    unnamed x6 -> x16, local copies, waits for them, and re-layouts: 1.02 us -> 2.47 us
    pallas_call x4 -> x3, Pallas kernels: 7.93 us -> 8.14 us  [the longest x2 7.92 us: project(): pl.pallas_call(functools.partial(project_kernel, items, extras, before is...]
  transfers between devices with their start and end apart: 21 -> 16, of which waited for: 8 -> 8; matrix products, arithmetic and copies ran while one was open for 0% -> 1% of each run, Pallas kernels for 17% -> 13%
where the time goes in v4:
time: 131 us; the launch traced here: 130 us
  waiting for transfers between devices  57.5 us (44%)
  starting transfers between devices  47.1 us (36%)
  Pallas kernels  21.8 us (17%)
  local copies, waits for them, and re-layouts  2.47 us (2%)
    all_to_all x1, waiting for transfers between devices, on_device(): got = lax.all_to_all(blocks, TOKENS, 0, 0, tiled=True)  23.2 us
    all_to_all x1, starting transfers between devices, on_device(): got = lax.all_to_all(blocks, TOKENS, 0, 0, tiled=True)  12.6 us
    all_to_all x1, waiting for transfers between devices, on_device(): conv = lax.all_to_all(conv, TOKENS, 0, 0, tiled=True)  10.6 us
    pallas_call x1, Pallas kernels, convolve(): pl.pallas_call(convolve_kernel, out_shape=jax.ShapeDtypeStruct((BLOCKS, C...  9.37 us
    ppermute x3, waiting for transfers between devices, on_device(): weight = [weight] + [lax.ppermute(weight, 'x', along(k)) for k in (1, 2, 3)]  9.24 us
    ppermute x3, starting transfers between devices, on_device(): lax.ppermute(weight, 'zh', along(k))  8.95 us
    pallas_call x2, Pallas kernels, project(): pl.pallas_call(functools.partial(project_kernel, items, extras, before is...  7.92 us
    all_to_all x1, starting transfers between devices, on_device(): conv = lax.all_to_all(conv, TOKENS, 0, 0, tiled=True)  6.63 us
  transfers between devices with their start and end apart: 16, of which 8 were waited for; matrix products, arithmetic and copies ran while one was open for 1% of the time, Pallas kernels for 13%

profile of v4, /device:TPU:1, one launch (start us, length us, event | category | flops | bytes accessed | tf_op | source)
XLA Modules:
  0.0 130.3 jit_solution(18027891781930389629)
XLA Ops:
  0.0 0.0 copy-start.7
  0.0 0.0 copy-start.6
  0.0 2.8 %prepare.1 = bf16[32,32,512]{2,1,0:T(8,128)(2,1)} custom-call(bf16[512,512]{1,0:T(8,128)(2,1)} %key_hbm.1, bf16[512,512]{1,0:T(8,128)(2,1)} %value_hbm.1, f32[512,512]{1,0:T(8,128)} %filter_hbm.1), custom_call_target="tpu_custom_call" | custom-call | tf_op jit(solution)/shard_map/prepare/pallas_call | solution.py:99
  2.8 12.6 %all-to-all-start = ((bf16[32,32,512]{2,1,0:T(8,128)(2,1)}), bf16[32,32,512]{2,1,0:T(8,128)(2,1)S(1)}, u32[]{:S(2)}, u32[]{:S(2)}) async-start(bf16[32,32,512]{2,1,0:T(8,128)(2,1)} %prepare.1), calls=%async_computation | async-start | bytes 2097152 | tf_op jit(solution)/shard_map/all_to_all | solution.py:305
  15.4 0.0 copy-done.7
  15.4 2.4 %collective-permute-start = (bf16[128,512]{1,0:T(8,128)(2,1)S(1)}, bf16[128,512]{1,0:T(8,128)(2,1)S(1)}, u32[]{:S(2)}, u32[]{:S(2)}) collective-permute-start(bf16[128,512]{1,0:T(8,128)(2,1)S(1)} %copy-done.7), channel_id=1, source_target_pairs={{0,16},{16,32},{32,48},{48,0},{1,17},{17,33},{33,49},{49,1},{2,18}... | collective-permute-start | bytes 393224 | tf_op jit(solution)/shard_map/ppermute | solution.py:307
  17.8 3.3 %collective-permute-start.1 = (bf16[128,512]{1,0:T(8,128)(2,1)S(1)}, bf16[128,512]{1,0:T(8,128)(2,1)}, u32[]{:S(2)}, u32[]{:S(2)}) collective-permute-start(bf16[128,512]{1,0:T(8,128)(2,1)S(1)} %copy-done.7), channel_id=1, source_target_pairs={{0,32},{16,48},{32,0},{48,16},{1,33},{17,49},{33,1},{49,17},{2,34}... | collective-permute-start | bytes 393224 | tf_op jit(solution)/shard_map/ppermute | solution.py:307
  21.1 3.3 %collective-permute-start.2 = (bf16[128,512]{1,0:T(8,128)(2,1)S(1)}, bf16[128,512]{1,0:T(8,128)(2,1)}, u32[]{:S(2)}, u32[]{:S(2)}) collective-permute-start(bf16[128,512]{1,0:T(8,128)(2,1)S(1)} %copy-done.7), channel_id=1, source_target_pairs={{0,48},{16,0},{32,16},{48,32},{1,49},{17,1},{33,17},{49,33},{2,50}... | collective-permute-start | bytes 393224 | tf_op jit(solution)/shard_map/ppermute | solution.py:307
  24.4 23.2 %all-to-all-done.got_ref = bf16[32,32,512]{2,1,0:T(8,128)(2,1)S(1)} async-done(((bf16[32,32,512]{2,1,0:T(8,128)(2,1)}), bf16[32,32,512]{2,1,0:T(8,128)(2,1)S(1)}, u32[]{:S(2)}, u32[]{:S(2)}) %all-to-all-start) | async-done | bytes 1048608 | tf_op jit(solution)/shard_map/all_to_all | solution.py:305
  47.6 0.0 copy-done
  47.6 0.0 copy-start.2
  47.6 1.2 copy-done.2
  48.8 1.2 copy-done.3
  50.0 9.4 %convolve.1 = bf16[32,16,512]{2,1,0:T(8,128)(2,1)} custom-call(bf16[32,32,512]{2,1,0:T(8,128)(2,1)S(1)} %all-to-all-done.got_ref, f32[1,512]{1,0:T(1,128)S(1)} %bitcast.9, f32[2,64,256]{2,1,0:T(8,128)S(1)} %copy-done.5, bf16[2,512,512]{2,1,0:T(8,128)(2,1)S(1)} %copy-done, bf16[1024,512]{1,0:T(8,128)(2,1)S(1)} %copy-done.1, bf16[1024,512]{1,0:T(8,128)(2,1)S(1)} %copy-done.2, ...), custom_call_target="tpu_custom_call" | custom-call | tf_op jit(solution)/shard_map/convolve/pallas_call | solution.py:204
  59.4 0.0 copy-start.4
  59.4 0.0 collective-permute-done
  59.4 0.0 collective-permute-done.1
  59.5 0.0 collective-permute-done.2
  59.5 6.6 %all-to-all-start.1 = ((bf16[32,16,512]{2,1,0:T(8,128)(2,1)}), bf16[32,16,512]{2,1,0:T(8,128)(2,1)S(1)}, u32[]{:S(2)}, u32[]{:S(2)}) async-start(bf16[32,16,512]{2,1,0:T(8,128)(2,1)} %convolve.1), calls=%async_computation.1 | async-start | bytes 1048576 | tf_op jit(solution)/shard_map/all_to_all | solution.py:312
  66.1 1.0 pad_maximum_fusion.1
  67.1 1.5 %collective-permute-start.6 = (bf16[4,128,512]{2,1,0:T(8,128)(2,1)S(1)}, bf16[4,128,512]{2,1,0:T(8,128)(2,1)S(1)}, u32[]{:S(2)}, u32[]{:S(2)}) collective-permute-start(bf16[4,128,512]{2,1,0:T(8,128)(2,1)S(1)} %pad_maximum_fusion.1), channel_id=1, source_target_pairs={{0,64},{64,128},{128,192},{192,0},{1,65},{65,129},{129,193},{193,1... | collective-permute-start | bytes 1572872 | tf_op jit(solution)/shard_map/ppermute | solution.py:311
  68.6 2.4 %collective-permute-start.7 = (bf16[4,128,512]{2,1,0:T(8,128)(2,1)S(1)}, bf16[4,128,512]{2,1,0:T(8,128)(2,1)S(1)}, u32[]{:S(2)}, u32[]{:S(2)}) collective-permute-start(bf16[4,128,512]{2,1,0:T(8,128)(2,1)S(1)} %pad_maximum_fusion.1), channel_id=1, source_target_pairs={{0,128},{64,192},{128,0},{192,64},{1,129},{65,193},{129,1},{193,65... | collective-permute-start | bytes 1572872 | tf_op jit(solution)/shard_map/ppermute | solution.py:311
  71.0 1.1 collective-permute-start.8
  72.2 10.6 %all-to-all-done.1.conv_ref = bf16[32,16,512]{2,1,0:T(8,128)(2,1)S(1)} async-done(((bf16[32,16,512]{2,1,0:T(8,128)(2,1)}), bf16[32,16,512]{2,1,0:T(8,128)(2,1)S(1)}, u32[]{:S(2)}, u32[]{:S(2)}) %all-to-all-start.1) | async-done | bytes 524320 | tf_op jit(solution)/shard_map/all_to_all | solution.py:312
  82.7 0.2 gate.1.refs_0_
  83.0 3.6 %collective-permute-start.3 = (bf16[512,512]{1,0:T(8,128)(2,1)S(1)}, bf16[512,512]{1,0:T(8,128)(2,1)S(1)}, u32[]{:S(2)}, u32[]{:S(2)}) collective-permute-start(bf16[512,512]{1,0:T(8,128)(2,1)S(1)} %gate.1.refs_0_), channel_id=1, source_target_pairs={{0,1},{1,0},{2,3},{3,2},{4,5},{5,4},{6,7},{7,6},{8,9},{9,8},{10,11... | collective-permute-start | bytes 1572872 | tf_op jit(solution)/shard_map/ppermute | solution.py:315
  86.5 2.9 %collective-permute-start.9 = (bf16[512,512]{1,0:T(8,128)(2,1)S(1)}, bf16[512,512]{1,0:T(8,128)(2,1)S(1)}, u32[]{:S(2)}, u32[]{:S(2)}) collective-permute-start(bf16[512,512]{1,0:T(8,128)(2,1)S(1)} %gate.1.refs_0_), channel_id=1, source_target_pairs={{0,4},{2,6},{4,0},{6,2},{1,5},{3,7},{5,1},{7,3},{8,12},{10,14},{12... | collective-permute-start | bytes 1572872 | tf_op jit(solution)/shard_map/ppermute | solution.py:314
  89.5 0.0 collective-permute-done.6
  89.5 9.2 %collective-permute-done.7 = bf16[4,128,512]{2,1,0:T(8,128)(2,1)S(1)} collective-permute-done((bf16[4,128,512]{2,1,0:T(8,128)(2,1)S(1)}, bf16[4,128,512]{2,1,0:T(8,128)(2,1)S(1)}, u32[]{:S(2)}, u32[]{:S(2)}) %collective-permute-start.7) | collective-permute-done | bytes 524320 | tf_op jit(solution)/shard_map/ppermute | solution.py:311
  98.7 0.0 collective-permute-done.8
  98.7 0.0 collective-permute-done.3.refs_1_
  98.7 2.0 %collective-permute-done.9.refs_2_ = bf16[512,512]{1,0:T(8,128)(2,1)S(1)} collective-permute-done((bf16[512,512]{1,0:T(8,128)(2,1)S(1)}, bf16[512,512]{1,0:T(8,128)(2,1)S(1)}, u32[]{:S(2)}, u32[]{:S(2)}) %collective-permute-start.9) | collective-permute-done | bytes 524320 | tf_op jit(solution)/shard_map/ppermute | solution.py:314
  100.7 0.3 pad_maximum_fusion.own_w
  101.0 1.8 %collective-permute-start.10 = (bf16[4,4,128,512]{3,2,1,0:T(8,128)(2,1)S(1)}, bf16[4,4,128,512]{3,2,1,0:T(8,128)(2,1)S(1)}, u32[]{:S(2)}, u32[]{:S(2)}) collective-permute-start(bf16[4,4,128,512]{3,2,1,0:T(8,128)(2,1)S(1)} %pad_maximum_fusion.own_w), channel_id=1, source_target_pairs={{0,8},{8,0},{1,9},{9,1},{2,10},{10,2},{3,11},{11,3},{4,12},{12,4},... | collective-permute-start | bytes 6291464 | tf_op jit(solution)/shard_map/ppermute | solution.py:323
  102.7 1.3 collective-permute-start.11
  104.0 1.5 %collective-permute-start.12 = (bf16[512,512]{1,0:T(8,128)(2,1)S(1)}, bf16[512,512]{1,0:T(8,128)(2,1)S(1)}, u32[]{:S(2)}, u32[]{:S(2)}) collective-permute-start(bf16[512,512]{1,0:T(8,128)(2,1)S(1)} %gate.1.refs_0_), channel_id=1, source_target_pairs={{0,6},{2,0},{4,2},{6,4},{1,7},{3,1},{5,3},{7,5},{8,14},{10,8},{12,... | collective-permute-start | bytes 1572872 | tf_op jit(solution)/shard_map/ppermute | solution.py:317
  105.5 0.1 collective-permute-start.13
  105.6 0.0 collective-permute-start.4
  105.6 0.9 collective-permute-done.10.sibling_w
  106.5 2.8 %collective-permute-start.5 = (bf16[512,512]{1,0:T(8,128)(2,1)S(1)}, bf16[512,512]{1,0:T(8,128)(2,1)S(1)}, u32[]{:S(2)}, u32[]{:S(2)}) collective-permute-start(bf16[512,512]{1,0:T(8,128)(2,1)S(1)} %collective-permute-done.3.refs_1_), channel_id=1, source_target_pairs={{0,6},{2,0},{4,2},{6,4},{1,7},{3,1},{5,3},{7,5},{8,14},{10,8},{12,... | collective-permute-start | bytes 1572872 | tf_op jit(solution)/shard_map/ppermute | solution.py:320
  109.3 3.2 %project.2.refs_3_ = f32[512,512]{1,0:T(8,128)S(1)} custom-call(bf16[4,4,128,512]{3,2,1,0:T(8,128)(2,1)S(1)} %pad_maximum_fusion.own_w, bf16[4,4,128,512]{3,2,1,0:T(8,128)(2,1)S(1)} %collective-permute-done.10.sibling_w, bf16[512,512]{1,0:T(8,128)(2,1)S(1)} %gate.1.refs_0_, bf16[512,512]{1,0:T(8,128)(2,1)S(1)} %collective-permute-done.3.refs_1_, ...), custom_call_target="tpu_custom_call" | custom-call | flops 805306368 | bytes 6291456 | tf_op jit(solution)/shard_map/project/pallas_call | solution.py:266
  112.5 5.1 %collective-permute-done.11.refs_0_ = bf16[512,512]{1,0:T(8,128)(2,1)S(1)} collective-permute-done((bf16[512,512]{1,0:T(8,128)(2,1)S(1)}, bf16[512,512]{1,0:T(8,128)(2,1)S(1)}, u32[]{:S(2)}, u32[]{:S(2)}) %collective-permute-start.11) | collective-permute-done | bytes 524320 | tf_op jit(solution)/shard_map/ppermute | solution.py:316
  117.5 0.0 collective-permute-done.12.refs_1_
  117.6 0.8 collective-permute-done.13.refs_2_
  118.4 4.7 %project.3 = (f32[512,512]{1,0:T(8,128)S(1)}, bf16[2,512,512]{2,1,0:T(8,128)(2,1)S(1)}) custom-call(bf16[4,4,128,512]{3,2,1,0:T(8,128)(2,1)S(1)} %pad_maximum_fusion.own_w, bf16[4,4,128,512]{3,2,1,0:T(8,128)(2,1)S(1)} %collective-permute-done.10.sibling_w, bf16[512,512]{1,0:T(8,128)(2,1)S(1)} %collective-permute-done.11.refs_0_, ...), custom_call_target="tpu_custom_call" | custom-call | flops 805306368 | bytes 6291456 | tf_op jit(solution)/shard_map/project/pallas_call | solution.py:266
  123.1 5.7 %collective-permute-done.4.after_ref = bf16[512,512]{1,0:T(8,128)(2,1)S(1)} collective-permute-done((bf16[512,512]{1,0:T(8,128)(2,1)S(1)}, bf16[512,512]{1,0:T(8,128)(2,1)S(1)}, u32[]{:S(2)}, u32[]{:S(2)}) %collective-permute-start.4) | collective-permute-done | bytes 524320 | tf_op jit(solution)/shard_map/ppermute | solution.py:319
  128.8 0.0 collective-permute-done.5.ahead_ref
  128.8 1.5 %finish.1 = bf16[512,512]{1,0:T(8,128)(2,1)} custom-call(bf16[512,512]{1,0:T(8,128)(2,1)S(1)} %collective-permute-done.4.after_ref, bf16[512,512]{1,0:T(8,128)(2,1)S(1)} %collective-permute-done.5.ahead_ref, bf16[2,512,512]{2,1,0:T(8,128)(2,1)S(1)} %get-tuple-element.27.weight_ref, f32[512,512]{1,0:T(8,128)S(1)} %get-tuple-element.28.before_ref), custom_call_target="tpu_custom_call" | custom-call | tf_op jit(solution)/shard_map/finish/pallas_call | solution.py:289
  (8 shorter events, 0.0 us)
Async XLA Ops:
  0.0 47.6 %copy-start = (bf16[2,512,512]{2,1,0:T(8,128)(2,1)S(1)}, bf16[2,512,512]{2,1,0:T(8,128)(2,1)}, u32[]{:S(2)}) copy-start(bf16[2,512,512]{2,1,0:T(8,128)(2,1)} %constant.11.clone.refs_0_) | copy-start | bytes 3145732
  0.0 47.6 %copy-start.1 = (bf16[1024,512]{1,0:T(8,128)(2,1)S(1)}, bf16[1024,512]{1,0:T(8,128)(2,1)}, u32[]{:S(2)}) copy-start(bf16[1024,512]{1,0:T(8,128)(2,1)} %constant.12.clone.refs_1_) | copy-start | bytes 3145732
  0.0 47.6 %copy-start.5 = (f32[2,64,256]{2,1,0:T(8,128)S(1)}, f32[2,64,256]{2,1,0:T(8,128)}, u32[]{:S(2)}) copy-start(f32[2,64,256]{2,1,0:T(8,128)} %constant.10.clone.turn_ref) | copy-start | bytes 393220
  0.0 15.4 %copy-start.7 = (bf16[128,512]{1,0:T(8,128)(2,1)S(1)}, bf16[128,512]{1,0:T(8,128)(2,1)}, u32[]{:S(2)}) copy-start(bf16[128,512]{1,0:T(8,128)(2,1)} %param.16) | copy-start | bytes 393220
  0.0 47.6 %copy-start.6 = (f32[512]{0:T(512)S(1)}, f32[512]{0:T(512)}, u32[]{:S(2)}) copy-start(f32[512]{0:T(512)} %param.15) | copy-start | bytes 6148
  2.8 44.8 %all-to-all-start = ((bf16[32,32,512]{2,1,0:T(8,128)(2,1)}), bf16[32,32,512]{2,1,0:T(8,128)(2,1)S(1)}, u32[]{:S(2)}, u32[]{:S(2)}) async-start(bf16[32,32,512]{2,1,0:T(8,128)(2,1)} %prepare.1), calls=%async_computation | async-start | bytes 2097152 | tf_op jit(solution)/shard_map/all_to_all | solution.py:305
  15.4 44.0 %collective-permute-start = (bf16[128,512]{1,0:T(8,128)(2,1)S(1)}, bf16[128,512]{1,0:T(8,128)(2,1)S(1)}, u32[]{:S(2)}, u32[]{:S(2)}) collective-permute-start(bf16[128,512]{1,0:T(8,128)(2,1)S(1)} %copy-done.7), channel_id=1, source_target_pairs={{0,16},{16,32},{32,48},{48,0},{1,17},{17,33},{33,49},{49,1},{2,18}... | collective-permute-start | bytes 393224 | tf_op jit(solution)/shard_map/ppermute | solution.py:307
  17.8 41.7 %collective-permute-start.1 = (bf16[128,512]{1,0:T(8,128)(2,1)S(1)}, bf16[128,512]{1,0:T(8,128)(2,1)}, u32[]{:S(2)}, u32[]{:S(2)}) collective-permute-start(bf16[128,512]{1,0:T(8,128)(2,1)S(1)} %copy-done.7), channel_id=1, source_target_pairs={{0,32},{16,48},{32,0},{48,16},{1,33},{17,49},{33,1},{49,17},{2,34}... | collective-permute-start | bytes 393224 | tf_op jit(solution)/shard_map/ppermute | solution.py:307
  21.1 38.4 %collective-permute-start.2 = (bf16[128,512]{1,0:T(8,128)(2,1)S(1)}, bf16[128,512]{1,0:T(8,128)(2,1)}, u32[]{:S(2)}, u32[]{:S(2)}) collective-permute-start(bf16[128,512]{1,0:T(8,128)(2,1)S(1)} %copy-done.7), channel_id=1, source_target_pairs={{0,48},{16,0},{32,16},{48,32},{1,49},{17,1},{33,17},{49,33},{2,50}... | collective-permute-start | bytes 393224 | tf_op jit(solution)/shard_map/ppermute | solution.py:307
  47.6 1.2 copy-start.2
  48.8 1.2 copy-start.3
  59.4 23.3 %copy-start.4 = (bf16[512,512]{1,0:T(8,128)(2,1)S(1)}, bf16[512,512]{1,0:T(8,128)(2,1)}, u32[]{:S(2)}) copy-start(bf16[512,512]{1,0:T(8,128)(2,1)} %query_ref.1) | copy-start | bytes 1572868
  59.5 23.3 %all-to-all-start.1 = ((bf16[32,16,512]{2,1,0:T(8,128)(2,1)}), bf16[32,16,512]{2,1,0:T(8,128)(2,1)S(1)}, u32[]{:S(2)}, u32[]{:S(2)}) async-start(bf16[32,16,512]{2,1,0:T(8,128)(2,1)} %convolve.1), calls=%async_computation.1 | async-start | bytes 1048576 | tf_op jit(solution)/shard_map/all_to_all | solution.py:312
  67.1 22.3 %collective-permute-start.6 = (bf16[4,128,512]{2,1,0:T(8,128)(2,1)S(1)}, bf16[4,128,512]{2,1,0:T(8,128)(2,1)S(1)}, u32[]{:S(2)}, u32[]{:S(2)}) collective-permute-start(bf16[4,128,512]{2,1,0:T(8,128)(2,1)S(1)} %pad_maximum_fusion.1), channel_id=1, source_target_pairs={{0,64},{64,128},{128,192},{192,0},{1,65},{65,129},{129,193},{193,1... | collective-permute-start | bytes 1572872 | tf_op jit(solution)/shard_map/ppermute | solution.py:311
  68.6 30.1 %collective-permute-start.7 = (bf16[4,128,512]{2,1,0:T(8,128)(2,1)S(1)}, bf16[4,128,512]{2,1,0:T(8,128)(2,1)S(1)}, u32[]{:S(2)}, u32[]{:S(2)}) collective-permute-start(bf16[4,128,512]{2,1,0:T(8,128)(2,1)S(1)} %pad_maximum_fusion.1), channel_id=1, source_target_pairs={{0,128},{64,192},{128,0},{192,64},{1,129},{65,193},{129,1},{193,65... | collective-permute-start | bytes 1572872 | tf_op jit(solution)/shard_map/ppermute | solution.py:311
  71.0 27.7 %collective-permute-start.8 = (bf16[4,128,512]{2,1,0:T(8,128)(2,1)S(1)}, bf16[4,128,512]{2,1,0:T(8,128)(2,1)S(1)}, u32[]{:S(2)}, u32[]{:S(2)}) collective-permute-start(bf16[4,128,512]{2,1,0:T(8,128)(2,1)S(1)} %pad_maximum_fusion.1), channel_id=1, source_target_pairs={{0,192},{64,0},{128,64},{192,128},{1,193},{65,1},{129,65},{193,129... | collective-permute-start | bytes 1572872 | tf_op jit(solution)/shard_map/ppermute | solution.py:311
  83.0 15.7 %collective-permute-start.3 = (bf16[512,512]{1,0:T(8,128)(2,1)S(1)}, bf16[512,512]{1,0:T(8,128)(2,1)S(1)}, u32[]{:S(2)}, u32[]{:S(2)}) collective-permute-start(bf16[512,512]{1,0:T(8,128)(2,1)S(1)} %gate.1.refs_0_), channel_id=1, source_target_pairs={{0,1},{1,0},{2,3},{3,2},{4,5},{5,4},{6,7},{7,6},{8,9},{9,8},{10,11... | collective-permute-start | bytes 1572872 | tf_op jit(solution)/shard_map/ppermute | solution.py:315
  86.5 14.2 %collective-permute-start.9 = (bf16[512,512]{1,0:T(8,128)(2,1)S(1)}, bf16[512,512]{1,0:T(8,128)(2,1)S(1)}, u32[]{:S(2)}, u32[]{:S(2)}) collective-permute-start(bf16[512,512]{1,0:T(8,128)(2,1)S(1)} %gate.1.refs_0_), channel_id=1, source_target_pairs={{0,4},{2,6},{4,0},{6,2},{1,5},{3,7},{5,1},{7,3},{8,12},{10,14},{12... | collective-permute-start | bytes 1572872 | tf_op jit(solution)/shard_map/ppermute | solution.py:314
  101.0 5.5 %collective-permute-start.10 = (bf16[4,4,128,512]{3,2,1,0:T(8,128)(2,1)S(1)}, bf16[4,4,128,512]{3,2,1,0:T(8,128)(2,1)S(1)}, u32[]{:S(2)}, u32[]{:S(2)}) collective-permute-start(bf16[4,4,128,512]{3,2,1,0:T(8,128)(2,1)S(1)} %pad_maximum_fusion.own_w), channel_id=1, source_target_pairs={{0,8},{8,0},{1,9},{9,1},{2,10},{10,2},{3,11},{11,3},{4,12},{12,4},... | collective-permute-start | bytes 6291464 | tf_op jit(solution)/shard_map/ppermute | solution.py:323
  102.7 14.8 %collective-permute-start.11 = (bf16[512,512]{1,0:T(8,128)(2,1)S(1)}, bf16[512,512]{1,0:T(8,128)(2,1)S(1)}, u32[]{:S(2)}, u32[]{:S(2)}) collective-permute-start(bf16[512,512]{1,0:T(8,128)(2,1)S(1)} %gate.1.refs_0_), channel_id=1, source_target_pairs={{0,2},{2,4},{4,6},{6,0},{1,3},{3,5},{5,7},{7,1},{8,10},{10,12},{12... | collective-permute-start | bytes 1572872 | tf_op jit(solution)/shard_map/ppermute | solution.py:316
  104.0 13.5 %collective-permute-start.12 = (bf16[512,512]{1,0:T(8,128)(2,1)S(1)}, bf16[512,512]{1,0:T(8,128)(2,1)S(1)}, u32[]{:S(2)}, u32[]{:S(2)}) collective-permute-start(bf16[512,512]{1,0:T(8,128)(2,1)S(1)} %gate.1.refs_0_), channel_id=1, source_target_pairs={{0,6},{2,0},{4,2},{6,4},{1,7},{3,1},{5,3},{7,5},{8,14},{10,8},{12,... | collective-permute-start | bytes 1572872 | tf_op jit(solution)/shard_map/ppermute | solution.py:317
  105.5 12.9 %collective-permute-start.13 = (bf16[512,512]{1,0:T(8,128)(2,1)S(1)}, bf16[512,512]{1,0:T(8,128)(2,1)S(1)}, u32[]{:S(2)}, u32[]{:S(2)}) collective-permute-start(bf16[512,512]{1,0:T(8,128)(2,1)S(1)} %collective-permute-done.9.refs_2_), channel_id=1, source_target_pairs={{0,1},{1,0},{2,3},{3,2},{4,5},{5,4},{6,7},{7,6},{8,9},{9,8},{10,11... | collective-permute-start | bytes 1572872 | tf_op jit(solution)/shard_map/ppermute | solution.py:318
  105.6 23.2 %collective-permute-start.4 = (bf16[512,512]{1,0:T(8,128)(2,1)S(1)}, bf16[512,512]{1,0:T(8,128)(2,1)S(1)}, u32[]{:S(2)}, u32[]{:S(2)}) collective-permute-start(bf16[512,512]{1,0:T(8,128)(2,1)S(1)} %collective-permute-done.3.refs_1_), channel_id=1, source_target_pairs={{0,2},{2,4},{4,6},{6,0},{1,3},{3,5},{5,7},{7,1},{8,10},{10,12},{12... | collective-permute-start | bytes 1572872 | tf_op jit(solution)/shard_map/ppermute | solution.py:319
  106.5 22.3 %collective-permute-start.5 = (bf16[512,512]{1,0:T(8,128)(2,1)S(1)}, bf16[512,512]{1,0:T(8,128)(2,1)S(1)}, u32[]{:S(2)}, u32[]{:S(2)}) collective-permute-start(bf16[512,512]{1,0:T(8,128)(2,1)S(1)} %collective-permute-done.3.refs_1_), channel_id=1, source_target_pairs={{0,6},{2,0},{4,2},{6,4},{1,7},{3,1},{5,3},{7,5},{8,14},{10,8},{12,... | collective-permute-start | bytes 1572872 | tf_op jit(solution)/shard_map/ppermute | solution.py:320

commit v5 on v4

--- a/solution.py
+++ b/solution.py
@@ -304,11 +304,17 @@
     blocks = prepare(key, value, taps)
     got = lax.all_to_all(blocks, TOKENS, 0, 0, tiled=True)
     weight, _ = lax.optimization_barrier((weight, blocks))
-    weight = [weight] + [lax.ppermute(weight, "zh", along(k)) for k in (1, 2, 3)]
+    next_1, next_3 = [lax.ppermute(weight, "zh", along(k)) for k in (1, 3)]
+    next_top = lax.ppermute(next_1[:64], "zh", along(1))
+    next_low = lax.ppermute(next_3[64:], "zh", along(3))
+    weight = [weight, next_1, next_top, next_low, next_3]
     conv = convolve(got, gain.reshape(1, BLOCK))
     conv, *weight = lax.optimization_barrier((conv, *weight))
-    weight = jnp.stack(weight)
-    weight = [weight] + [lax.ppermute(weight, "x", along(k)) for k in (1, 2, 3)]
+    weight = jnp.concatenate(weight, 0).reshape(4, 128, BLOCK)
+    weight_1, weight_3 = [lax.ppermute(weight, "x", along(k)) for k in (1, 3)]
+    weight_top = lax.ppermute(weight_1[:2], "x", along(1))
+    weight_low = lax.ppermute(weight_3[2:], "x", along(3))
+    weight = [weight, weight_1, weight_top, weight_low, weight_3]
     conv = lax.all_to_all(conv, TOKENS, 0, 0, tiled=True)
     gated = gate(conv, query)
     across = lax.ppermute(gated, "y", along(2))
@@ -319,7 +325,7 @@
     after_far = lax.ppermute(far, "y", along(1))
     ahead_far = lax.ppermute(far, "y", along(3))
     *weight, _, _ = lax.optimization_barrier((*weight, far, across))
-    weight = jnp.stack(weight)
+    weight = jnp.concatenate(weight, 0).reshape(4, 4, 128, BLOCK)
     weight = (weight, lax.ppermute(weight, "core", PAIR))
     (total,) = project(weight, ((0, 0), (0, 1), (2, 0)), [gated, far, across])
     total, last = project(

time: 131 us -> 136 us (1.038)
  local copies, waits for them, and re-layouts: 2.47 us -> 6.51 us
  waiting for transfers between devices: 57.5 us -> 60.4 us
    ppermute x6 -> x8, waiting for transfers between devices: 9.25 us -> 34.6 us  [the longest x2 27 us: on_device(): next_1, next_3 = [lax.ppermute(weight, 'zh', along(k)) for k in (1, 3)]]
    all_to_all x1, waiting for transfers between devices: 23.2 us -> 0.01 us  [on_device(): got = lax.all_to_all(blocks, TOKENS, 0, 0, tiled=True)]
    ppermute x6 -> x8, starting transfers between devices: 14 us -> 9.49 us  [the longest x2 3.67 us: on_device(): next_1, next_3 = [lax.ppermute(weight, 'zh', along(k)) for k in (1, 3)]]
    all_to_all x1, starting transfers between devices: 6.63 us -> 10.5 us  [on_device(): conv = lax.all_to_all(conv, TOKENS, 0, 0, tiled=True)]
    unnamed x16 -> x22, local copies, waits for them, and re-layouts: 2.47 us -> 5.19 us
  transfers between devices with their start and end apart: 16 -> 18, of which waited for: 8 -> 10; matrix products, arithmetic and copies ran while one was open for 1% -> 3% of each run, Pallas kernels for 13% -> 13%
where the time goes in v5:
time: 136 us; the launch traced here: 135 us
  waiting for transfers between devices  60.4 us (44%)
  starting transfers between devices  46.3 us (34%)
  Pallas kernels  21.7 us (16%)
  local copies, waits for them, and re-layouts  6.51 us (5%)
    ppermute x2, waiting for transfers between devices, on_device(): next_1, next_3 = [lax.ppermute(weight, 'zh', along(k)) for k in (1, 3)]  27 us
    all_to_all x1, starting transfers between devices, on_device(): got = lax.all_to_all(blocks, TOKENS, 0, 0, tiled=True)  12.6 us
    all_to_all x1, waiting for transfers between devices, on_device(): conv = lax.all_to_all(conv, TOKENS, 0, 0, tiled=True)  11.3 us
    all_to_all x1, starting transfers between devices, on_device(): conv = lax.all_to_all(conv, TOKENS, 0, 0, tiled=True)  10.5 us
    pallas_call x1, Pallas kernels, convolve(): pl.pallas_call(convolve_kernel, out_shape=jax.ShapeDtypeStruct((BLOCKS, C...  9.37 us
    pallas_call x2, Pallas kernels, project(): pl.pallas_call(functools.partial(project_kernel, items, extras, before is...  7.92 us
    ppermute x1, waiting for transfers between devices, on_device(): after_far = lax.ppermute(far, 'y', along(1))  5.69 us
    ppermute x1, waiting for transfers between devices, on_device(): weight_low = lax.ppermute(weight_3[2:], 'x', along(3))  5.28 us
  transfers between devices with their start and end apart: 18, of which 10 were waited for; matrix products, arithmetic and copies ran while one was open for 3% of the time, Pallas kernels for 13%

profile of v5, /device:TPU:1, one launch (start us, length us, event | category | flops | bytes accessed | tf_op | source)
XLA Modules:
  0.0 135.2 jit_solution(16760226515683740379)
XLA Ops:
  0.0 2.7 %prepare.1 = bf16[32,32,512]{2,1,0:T(8,128)(2,1)} custom-call(bf16[512,512]{1,0:T(8,128)(2,1)} %key_hbm.1, bf16[512,512]{1,0:T(8,128)(2,1)} %value_hbm.1, f32[512,512]{1,0:T(8,128)} %filter_hbm.1), custom_call_target="tpu_custom_call" | custom-call | tf_op jit(solution)/shard_map/prepare/pallas_call | solution.py:99
  2.8 12.6 %all-to-all-start = ((bf16[32,32,512]{2,1,0:T(8,128)(2,1)}), bf16[32,32,512]{2,1,0:T(8,128)(2,1)S(1)}, u32[]{:S(2)}, u32[]{:S(2)}) async-start(bf16[32,32,512]{2,1,0:T(8,128)(2,1)} %prepare.1), calls=%async_computation | async-start | bytes 2097152 | tf_op jit(solution)/shard_map/all_to_all | solution.py:305
  15.4 2.4 %collective-permute-start = (bf16[128,512]{1,0:T(8,128)(2,1)}, bf16[128,512]{1,0:T(8,128)(2,1)S(1)}, u32[]{:S(2)}, u32[]{:S(2)}) collective-permute-start(bf16[128,512]{1,0:T(8,128)(2,1)} %param.16), channel_id=1, source_target_pairs={{0,16},{16,32},{32,48},{48,0},{1,17},{17,33},{33,49},{49,1},{2,18}... | collective-permute-start | bytes 393224 | tf_op jit(solution)/shard_map/ppermute | solution.py:307
  17.7 1.3 collective-permute-start.2
  19.0 24.7 %collective-permute-done = bf16[128,512]{1,0:T(8,128)(2,1)S(1)} collective-permute-done((bf16[128,512]{1,0:T(8,128)(2,1)}, bf16[128,512]{1,0:T(8,128)(2,1)S(1)}, u32[]{:S(2)}, u32[]{:S(2)}) %collective-permute-start) | collective-permute-done | bytes 131104 | tf_op jit(solution)/shard_map/ppermute | solution.py:307
  43.7 0.6 slice.16
  44.3 0.0 collective-permute-start.1
  44.3 2.3 %collective-permute-done.2 = bf16[128,512]{1,0:T(8,128)(2,1)S(1)} collective-permute-done((bf16[128,512]{1,0:T(8,128)(2,1)}, bf16[128,512]{1,0:T(8,128)(2,1)S(1)}, u32[]{:S(2)}, u32[]{:S(2)}) %collective-permute-start.2) | collective-permute-done | bytes 131104 | tf_op jit(solution)/shard_map/ppermute | solution.py:307
  46.6 0.6 slice.17
  47.2 1.5 %collective-permute-start.3 = (bf16[64,512]{1,0:T(8,128)(2,1)}, bf16[64,512]{1,0:T(8,128)(2,1)}, u32[]{:S(2)}, u32[]{:S(2)}) collective-permute-start(bf16[64,512]{1,0:T(8,128)(2,1)} %slice.17), channel_id=1, source_target_pairs={{0,48},{16,0},{32,16},{48,32},{1,49},{17,1},{33,17},{49,33},{2,50}... | collective-permute-start | bytes 196616 | tf_op jit(solution)/shard_map/ppermute | solution.py:309
  48.7 0.0 all-to-all-done.got_ref
  48.7 0.0 copy-start.2
  48.8 1.2 copy-done.2
  50.0 1.2 copy-done.3
  51.2 9.4 %convolve.1 = bf16[32,16,512]{2,1,0:T(8,128)(2,1)} custom-call(bf16[32,32,512]{2,1,0:T(8,128)(2,1)S(1)} %all-to-all-done.got_ref, f32[1,512]{1,0:T(1,128)S(1)} %bitcast.6, f32[2,64,256]{2,1,0:T(8,128)S(1)} %copy-done.5, bf16[2,512,512]{2,1,0:T(8,128)(2,1)S(1)} %copy-done, bf16[1024,512]{1,0:T(8,128)(2,1)S(1)} %copy-done.1, bf16[1024,512]{1,0:T(8,128)(2,1)S(1)} %copy-done.2, ...), custom_call_target="tpu_custom_call" | custom-call | tf_op jit(solution)/shard_map/convolve/pallas_call | solution.py:204
  60.6 0.0 copy-start.4
  60.6 0.0 collective-permute-done.1
  60.6 0.0 collective-permute-done.3
  60.6 10.5 %all-to-all-start.1 = ((bf16[32,16,512]{2,1,0:T(8,128)(2,1)}), bf16[32,16,512]{2,1,0:T(8,128)(2,1)S(1)}, u32[]{:S(2)}, u32[]{:S(2)}) async-start(bf16[32,16,512]{2,1,0:T(8,128)(2,1)} %convolve.1), calls=%async_computation.1 | async-start | bytes 1048576 | tf_op jit(solution)/shard_map/all_to_all | solution.py:318
  71.1 0.9 constant_dynamic-update-slice_fusion.4
  72.0 0.8 constant_dynamic-update-slice_fusion.2
  72.9 0.8 constant_dynamic-update-slice_fusion.1
  73.7 2.7 %collective-permute-start.9 = (bf16[4,128,512]{2,1,0:T(8,128)(2,1)S(1)}, bf16[4,128,512]{2,1,0:T(8,128)(2,1)S(1)}, u32[]{:S(2)}, u32[]{:S(2)}) collective-permute-start(bf16[4,128,512]{2,1,0:T(8,128)(2,1)S(1)} %bitcast.7), channel_id=1, source_target_pairs={{0,192},{64,0},{128,64},{192,128},{1,193},{65,1},{129,65},{193,129... | collective-permute-start | bytes 1572872 | tf_op jit(solution)/shard_map/ppermute | solution.py:314
  76.4 0.0 collective-permute-start.7
  76.4 11.3 %all-to-all-done.1.conv_ref = bf16[32,16,512]{2,1,0:T(8,128)(2,1)S(1)} async-done(((bf16[32,16,512]{2,1,0:T(8,128)(2,1)}), bf16[32,16,512]{2,1,0:T(8,128)(2,1)S(1)}, u32[]{:S(2)}, u32[]{:S(2)}) %all-to-all-start.1) | async-done | bytes 524320 | tf_op jit(solution)/shard_map/all_to_all | solution.py:318
  87.7 0.2 gate.1.refs_0_
  87.9 3.6 %collective-permute-start.4 = (bf16[512,512]{1,0:T(8,128)(2,1)S(1)}, bf16[512,512]{1,0:T(8,128)(2,1)S(1)}, u32[]{:S(2)}, u32[]{:S(2)}) collective-permute-start(bf16[512,512]{1,0:T(8,128)(2,1)S(1)} %gate.1.refs_0_), channel_id=1, source_target_pairs={{0,1},{1,0},{2,3},{3,2},{4,5},{5,4},{6,7},{7,6},{8,9},{9,8},{10,11... | collective-permute-start | bytes 1572872 | tf_op jit(solution)/shard_map/ppermute | solution.py:321
  91.5 2.9 %collective-permute-start.11 = (bf16[512,512]{1,0:T(8,128)(2,1)S(1)}, bf16[512,512]{1,0:T(8,128)(2,1)S(1)}, u32[]{:S(2)}, u32[]{:S(2)}) collective-permute-start(bf16[512,512]{1,0:T(8,128)(2,1)S(1)} %gate.1.refs_0_), channel_id=1, source_target_pairs={{0,4},{2,6},{4,0},{6,2},{1,5},{3,7},{5,1},{7,3},{8,12},{10,14},{12... | collective-permute-start | bytes 1572872 | tf_op jit(solution)/shard_map/ppermute | solution.py:320
  94.5 0.0 collective-permute-done.9
  94.5 1.0 collective-permute-start.10
  95.5 0.6 collective-permute-start.8
  96.1 5.3 %collective-permute-done.10 = bf16[2,128,512]{2,1,0:T(8,128)(2,1)S(1)} collective-permute-done((bf16[2,128,512]{2,1,0:T(8,128)(2,1)S(1)}, bf16[2,128,512]{2,1,0:T(8,128)(2,1)S(1)}, u32[]{:S(2)}, u32[]{:S(2)}) %collective-permute-start.10) | collective-permute-done | bytes 262176 | tf_op jit(solution)/shard_map/ppermute | solution.py:316
  101.4 2.3 %collective-permute-done.8 = bf16[2,128,512]{2,1,0:T(8,128)(2,1)S(1)} collective-permute-done((bf16[2,128,512]{2,1,0:T(8,128)(2,1)S(1)}, bf16[2,128,512]{2,1,0:T(8,128)(2,1)S(1)}, u32[]{:S(2)}, u32[]{:S(2)}) %collective-permute-start.8) | collective-permute-done | bytes 262176 | tf_op jit(solution)/shard_map/ppermute | solution.py:315
  103.8 2.1 %collective-permute-done.11.refs_2_ = bf16[512,512]{1,0:T(8,128)(2,1)S(1)} collective-permute-done((bf16[512,512]{1,0:T(8,128)(2,1)S(1)}, bf16[512,512]{1,0:T(8,128)(2,1)S(1)}, u32[]{:S(2)}, u32[]{:S(2)}) %collective-permute-start.11) | collective-permute-done | bytes 524320 | tf_op jit(solution)/shard_map/ppermute | solution.py:320
  106.0 1.6 %collective-permute-start.12 = (bf16[4,4,128,512]{3,2,1,0:T(8,128)(2,1)S(1)}, bf16[4,4,128,512]{3,2,1,0:T(8,128)(2,1)S(1)}, u32[]{:S(2)}, u32[]{:S(2)}) collective-permute-start(bf16[4,4,128,512]{3,2,1,0:T(8,128)(2,1)S(1)} %bitcast.3), channel_id=1, source_target_pairs={{0,8},{8,0},{1,9},{9,1},{2,10},{10,2},{3,11},{11,3},{4,12},{12,4},... | collective-permute-start | bytes 6291464 | tf_op jit(solution)/shard_map/ppermute | solution.py:329
  107.7 1.3 collective-permute-start.13
  109.0 1.4 %collective-permute-start.14 = (bf16[512,512]{1,0:T(8,128)(2,1)S(1)}, bf16[512,512]{1,0:T(8,128)(2,1)S(1)}, u32[]{:S(2)}, u32[]{:S(2)}) collective-permute-start(bf16[512,512]{1,0:T(8,128)(2,1)S(1)} %gate.1.refs_0_), channel_id=1, source_target_pairs={{0,6},{2,0},{4,2},{6,4},{1,7},{3,1},{5,3},{7,5},{8,14},{10,8},{12,... | collective-permute-start | bytes 1572872 | tf_op jit(solution)/shard_map/ppermute | solution.py:323
  110.4 0.1 collective-permute-start.15
  110.5 0.0 collective-permute-start.5
  110.5 0.9 collective-permute-done.12.sibling_w
  111.4 2.7 %collective-permute-start.6 = (bf16[512,512]{1,0:T(8,128)(2,1)S(1)}, bf16[512,512]{1,0:T(8,128)(2,1)S(1)}, u32[]{:S(2)}, u32[]{:S(2)}) collective-permute-start(bf16[512,512]{1,0:T(8,128)(2,1)S(1)} %collective-permute-done.4.refs_1_), channel_id=1, source_target_pairs={{0,6},{2,0},{4,2},{6,4},{1,7},{3,1},{5,3},{7,5},{8,14},{10,8},{12,... | collective-permute-start | bytes 1572872 | tf_op jit(solution)/shard_map/ppermute | solution.py:326
  114.2 3.2 %project.2.refs_3_ = f32[512,512]{1,0:T(8,128)S(1)} custom-call(bf16[4,4,128,512]{3,2,1,0:T(8,128)(2,1)S(1)} %bitcast.4, bf16[4,4,128,512]{3,2,1,0:T(8,128)(2,1)S(1)} %collective-permute-done.12.sibling_w, bf16[512,512]{1,0:T(8,128)(2,1)S(1)} %gate.1.refs_0_, bf16[512,512]{1,0:T(8,128)(2,1)S(1)} %collective-permute-done.4.refs_1_, ...), custom_call_target="tpu_custom_call" | custom-call | flops 805306368 | bytes 6291456 | tf_op jit(solution)/shard_map/project/pallas_call | solution.py:266
  117.4 5.0 %collective-permute-done.13.refs_0_ = bf16[512,512]{1,0:T(8,128)(2,1)S(1)} collective-permute-done((bf16[512,512]{1,0:T(8,128)(2,1)S(1)}, bf16[512,512]{1,0:T(8,128)(2,1)S(1)}, u32[]{:S(2)}, u32[]{:S(2)}) %collective-permute-start.13) | collective-permute-done | bytes 524320 | tf_op jit(solution)/shard_map/ppermute | solution.py:322
  122.4 0.0 collective-permute-done.14.refs_1_
  122.4 0.8 collective-permute-done.15.refs_2_
  123.3 4.7 %project.3 = (f32[512,512]{1,0:T(8,128)S(1)}, bf16[2,512,512]{2,1,0:T(8,128)(2,1)S(1)}) custom-call(bf16[4,4,128,512]{3,2,1,0:T(8,128)(2,1)S(1)} %bitcast.5, bf16[4,4,128,512]{3,2,1,0:T(8,128)(2,1)S(1)} %collective-permute-done.12.sibling_w, bf16[512,512]{1,0:T(8,128)(2,1)S(1)} %collective-permute-done.13.refs_0_, ...), custom_call_target="tpu_custom_call" | custom-call | flops 805306368 | bytes 6291456 | tf_op jit(solution)/shard_map/project/pallas_call | solution.py:266
  128.0 5.7 %collective-permute-done.5.after_ref = bf16[512,512]{1,0:T(8,128)(2,1)S(1)} collective-permute-done((bf16[512,512]{1,0:T(8,128)(2,1)S(1)}, bf16[512,512]{1,0:T(8,128)(2,1)S(1)}, u32[]{:S(2)}, u32[]{:S(2)}) %collective-permute-start.5) | collective-permute-done | bytes 524320 | tf_op jit(solution)/shard_map/ppermute | solution.py:325
  133.7 1.5 %finish.1 = bf16[512,512]{1,0:T(8,128)(2,1)} custom-call(bf16[512,512]{1,0:T(8,128)(2,1)S(1)} %collective-permute-done.5.after_ref, bf16[512,512]{1,0:T(8,128)(2,1)S(1)} %collective-permute-done.6.ahead_ref, bf16[2,512,512]{2,1,0:T(8,128)(2,1)S(1)} %get-tuple-element.31.weight_ref, f32[512,512]{1,0:T(8,128)S(1)} %get-tuple-element.32.before_ref), custom_call_target="tpu_custom_call" | custom-call | tf_op jit(solution)/shard_map/finish/pallas_call | solution.py:289
  (22 shorter events, 0.2 us)
Async XLA Ops:
  0.0 48.7 %copy-start = (bf16[2,512,512]{2,1,0:T(8,128)(2,1)S(1)}, bf16[2,512,512]{2,1,0:T(8,128)(2,1)}, u32[]{:S(2)}) copy-start(bf16[2,512,512]{2,1,0:T(8,128)(2,1)} %constant.11.clone.refs_0_) | copy-start | bytes 3145732
  0.0 48.7 %copy-start.1 = (bf16[1024,512]{1,0:T(8,128)(2,1)S(1)}, bf16[1024,512]{1,0:T(8,128)(2,1)}, u32[]{:S(2)}) copy-start(bf16[1024,512]{1,0:T(8,128)(2,1)} %constant.12.clone.refs_1_) | copy-start | bytes 3145732
  0.0 48.7 %copy-start.5 = (f32[2,64,256]{2,1,0:T(8,128)S(1)}, f32[2,64,256]{2,1,0:T(8,128)}, u32[]{:S(2)}) copy-start(f32[2,64,256]{2,1,0:T(8,128)} %constant.10.clone.turn_ref) | copy-start | bytes 393220
  0.0 48.7 %copy-start.6 = (f32[512]{0:T(512)S(1)}, f32[512]{0:T(512)}, u32[]{:S(2)}) copy-start(f32[512]{0:T(512)} %param.15) | copy-start | bytes 6148
  2.8 46.0 %all-to-all-start = ((bf16[32,32,512]{2,1,0:T(8,128)(2,1)}), bf16[32,32,512]{2,1,0:T(8,128)(2,1)S(1)}, u32[]{:S(2)}, u32[]{:S(2)}) async-start(bf16[32,32,512]{2,1,0:T(8,128)(2,1)} %prepare.1), calls=%async_computation | async-start | bytes 2097152 | tf_op jit(solution)/shard_map/all_to_all | solution.py:305
  15.4 28.3 %collective-permute-start = (bf16[128,512]{1,0:T(8,128)(2,1)}, bf16[128,512]{1,0:T(8,128)(2,1)S(1)}, u32[]{:S(2)}, u32[]{:S(2)}) collective-permute-start(bf16[128,512]{1,0:T(8,128)(2,1)} %param.16), channel_id=1, source_target_pairs={{0,16},{16,32},{32,48},{48,0},{1,17},{17,33},{33,49},{49,1},{2,18}... | collective-permute-start | bytes 393224 | tf_op jit(solution)/shard_map/ppermute | solution.py:307
  17.7 28.9 %collective-permute-start.2 = (bf16[128,512]{1,0:T(8,128)(2,1)}, bf16[128,512]{1,0:T(8,128)(2,1)S(1)}, u32[]{:S(2)}, u32[]{:S(2)}) collective-permute-start(bf16[128,512]{1,0:T(8,128)(2,1)} %param.16), channel_id=1, source_target_pairs={{0,48},{16,0},{32,16},{48,32},{1,49},{17,1},{33,17},{49,33},{2,50}... | collective-permute-start | bytes 393224 | tf_op jit(solution)/shard_map/ppermute | solution.py:307
  44.3 16.3 %collective-permute-start.1 = (bf16[64,512]{1,0:T(8,128)(2,1)}, bf16[64,512]{1,0:T(8,128)(2,1)}, u32[]{:S(2)}, u32[]{:S(2)}) collective-permute-start(bf16[64,512]{1,0:T(8,128)(2,1)} %slice.16), channel_id=1, source_target_pairs={{0,16},{16,32},{32,48},{48,0},{1,17},{17,33},{33,49},{49,1},{2,18}... | collective-permute-start | bytes 196616 | tf_op jit(solution)/shard_map/ppermute | solution.py:308
  47.2 13.4 %collective-permute-start.3 = (bf16[64,512]{1,0:T(8,128)(2,1)}, bf16[64,512]{1,0:T(8,128)(2,1)}, u32[]{:S(2)}, u32[]{:S(2)}) collective-permute-start(bf16[64,512]{1,0:T(8,128)(2,1)} %slice.17), channel_id=1, source_target_pairs={{0,48},{16,0},{32,16},{48,32},{1,49},{17,1},{33,17},{49,33},{2,50}... | collective-permute-start | bytes 196616 | tf_op jit(solution)/shard_map/ppermute | solution.py:309
  48.7 1.2 copy-start.2
  50.0 1.2 copy-start.3
  60.6 27.1 %copy-start.4 = (bf16[512,512]{1,0:T(8,128)(2,1)S(1)}, bf16[512,512]{1,0:T(8,128)(2,1)}, u32[]{:S(2)}) copy-start(bf16[512,512]{1,0:T(8,128)(2,1)} %query_ref.1) | copy-start | bytes 1572868
  60.6 27.1 %all-to-all-start.1 = ((bf16[32,16,512]{2,1,0:T(8,128)(2,1)}), bf16[32,16,512]{2,1,0:T(8,128)(2,1)S(1)}, u32[]{:S(2)}, u32[]{:S(2)}) async-start(bf16[32,16,512]{2,1,0:T(8,128)(2,1)} %convolve.1), calls=%async_computation.1 | async-start | bytes 1048576 | tf_op jit(solution)/shard_map/all_to_all | solution.py:318
  73.7 20.7 %collective-permute-start.9 = (bf16[4,128,512]{2,1,0:T(8,128)(2,1)S(1)}, bf16[4,128,512]{2,1,0:T(8,128)(2,1)S(1)}, u32[]{:S(2)}, u32[]{:S(2)}) collective-permute-start(bf16[4,128,512]{2,1,0:T(8,128)(2,1)S(1)} %bitcast.7), channel_id=1, source_target_pairs={{0,192},{64,0},{128,64},{192,128},{1,193},{65,1},{129,65},{193,129... | collective-permute-start | bytes 1572872 | tf_op jit(solution)/shard_map/ppermute | solution.py:314
  76.4 19.1 %collective-permute-start.7 = (bf16[4,128,512]{2,1,0:T(8,128)(2,1)S(1)}, bf16[4,128,512]{2,1,0:T(8,128)(2,1)S(1)}, u32[]{:S(2)}, u32[]{:S(2)}) collective-permute-start(bf16[4,128,512]{2,1,0:T(8,128)(2,1)S(1)} %bitcast.8), channel_id=1, source_target_pairs={{0,64},{64,128},{128,192},{192,0},{1,65},{65,129},{129,193},{193,1... | collective-permute-start | bytes 1572872 | tf_op jit(solution)/shard_map/ppermute | solution.py:314
  87.9 15.8 %collective-permute-start.4 = (bf16[512,512]{1,0:T(8,128)(2,1)S(1)}, bf16[512,512]{1,0:T(8,128)(2,1)S(1)}, u32[]{:S(2)}, u32[]{:S(2)}) collective-permute-start(bf16[512,512]{1,0:T(8,128)(2,1)S(1)} %gate.1.refs_0_), channel_id=1, source_target_pairs={{0,1},{1,0},{2,3},{3,2},{4,5},{5,4},{6,7},{7,6},{8,9},{9,8},{10,11... | collective-permute-start | bytes 1572872 | tf_op jit(solution)/shard_map/ppermute | solution.py:321
  91.5 14.3 %collective-permute-start.11 = (bf16[512,512]{1,0:T(8,128)(2,1)S(1)}, bf16[512,512]{1,0:T(8,128)(2,1)S(1)}, u32[]{:S(2)}, u32[]{:S(2)}) collective-permute-start(bf16[512,512]{1,0:T(8,128)(2,1)S(1)} %gate.1.refs_0_), channel_id=1, source_target_pairs={{0,4},{2,6},{4,0},{6,2},{1,5},{3,7},{5,1},{7,3},{8,12},{10,14},{12... | collective-permute-start | bytes 1572872 | tf_op jit(solution)/shard_map/ppermute | solution.py:320
  94.5 6.9 %collective-permute-start.10 = (bf16[2,128,512]{2,1,0:T(8,128)(2,1)S(1)}, bf16[2,128,512]{2,1,0:T(8,128)(2,1)S(1)}, u32[]{:S(2)}, u32[]{:S(2)}) collective-permute-start(bf16[2,128,512]{2,1,0:T(8,128)(2,1)S(1)} %slice.19), channel_id=1, source_target_pairs={{0,192},{64,0},{128,64},{192,128},{1,193},{65,1},{129,65},{193,129... | collective-permute-start | bytes 786440 | tf_op jit(solution)/shard_map/ppermute | solution.py:316
  95.5 8.2 %collective-permute-start.8 = (bf16[2,128,512]{2,1,0:T(8,128)(2,1)S(1)}, bf16[2,128,512]{2,1,0:T(8,128)(2,1)S(1)}, u32[]{:S(2)}, u32[]{:S(2)}) collective-permute-start(bf16[2,128,512]{2,1,0:T(8,128)(2,1)S(1)} %slice.18), channel_id=1, source_target_pairs={{0,64},{64,128},{128,192},{192,0},{1,65},{65,129},{129,193},{193,1... | collective-permute-start | bytes 786440 | tf_op jit(solution)/shard_map/ppermute | solution.py:315
  106.0 5.4 %collective-permute-start.12 = (bf16[4,4,128,512]{3,2,1,0:T(8,128)(2,1)S(1)}, bf16[4,4,128,512]{3,2,1,0:T(8,128)(2,1)S(1)}, u32[]{:S(2)}, u32[]{:S(2)}) collective-permute-start(bf16[4,4,128,512]{3,2,1,0:T(8,128)(2,1)S(1)} %bitcast.3), channel_id=1, source_target_pairs={{0,8},{8,0},{1,9},{9,1},{2,10},{10,2},{3,11},{11,3},{4,12},{12,4},... | collective-permute-start | bytes 6291464 | tf_op jit(solution)/shard_map/ppermute | solution.py:329
  107.7 14.8 %collective-permute-start.13 = (bf16[512,512]{1,0:T(8,128)(2,1)S(1)}, bf16[512,512]{1,0:T(8,128)(2,1)S(1)}, u32[]{:S(2)}, u32[]{:S(2)}) collective-permute-start(bf16[512,512]{1,0:T(8,128)(2,1)S(1)} %gate.1.refs_0_), channel_id=1, source_target_pairs={{0,2},{2,4},{4,6},{6,0},{1,3},{3,5},{5,7},{7,1},{8,10},{10,12},{12... | collective-permute-start | bytes 1572872 | tf_op jit(solution)/shard_map/ppermute | solution.py:322
  109.0 13.5 %collective-permute-start.14 = (bf16[512,512]{1,0:T(8,128)(2,1)S(1)}, bf16[512,512]{1,0:T(8,128)(2,1)S(1)}, u32[]{:S(2)}, u32[]{:S(2)}) collective-permute-start(bf16[512,512]{1,0:T(8,128)(2,1)S(1)} %gate.1.refs_0_), channel_id=1, source_target_pairs={{0,6},{2,0},{4,2},{6,4},{1,7},{3,1},{5,3},{7,5},{8,14},{10,8},{12,... | collective-permute-start | bytes 1572872 | tf_op jit(solution)/shard_map/ppermute | solution.py:323
  110.4 12.9 %collective-permute-start.15 = (bf16[512,512]{1,0:T(8,128)(2,1)S(1)}, bf16[512,512]{1,0:T(8,128)(2,1)S(1)}, u32[]{:S(2)}, u32[]{:S(2)}) collective-permute-start(bf16[512,512]{1,0:T(8,128)(2,1)S(1)} %collective-permute-done.11.refs_2_), channel_id=1, source_target_pairs={{0,1},{1,0},{2,3},{3,2},{4,5},{5,4},{6,7},{7,6},{8,9},{9,8},{10,11... | collective-permute-start | bytes 1572872 | tf_op jit(solution)/shard_map/ppermute | solution.py:324
  110.5 23.2 %collective-permute-start.5 = (bf16[512,512]{1,0:T(8,128)(2,1)S(1)}, bf16[512,512]{1,0:T(8,128)(2,1)S(1)}, u32[]{:S(2)}, u32[]{:S(2)}) collective-permute-start(bf16[512,512]{1,0:T(8,128)(2,1)S(1)} %collective-permute-done.4.refs_1_), channel_id=1, source_target_pairs={{0,2},{2,4},{4,6},{6,0},{1,3},{3,5},{5,7},{7,1},{8,10},{10,12},{12... | collective-permute-start | bytes 1572872 | tf_op jit(solution)/shard_map/ppermute | solution.py:325
  111.4 22.2 %collective-permute-start.6 = (bf16[512,512]{1,0:T(8,128)(2,1)S(1)}, bf16[512,512]{1,0:T(8,128)(2,1)S(1)}, u32[]{:S(2)}, u32[]{:S(2)}) collective-permute-start(bf16[512,512]{1,0:T(8,128)(2,1)S(1)} %collective-permute-done.4.refs_1_), channel_id=1, source_target_pairs={{0,6},{2,0},{4,2},{6,4},{1,7},{3,1},{5,3},{7,5},{8,14},{10,8},{12,... | collective-permute-start | bytes 1572872 | tf_op jit(solution)/shard_map/ppermute | solution.py:326
